TPU v7x, 32 devices: a whole 2x2x4 slice. The times are simulated.
32 devices in a mesh: section: 2 (over z_hi), context: 8 (over y, x, core), tensor: 2 (over z_lo).
Axes of the slice: x: 2, y: 2, z: 4 (z_hi: 2, z_lo: 2; z = z_hi * 2 + z_lo), core: 2. Of those that a mesh axis runs over, the one named last changes fastest.
Arguments:
- block_input: bfloat16 [4, 1024, 1536], P(None, 'context'), may hold values from -6 to 6
- norm_gain: float32 [2, 1536], P('section'), may hold values from 0.1 to 1.9
- w_gate: bfloat16 [2, 1536, 3072], P('section', 'context', 'tensor'), may hold values from -0.15625 to 0.15625
- w_value: bfloat16 [2, 1536, 3072], P('section', 'context', 'tensor'), may hold values from -0.15625 to 0.15625
- w_bc: bfloat16 [2, 1536, 256], P('section', 'context'), may hold values from -0.15625 to 0.15625
- w_dt: bfloat16 [2, 1536, 48], P('section', 'context', 'tensor'), may hold values from -0.15625 to 0.15625
- conv_value: float32 [2, 4, 3072], P('section', None, 'tensor'), may hold values from -3 to 3
- conv_bc: float32 [2, 4, 256], P('section'), may hold values from -3 to 3
- conv_value_bias: float32 [2, 3072], P('section', 'tensor'), may hold values from -3 to 3
- conv_bc_bias: float32 [2, 256], P('section'), may hold values from -3 to 3
- dt_bias: float32 [2, 48], P('section', 'tensor'), may hold values from -5 to -3
- decay_log: float32 [2, 48], P('section', 'tensor'), may hold values from -5.3 to 0.7
- skip: float32 [2, 48], P('section', 'tensor'), may hold values from 0.5 to 2
- gate_gain: float32 [2, 3072], P('section', 'tensor'), may hold values from 0.1 to 1.9
- w_out: bfloat16 [2, 3072, 1536], P('section', 'tensor', 'context'), may hold values from -0.109375 to 0.109375
- cotangent: bfloat16 [4, 1024, 1536], P(None, 'context'), may hold values from -6 to 6
Outputs:
- section_outputs: bfloat16 [2, 4, 1024, 1536], P('section', None, 'context')
- section_input_grads: float32 [2, 4, 1024, 1536], P('section', None, 'context')
- norm_gain_grad: float32 [2, 1536], P('section')
- w_gate_grad: float32 [2, 1536, 3072], P('section', 'context', 'tensor')
- w_value_grad: float32 [2, 1536, 3072], P('section', 'context', 'tensor')
- w_bc_grad: float32 [2, 1536, 256], P('section', 'context')
- w_dt_grad: float32 [2, 1536, 48], P('section', 'context', 'tensor')
- conv_value_grad: float32 [2, 4, 3072], P('section', None, 'tensor')
- conv_bc_grad: float32 [2, 4, 256], P('section')
- conv_value_bias_grad: float32 [2, 3072], P('section', 'tensor')
- conv_bc_bias_grad: float32 [2, 256], P('section')
- dt_bias_grad: float32 [2, 48], P('section', 'tensor')
- decay_log_grad: float32 [2, 48], P('section', 'tensor')
- skip_grad: float32 [2, 48], P('section', 'tensor')
- gate_gain_grad: float32 [2, 3072], P('section', 'tensor')
- w_out_grad: float32 [2, 3072, 1536], P('section', 'tensor', 'context')
All inputs are finite; a program needn't handle non-finite values.
Results may differ from a plain program's by a relative error of at most 0.019.
Values may be sent and summed in bfloat16 or wider, within the bound.
No kernel may reach another device: no remote copies, remote signals or barrier semaphores. Data moves between devices by JAX's collectives and lax.ppermute only.
A program may use at most 256 MiB of HBM per device.

v0:
```python
import jax
import jax.numpy as jnp
from jax import lax
from jax.sharding import PartitionSpec as P

HEAD_DIM = 64
STATE = 128
CONV = 4
INNER = 3072


epsilon = 1e-05
highest = lax.Precision.HIGHEST


def from_behind(block, axis, distance):
    devices = range(lax.axis_size(axis))
    route = [(i - distance, i) for i in devices if i - distance in devices]
    return lax.ppermute(block, axis, route)


def entering(part, axis, combine, identity, reverse):
    count = lax.axis_size(axis)
    place = lax.axis_index(axis)
    ahead = count - 1 - place if reverse else place
    gathered = jax.tree.map(lambda a: lax.all_gather(a, axis), part)
    state = jax.tree.map(lambda a, e: jnp.zeros_like(a) + jnp.asarray(e, a.dtype), part, identity)

    def one(lap, state):
        source = count - 1 - lap if reverse else lap
        return combine(
            state, jax.tree.map(lambda a: lax.dynamic_index_in_dim(a, source, 0, False), gathered)
        )

    return lax.fori_loop(0, ahead, one, state)


def conv_apply(mixed_pre, border, kernel, kernel_bias):
    token_count = mixed_pre.shape[0]
    padded = jnp.concatenate([border, mixed_pre], axis=0)
    running = kernel_bias[None, :]
    for tap_index in range(CONV):
        running = running + kernel[tap_index][None, :] * padded[tap_index : tap_index + token_count]
    return jax.nn.silu(running)


def split_mixed(mixed, head_count):
    inner_width = head_count * HEAD_DIM
    token_count = mixed.shape[0]
    values = mixed[:, :inner_width].reshape(token_count, head_count, HEAD_DIM)
    return (values, mixed[:, inner_width : inner_width + STATE], mixed[:, inner_width + STATE :])


def decay_rates(step_pre, step_bias, decay_log):
    step_size = jax.nn.softplus(step_pre + step_bias[None, :])
    log_decay = jnp.cumsum(-jnp.exp(decay_log)[None, :] * step_size, axis=0)
    return (step_size, log_decay)


def summaries(values, input_map, step_size, log_decay):
    total_decay = jnp.exp(log_decay[-1])
    weight_rows = jnp.exp(log_decay[-1][None, :] - log_decay) * step_size
    end_state = jnp.einsum("th,thp,tn->hpn", weight_rows, values, input_map, precision=highest)
    return (total_decay, end_state)


def outputs(values, input_map, output_map, step_size, log_decay, skip_gain, state_in):
    token_count = log_decay.shape[0]
    positions = jnp.arange(token_count)
    causal = (positions[:, None] >= positions[None, :])[:, :, None]
    log_gap = log_decay[:, None, :] - log_decay[None, :, :]
    decay = jnp.where(causal, jnp.exp(jnp.where(causal, log_gap, 0.0)), 0.0)
    contact = jnp.einsum("tn,sn->ts", output_map, input_map, precision=highest)
    mixing = decay * contact[:, :, None] * step_size[None, :, :]
    inside = jnp.einsum("tsh,shp->thp", mixing, values, precision=highest)
    carried = jnp.exp(log_decay)[:, :, None] * jnp.einsum(
        "tn,hpn->thp", output_map, state_in, precision=highest
    )
    result = inside + carried + skip_gain[None, :, None] * values
    return result.reshape(token_count, -1)


def ssm_local(mixed, step_pre, step_bias, decay_log, skip_gain, state_in):
    values, input_map, output_map = split_mixed(mixed, step_pre.shape[1])
    step_size, log_decay = decay_rates(step_pre, step_bias, decay_log)
    total_decay, end_state = summaries(values, input_map, step_size, log_decay)
    result = outputs(values, input_map, output_map, step_size, log_decay, skip_gain, state_in)
    return (result, total_decay, end_state)


def carry_combine(earlier_part, later_part):
    return (
        earlier_part[0] * later_part[0],
        later_part[0][:, None, None] * earlier_part[1] + later_part[1],
    )


def forward_layer(residual, matrices, small_params):
    gate_full, mix_full, step_full, out_full = matrices
    norm_in, kernel, kernel_bias, step_bias, decay_log, skip_gain, gate_gain = small_params
    token_count = residual.shape[0]
    in_scale = lax.rsqrt(jnp.mean(residual * residual, axis=1, keepdims=True) + epsilon)
    normed_in = (residual * in_scale * norm_in[None, :]).astype(jnp.bfloat16)
    gate_pre = jnp.dot(normed_in, gate_full, preferred_element_type=jnp.float32)
    mixed_pre = jnp.dot(normed_in, mix_full, preferred_element_type=jnp.float32)
    step_pre = jnp.dot(normed_in, step_full, preferred_element_type=jnp.float32)
    border = from_behind(mixed_pre[token_count - (CONV - 1) :], "context", 1)
    mixed = conv_apply(mixed_pre, border, kernel, kernel_bias)
    values, input_map, output_map = split_mixed(mixed, step_pre.shape[1])
    step_size, log_decay = decay_rates(step_pre, step_bias, decay_log)
    total_decay, end_state = summaries(values, input_map, step_size, log_decay)
    identity = (jnp.ones_like(total_decay), jnp.zeros_like(end_state))
    carried_in = entering((total_decay, end_state), "context", carry_combine, identity, False)
    state_in = carried_in[1]
    ssm_out = outputs(values, input_map, output_map, step_size, log_decay, skip_gain, state_in)
    gated = ssm_out * jax.nn.silu(gate_pre)
    squares = lax.psum(jnp.sum(gated * gated, axis=1), "tensor")
    gate_scale = lax.rsqrt(squares / INNER + epsilon)
    gate_normed = (gated * gate_scale[:, None] * gate_gain[None, :]).astype(jnp.bfloat16)
    kept_values = (
        residual,
        in_scale,
        normed_in,
        gate_pre,
        mixed_pre,
        border,
        mixed,
        step_pre,
        state_in,
        ssm_out,
        gated,
        gate_scale,
        gate_normed,
    )
    partial_out = jnp.dot(gate_normed, out_full, preferred_element_type=jnp.float32)
    branch = lax.psum(partial_out, "tensor")
    return (residual + branch, kept_values)


def backward_layer(out_grad, kept_values, matrices, small_params):
    gate_full, mix_full, step_full, out_full = matrices
    norm_in, kernel, kernel_bias, step_bias, decay_log, skip_gain, gate_gain = small_params
    (
        residual,
        in_scale,
        normed_in,
        gate_pre,
        mixed_pre,
        border,
        mixed,
        step_pre,
        state_in,
        ssm_out,
        gated,
        gate_scale,
        gate_normed,
    ) = kept_values
    token_count = residual.shape[0]
    head_count = step_pre.shape[1]
    grad_out_w = jnp.einsum("ti,td->id", gate_normed, out_grad, preferred_element_type=jnp.float32)
    grad_normed = jnp.einsum("td,id->ti", out_grad, out_full, preferred_element_type=jnp.float32)
    scaled = grad_normed * gate_gain[None, :]
    grad_gate_gain = jnp.sum(grad_normed * gated * gate_scale[:, None], axis=0)
    inner_sum = lax.psum(jnp.sum(scaled * gated, axis=1), "tensor")
    grad_gated = gate_scale[:, None] * scaled - gated * (gate_scale**3 * inner_sum / INNER)[:, None]
    sigmoid_gate = jax.nn.sigmoid(gate_pre)
    grad_ssm = grad_gated * gate_pre * sigmoid_gate
    grad_gate_pre = grad_gated * ssm_out * sigmoid_gate * (1.0 + gate_pre * (1.0 - sigmoid_gate))
    values, input_map, output_map = split_mixed(mixed, head_count)
    step_size, log_decay = decay_rates(step_pre, step_bias, decay_log)
    grad_heads = grad_ssm.reshape(token_count, head_count, HEAD_DIM)
    grad_state_in = jnp.einsum(
        "th,thp,tn->hpn", jnp.exp(log_decay), grad_heads, output_map, precision=highest
    )
    total_decay = jnp.exp(log_decay[-1])
    identity = (jnp.ones_like(total_decay), jnp.zeros_like(grad_state_in))
    carried_back = entering((total_decay, grad_state_in), "context", carry_combine, identity, True)
    grad_end = carried_back[1]
    grad_decay = jnp.sum(grad_end * state_in, axis=(1, 2))
    _, pullback = jax.vjp(ssm_local, mixed, step_pre, step_bias, decay_log, skip_gain, state_in)
    grad_mixed, grad_step_pre, grad_step_bias, grad_decay_log, grad_skip, _ = pullback(
        (grad_ssm, grad_decay, grad_end)
    )
    mix_width = grad_mixed.shape[1] - 2 * STATE
    grad_maps = lax.psum(grad_mixed[:, mix_width:].astype(jnp.bfloat16), "tensor").astype(
        jnp.float32
    )
    grad_mixed = jnp.concatenate([grad_mixed[:, :mix_width], grad_maps], axis=1)
    _, conv_pull = jax.vjp(conv_apply, mixed_pre, border, kernel, kernel_bias)
    grad_mixed_pre, grad_border, grad_kernel, grad_kernel_bias = conv_pull(grad_mixed)
    returned = from_behind(grad_border, "context", -1)
    edge = token_count - (CONV - 1)
    grad_mixed_pre = jnp.concatenate(
        [grad_mixed_pre[:edge], grad_mixed_pre[edge:] + returned], axis=0
    )
    low_gate = grad_gate_pre.astype(jnp.bfloat16)
    low_mixed = grad_mixed_pre.astype(jnp.bfloat16)
    low_step = grad_step_pre.astype(jnp.bfloat16)
    grad_gate_w = jnp.einsum("td,ti->di", normed_in, low_gate, preferred_element_type=jnp.float32)
    grad_mix_w = jnp.einsum("td,ti->di", normed_in, low_mixed, preferred_element_type=jnp.float32)
    grad_step_w = jnp.einsum("td,ti->di", normed_in, low_step, preferred_element_type=jnp.float32)
    back_in = (
        jnp.einsum("ti,di->td", low_gate, gate_full, preferred_element_type=jnp.float32)
        + jnp.einsum(
            "ti,di->td",
            low_mixed[:, :mix_width],
            mix_full[:, :mix_width],
            preferred_element_type=jnp.float32,
        )
        + 0.5
        * jnp.einsum(
            "ti,di->td",
            low_mixed[:, mix_width:],
            mix_full[:, mix_width:],
            preferred_element_type=jnp.float32,
        )
        + jnp.einsum("ti,di->td", low_step, step_full, preferred_element_type=jnp.float32)
    )
    grad_in = lax.psum(back_in.astype(jnp.bfloat16), "tensor").astype(jnp.float32)
    scaled_in = grad_in * norm_in[None, :]
    grad_norm_in = jnp.sum(grad_in * residual * in_scale, axis=0)
    grad_residual = (
        out_grad.astype(jnp.float32)
        + in_scale * scaled_in
        - residual * in_scale**3 * jnp.mean(scaled_in * residual, axis=1, keepdims=True)
    )
    matrix_grads = (grad_gate_w, grad_mix_w, grad_step_w, grad_out_w)
    small_grads = (
        grad_norm_in,
        grad_kernel,
        grad_kernel_bias,
        grad_step_bias,
        grad_decay_log,
        grad_skip,
        grad_gate_gain,
    )
    return (grad_residual, matrix_grads, small_grads)


def reduce_grads(matrix_grads):
    return (
        lax.psum_scatter(
            matrix_grads[0].astype(jnp.bfloat16), "context", scatter_dimension=0, tiled=True
        ).astype(jnp.float32),
        lax.psum_scatter(
            matrix_grads[1].astype(jnp.bfloat16), "context", scatter_dimension=0, tiled=True
        ).astype(jnp.float32),
        lax.psum_scatter(
            matrix_grads[2].astype(jnp.bfloat16), "context", scatter_dimension=0, tiled=True
        ).astype(jnp.float32),
        lax.psum_scatter(
            matrix_grads[3].astype(jnp.bfloat16), "context", scatter_dimension=1, tiled=True
        ).astype(jnp.float32),
    )


def body(
    block_input,
    norm_gain,
    w_gate,
    w_value,
    w_bc,
    w_dt,
    conv_value,
    conv_bc,
    conv_value_bias,
    conv_bc_bias,
    dt_bias,
    decay_log,
    skip,
    gate_gain,
    w_out,
    cotangent,
):
    sections = lax.axis_size("section")
    section_index = lax.axis_index("section")
    micro_count = block_input.shape[0]
    tick_count = micro_count + sections - 1
    gate_full, value_full, maps_full, step_full, out_full = (
        lax.all_gather(w_gate[0], "context", axis=0, tiled=True),
        lax.all_gather(w_value[0], "context", axis=0, tiled=True),
        lax.all_gather(w_bc[0], "context", axis=0, tiled=True),
        lax.all_gather(w_dt[0], "context", axis=0, tiled=True),
        lax.all_gather(w_out[0], "context", axis=1, tiled=True),
    )
    mix_full = jnp.concatenate([value_full, maps_full], axis=1)
    matrices = (gate_full, mix_full, step_full, out_full)
    small_params = (
        norm_gain[0],
        jnp.concatenate([conv_value[0], conv_bc[0]], axis=1),
        jnp.concatenate([conv_value_bias[0], conv_bc_bias[0]], axis=0),
        dt_bias[0],
        decay_log[0],
        skip[0],
        gate_gain[0],
    )
    is_first = section_index == 0
    is_last = section_index == sections - 1
    received = jnp.zeros(block_input.shape[1:], jnp.float32)
    sent_list = []
    kept_list = []
    for tick_index in range(tick_count):
        fresh_input = block_input[min(tick_index, micro_count - 1)].astype(jnp.float32)
        residual = jnp.where(is_first, fresh_input, received)
        result, kept_values = forward_layer(residual, matrices, small_params)
        kept_list.append(kept_values)
        sent_rows = result.astype(jnp.bfloat16)
        sent_list.append(sent_rows)
        received = from_behind(sent_rows, "section", 1).astype(jnp.float32)
    section_outputs = lax.dynamic_slice_in_dim(jnp.stack(sent_list), section_index, micro_count, 0)
    saved = tuple(
        (jnp.stack([kept[field] for kept in kept_list]) for field in range(len(kept_list[0])))
    )
    back_received = jnp.zeros(block_input.shape[1:], jnp.bfloat16)
    grad_list = []
    matrix_total = None
    small_total = None
    for tick_index in range(tick_count):
        micro_index = tick_index - (sections - 1 - section_index)
        is_valid = ((micro_index >= 0) & (micro_index < micro_count)).astype(jnp.float32)
        forward_tick = jnp.clip(micro_index + section_index, 0, tick_count - 1)
        out_grad = jnp.where(is_last, cotangent[min(tick_index, micro_count - 1)], back_received)
        kept_values = tuple(
            (lax.dynamic_index_in_dim(item, forward_tick, 0, False) for item in saved)
        )
        grad_residual, matrix_grads, small_grads_now = backward_layer(
            out_grad, kept_values, matrices, small_params
        )
        grad_list.append(grad_residual)
        matrix_grads = jax.tree.map(lambda item: item * is_valid, matrix_grads)
        small_grads_now = jax.tree.map(lambda item: item * is_valid, small_grads_now)
        if matrix_total is None:
            matrix_total = matrix_grads
            small_total = small_grads_now
        else:
            matrix_total = jax.tree.map(jnp.add, matrix_total, matrix_grads)
            small_total = jax.tree.map(jnp.add, small_total, small_grads_now)
        back_received = from_behind(grad_residual.astype(jnp.bfloat16), "section", -1)
    matrix_total = reduce_grads(matrix_total)
    small_sum = (
        lax.psum(small_total[0].astype(jnp.bfloat16), "context").astype(jnp.float32),
        lax.psum(small_total[1].astype(jnp.bfloat16), "context").astype(jnp.float32),
        lax.psum(small_total[2].astype(jnp.bfloat16), "context").astype(jnp.float32),
        lax.psum(small_total[3].astype(jnp.bfloat16), "context").astype(jnp.float32),
        lax.psum(small_total[4].astype(jnp.bfloat16), "context").astype(jnp.float32),
        lax.psum(small_total[5].astype(jnp.bfloat16), "context").astype(jnp.float32),
        lax.psum(small_total[6].astype(jnp.bfloat16), "context").astype(jnp.float32),
    )
    input_grads = lax.dynamic_slice_in_dim(
        jnp.stack(grad_list), sections - 1 - section_index, micro_count, 0
    )
    grad_gate_w, grad_mix_w, grad_step_w, grad_out_w = matrix_total
    mix_width = w_value.shape[2]
    return (
        section_outputs[None],
        input_grads[None],
        small_sum[0][None],
        grad_gate_w[None],
        grad_mix_w[:, :mix_width][None],
        grad_mix_w[:, mix_width:][None],
        grad_step_w[None],
        small_sum[1][:, :mix_width][None],
        small_sum[1][:, mix_width:][None],
        small_sum[2][:mix_width][None],
        small_sum[2][mix_width:][None],
        small_sum[3][None],
        small_sum[4][None],
        small_sum[5][None],
        small_sum[6][None],
        grad_out_w[None],
    )


def solution(mesh):
    placed = (
        P(None, "context", None),
        P("section", None),
        P("section", "context", "tensor"),
        P("section", "context", "tensor"),
        P("section", "context", None),
        P("section", "context", "tensor"),
        P("section", None, "tensor"),
        P("section", None, None),
        P("section", "tensor"),
        P("section", None),
        P("section", "tensor"),
        P("section", "tensor"),
        P("section", "tensor"),
        P("section", "tensor"),
        P("section", "tensor", "context"),
        P(None, "context", None),
    )
    return jax.shard_map(
        body,
        mesh=mesh,
        in_specs=placed,
        out_specs=(
            P("section", None, "context", None),
            P("section", None, "context", None),
            P("section", None),
            P("section", "context", "tensor"),
            P("section", "context", "tensor"),
            P("section", "context", None),
            P("section", "context", "tensor"),
            P("section", None, "tensor"),
            P("section", None, None),
            P("section", "tensor"),
            P("section", None),
            P("section", "tensor"),
            P("section", "tensor"),
            P("section", "tensor"),
            P("section", "tensor"),
            P("section", "tensor", "context"),
        ),
        check_vma=False,
    )
```

profile of v0, /device:TPU:0, one launch (start us, length us, event | category | flops | bytes accessed | tf_op | source)
XLA Modules:
  0.0 2011.9 jit_solution(1124349811615769035)
XLA Ops:
  11.0 11.9 all-gather.2
  27.4 11.6 all-gather.1
  39.1 12.8 all-gather.39.cloned.1.call-done
  66.6 11.5 all-gather.15
  78.2 14.9 all-gather.43.cloned.1.call-done
  102.4 38.7 %all-gather.41.cloned.1.call-done = f32[192,64,128]{2,1,0:T(8,128)} async-done(((f32[24,64,128]{2,1,0:T(8,128)}), f32[192,64,128]{2,1,0:T(8,128)}) %all-gather.41.cloned.1.call-update) | async-done | bytes 6291472 | tf_op jit(solution)/shard_map/all_gather | solution.py:26
  156.4 25.4 %all-gather.45.cloned.1.call-done = bf16[1,1536,1536]{1,2,0:T(8,128)(2,1)} async-done(((bf16[1,1536,192]{1,2,0:T(8,128)(2,1)}), bf16[1,1536,1536]{1,2,0:T(8,128)(2,1)}) %all-gather.45.cloned.1.call-update) | async-done | bytes 4718608 | tf_op jit(solution)/shard_map/all_gather | solution.py:284
  187.0 35.0 %all-reduce.82.cloned.1.call-done = f32[128,1536]{1,0:T(8,128)} async-done(((f32[128,1536]{1,0:T(8,128)}), f32[128,1536]{1,0:T(8,128)}) %all-reduce.82.cloned.1.call-update) | async-done | bytes 786448 | tf_op jit(solution)/shard_map/psum | solution.py:136
  256.7 12.7 all-gather.16
  278.8 35.9 %all-gather.47.cloned.1.call-done = f32[192,64,128]{2,1,0:T(8,128)} async-done(((f32[24,64,128]{2,1,0:T(8,128)}), f32[192,64,128]{2,1,0:T(8,128)}) %all-gather.47.cloned.1.call-update) | async-done | bytes 6291472 | tf_op jit(solution)/shard_map/all_gather | solution.py:26
  334.5 43.3 %all-reduce.84.cloned.1.call-done = f32[128,1536]{1,0:T(8,128)} async-done(((f32[128,1536]{1,0:T(8,128)}), f32[128,1536]{1,0:T(8,128)}) %all-reduce.84.cloned.1.call-update) | async-done | bytes 786448 | tf_op jit(solution)/shard_map/psum | solution.py:136
  410.2 12.7 all-gather.17
  432.1 36.0 %all-gather.49.cloned.1.call-done = f32[192,64,128]{2,1,0:T(8,128)} async-done(((f32[24,64,128]{2,1,0:T(8,128)}), f32[192,64,128]{2,1,0:T(8,128)}) %all-gather.49.cloned.1.call-update) | async-done | bytes 6291472 | tf_op jit(solution)/shard_map/all_gather | solution.py:26
  484.9 43.3 %all-reduce.86.cloned.1.call-done = f32[128,1536]{1,0:T(8,128)} async-done(((f32[128,1536]{1,0:T(8,128)}), f32[128,1536]{1,0:T(8,128)}) %all-reduce.86.cloned.1.call-update) | async-done | bytes 786448 | tf_op jit(solution)/shard_map/psum | solution.py:136
  564.4 12.9 all-gather.18
  586.7 35.6 %all-gather.51.cloned.1.call-done = f32[192,64,128]{2,1,0:T(8,128)} async-done(((f32[24,64,128]{2,1,0:T(8,128)}), f32[192,64,128]{2,1,0:T(8,128)}) %all-gather.51.cloned.1.call-update) | async-done | bytes 6291472 | tf_op jit(solution)/shard_map/all_gather | solution.py:26
  642.1 43.3 %all-reduce.88.cloned.1.call-done = f32[128,1536]{1,0:T(8,128)} async-done(((f32[128,1536]{1,0:T(8,128)}), f32[128,1536]{1,0:T(8,128)}) %all-reduce.88.cloned.1.call-update) | async-done | bytes 786448 | tf_op jit(solution)/shard_map/psum | solution.py:136
  730.2 13.3 all-gather.19
  755.8 26.4 %all-gather.53.cloned.1.call-done = f32[192,64,128]{2,1,0:T(8,128)} async-done(((f32[24,64,128]{2,1,0:T(8,128)}), f32[192,64,128]{2,1,0:T(8,128)}) %all-gather.53.cloned.1.call-update) | async-done | bytes 6291472 | tf_op jit(solution)/shard_map/all_gather | solution.py:26
  839.3 21.6 %all-gather.20 = f32[8,1,24]{2,1,0:T(1,128)S(1)} all-gather(f32[1,1,24]{2,1,0:T(1,128)S(1)} %fusion.826), channel_id=1, replica_groups=mesh['section'=2,'context'=8,'tensor'=2] {'context'}, dimensions={0}, use_global_device_ids=true | all-gather | bytes 864 | tf_op jit(solution)/shard_map/all_gather | solution.py:26
  875.9 10.9 all-gather.55.cloned.1.call-done
  886.8 9.7 while.135
  921.1 19.8 all-reduce.92.cloned.1.call-done
  954.5 25.5 %all-reduce.94.cloned.1.call-done = bf16[128,1536]{1,0:T(8,128)(2,1)} async-done(((bf16[128,1536]{1,0:T(8,128)(2,1)}), bf16[128,1536]{1,0:T(8,128)(2,1)}) %all-reduce.94.cloned.1.call-update) | async-done | bytes 393232 | tf_op jit(solution)/shard_map/psum | solution.py:219
  987.8 18.8 collective-permute-done.10
  1044.7 23.0 %all-gather.57.cloned.1.call-done = f32[192,64,128]{2,1,0:T(8,128)} async-done(((f32[24,64,128]{2,1,0:T(8,128)}), f32[192,64,128]{2,1,0:T(8,128)}) %all-gather.57.cloned.1.call-update) | async-done | bytes 6291472 | tf_op jit(solution)/shard_map/all_gather | solution.py:26
  1067.9 14.6 while.136
  1126.6 19.4 all-reduce.96.cloned.1.call-done
  1157.5 27.6 %all-reduce.98.cloned.1.call-done = bf16[128,1536]{1,0:T(8,128)(2,1)} async-done(((bf16[128,1536]{1,0:T(8,128)(2,1)}), bf16[128,1536]{1,0:T(8,128)(2,1)}) %all-reduce.98.cloned.1.call-update) | async-done | bytes 393232 | tf_op jit(solution)/shard_map/psum | solution.py:219
  1191.6 19.1 collective-permute-done.12
  1248.3 24.1 %all-gather.59.cloned.1.call-done = f32[192,64,128]{2,1,0:T(8,128)} async-done(((f32[24,64,128]{2,1,0:T(8,128)}), f32[192,64,128]{2,1,0:T(8,128)}) %all-gather.59.cloned.1.call-update) | async-done | bytes 6291472 | tf_op jit(solution)/shard_map/all_gather | solution.py:26
  1272.5 9.7 while.137
  1314.2 19.4 all-reduce.100.cloned.1.call-done
  1346.0 27.5 %all-reduce.102.cloned.1.call-done = bf16[128,1536]{1,0:T(8,128)(2,1)} async-done(((bf16[128,1536]{1,0:T(8,128)(2,1)}), bf16[128,1536]{1,0:T(8,128)(2,1)}) %all-reduce.102.cloned.1.call-update) | async-done | bytes 393232 | tf_op jit(solution)/shard_map/psum | solution.py:219
  1380.0 19.1 collective-permute-done.14
  1436.8 24.0 %all-gather.61.cloned.1.call-done = f32[192,64,128]{2,1,0:T(8,128)} async-done(((f32[24,64,128]{2,1,0:T(8,128)}), f32[192,64,128]{2,1,0:T(8,128)}) %all-gather.61.cloned.1.call-update) | async-done | bytes 6291472 | tf_op jit(solution)/shard_map/all_gather | solution.py:26
  1460.9 9.7 while.138
  1502.5 19.4 all-reduce.104.cloned.1.call-done
  1534.2 27.6 %all-reduce.106.cloned.1.call-done = bf16[128,1536]{1,0:T(8,128)(2,1)} async-done(((bf16[128,1536]{1,0:T(8,128)(2,1)}), bf16[128,1536]{1,0:T(8,128)(2,1)}) %all-reduce.106.cloned.1.call-update) | async-done | bytes 393232 | tf_op jit(solution)/shard_map/psum | solution.py:219
  1569.7 18.9 collective-permute-done.16
  1637.9 15.0 all-gather.63.cloned.1.call-done
  1653.0 10.0 while.139
  1803.8 18.8 add_convert_fusion
  1843.0 31.2 %reduce-scatter.9.cloned.1.call-done = bf16[192,1536]{1,0:T(8,128)(2,1)} async-done(((bf16[1536,1536]{1,0:T(8,128)(2,1)}), bf16[192,1536]{1,0:T(8,128)(2,1)}) %reduce-scatter.9.cloned.1.call-update) | async-done | bytes 589840 | tf_op jit(solution)/shard_map/reduce_scatter | solution.py:242
  1876.8 34.4 %reduce-scatter.13.cloned.1.call-done = bf16[192,24]{1,0:T(8,128)(2,1)} async-done(((bf16[1536,24]{1,0:T(8,128)(2,1)}), bf16[192,24]{1,0:T(8,128)(2,1)}) %reduce-scatter.13.cloned.1.call-update) | async-done | bytes 9232
  1912.7 27.9 %all-reduce.110.cloned.1.call-done = bf16[128,1536]{1,0:T(8,128)(2,1)} async-done(((bf16[128,1536]{1,0:T(8,128)(2,1)}), bf16[128,1536]{1,0:T(8,128)(2,1)}) %all-reduce.110.cloned.1.call-update) | async-done | bytes 393232 | tf_op jit(solution)/shard_map/psum | solution.py:219
  1942.2 24.0 %all-reduce.65 = (bf16[1792]{0:T(1024)(128)(2,1)S(1)}, bf16[1,1536]{1,0:T(2,128)(2,1)S(1)}, bf16[4,1792]{1,0:T(4,128)(2,1)S(1)}, bf16[1,24]{1,0:T(2,128)(2,1)S(1...) all-reduce(bf16[1792]{0:T(1024)(128)(2,1)S(1)} %add_convert_fusion., ...), channel_id=1, replica_groups=mesh['section'=2,'context'=8,'tensor'=2] {'context'}, use_global_device_ids=true, to_apply=%region_155.157 | all-reduce | flops 12104 | bytes 48416 | tf_op jit(solution)/shard_map/psum | solution.py:343
  1977.6 24.3 %reduce-scatter.11.cloned.1.call-done = bf16[192,1792]{1,0:T(8,128)(2,1)} async-done(((bf16[1536,1792]{1,0:T(8,128)(2,1)}), bf16[192,1792]{1,0:T(8,128)(2,1)}) %reduce-scatter.11.cloned.1.call-update) | async-done | bytes 688144 | tf_op jit(solution)/shard_map/reduce_scatter | solution.py:245
  (1362 shorter events, 971.6 us)
Async XLA Ops:
  7.2 44.7 %all-gather.39.cloned.1.call-start = ((), (), s32[]{:S(2)}) async-start(), calls=%async_computation.21 | async-start | bytes 5308416 | tf_op jit(solution)/shard_map/all_gather | solution.py:281
  7.9 85.2 %all-gather.43.cloned.1.call-start = ((), (), s32[]{:S(2)}) async-start(), calls=%async_computation.23 | async-start | bytes 5308416 | tf_op jit(solution)/shard_map/all_gather | solution.py:280
  8.7 132.4 %all-gather.41.cloned.1.call-start = ((), (), s32[]{:S(2)}) async-start(), calls=%async_computation.22 | async-start | bytes 7077888 | tf_op jit(solution)/shard_map/all_gather | solution.py:26
  55.2 3.0 collective-permute-start
  65.9 115.9 %all-gather.45.cloned.1.call-start = ((), (), s32[]{:S(2)}) async-start(), calls=%async_computation.24 | async-start | bytes 5308416 | tf_op jit(solution)/shard_map/all_gather | solution.py:284
  66.5 155.6 %all-reduce.82.cloned.1.call-start = ((), (), s32[]{:S(2)}) async-start(), calls=%async_computation.4 | async-start | bytes 1572864 | tf_op jit(solution)/shard_map/psum | solution.py:136
  187.0 127.7 %all-gather.47.cloned.1.call-start = ((), (), s32[]{:S(2)}) async-start(), calls=%async_computation.25 | async-start | bytes 7077888 | tf_op jit(solution)/shard_map/all_gather | solution.py:26
  224.2 12.7 collective-permute-start.1
  244.4 2.1 collective-permute-start.2
  256.6 121.2 %all-reduce.84.cloned.1.call-start = ((), (), s32[]{:S(2)}) async-start(), calls=%async_computation.5 | async-start | bytes 1572864 | tf_op jit(solution)/shard_map/psum | solution.py:136
  334.5 133.6 %all-gather.49.cloned.1.call-start = ((), (), s32[]{:S(2)}) async-start(), calls=%async_computation.26 | async-start | bytes 7077888 | tf_op jit(solution)/shard_map/all_gather | solution.py:26
  380.0 12.7 collective-permute-start.3
  397.9 2.1 collective-permute-start.4
  410.1 118.1 %all-reduce.86.cloned.1.call-start = ((), (), s32[]{:S(2)}) async-start(), calls=%async_computation.6 | async-start | bytes 1572864 | tf_op jit(solution)/shard_map/psum | solution.py:136
  484.8 137.5 %all-gather.51.cloned.1.call-start = ((), (), s32[]{:S(2)}) async-start(), calls=%async_computation.27 | async-start | bytes 7077888 | tf_op jit(solution)/shard_map/all_gather | solution.py:26
  530.4 12.7 collective-permute-start.5
  564.2 121.2 %all-reduce.88.cloned.1.call-start = ((), (), s32[]{:S(2)}) async-start(), calls=%async_computation.7 | async-start | bytes 1572864 | tf_op jit(solution)/shard_map/psum | solution.py:136
  642.1 140.1 %all-gather.53.cloned.1.call-start = ((), (), s32[]{:S(2)}) async-start(), calls=%async_computation.28 | async-start | bytes 7077888 | tf_op jit(solution)/shard_map/all_gather | solution.py:26
  687.8 13.0 collective-permute-start.7
  724.1 162.6 %all-gather.55.cloned.1.call-start = ((), (), s32[]{:S(2)}) async-start(), calls=%async_computation.29 | async-start | bytes 7077888 | tf_op jit(solution)/shard_map/all_gather | solution.py:26
  827.0 113.9 %all-reduce.92.cloned.1.call-start = ((), (), s32[]{:S(2)}) async-start(), calls=%async_computation.9 | async-start | bytes 131072 | tf_op jit(solution)/shard_map/psum | solution.py:185
  920.3 59.7 %all-reduce.94.cloned.1.call-start = ((), (), s32[]{:S(2)}) async-start(), calls=%async_computation.10 | async-start | bytes 786432 | tf_op jit(solution)/shard_map/psum | solution.py:219
  944.1 3.4 collective-permute-start.9
  952.4 115.4 %all-gather.57.cloned.1.call-start = ((), (), s32[]{:S(2)}) async-start(), calls=%async_computation.30 | async-start | bytes 7077888 | tf_op jit(solution)/shard_map/all_gather | solution.py:26
  984.3 22.3 %collective-permute-start.10 = (bf16[128,1536]{1,0:T(8,128)(2,1)}, bf16[128,1536]{1,0:T(8,128)(2,1)}, u32[]{:S(2)}, u32[]{:S(2)}) collective-permute-start(bf16[128,1536]{1,0:T(8,128)(2,1)} %fusion.890), channel_id=1, source_target_pairs={{16,0},{17,1},{18,2},{19,3},{20,4},{21,5},{22,6},{23,7},{24,8},{25... | collective-permute-start | bytes 1179656 | tf_op jit(solution)/shard_map/ppermute | solution.py:19
  1023.9 122.1 %all-reduce.96.cloned.1.call-start = ((), (), s32[]{:S(2)}) async-start(), calls=%async_computation.11 | async-start | bytes 131072 | tf_op jit(solution)/shard_map/psum | solution.py:185
  1125.4 59.7 %all-reduce.98.cloned.1.call-start = ((), (), s32[]{:S(2)}) async-start(), calls=%async_computation.12 | async-start | bytes 786432 | tf_op jit(solution)/shard_map/psum | solution.py:219
  1149.2 3.4 collective-permute-start.11
  1157.5 114.9 %all-gather.59.cloned.1.call-start = ((), (), s32[]{:S(2)}) async-start(), calls=%async_computation.31 | async-start | bytes 7077888 | tf_op jit(solution)/shard_map/all_gather | solution.py:26
  1188.7 22.0 %collective-permute-start.12 = (bf16[128,1536]{1,0:T(8,128)(2,1)S(1)}, bf16[128,1536]{1,0:T(8,128)(2,1)S(1)}, u32[]{:S(2)}, u32[]{:S(2)}) collective-permute-start(bf16[128,1536]{1,0:T(8,128)(2,1)S(1)} %fusion.887), channel_id=1, source_target_pairs={{16,0},{17,1},{18,2},{19,3},{20,4},{21,5},{22,6},{23,7},{24,8},{25... | collective-permute-start | bytes 1179656 | tf_op jit(solution)/shard_map/ppermute | solution.py:19
  1228.5 105.1 %all-reduce.100.cloned.1.call-start = ((), (), s32[]{:S(2)}) async-start(), calls=%async_computation.13 | async-start | bytes 131072 | tf_op jit(solution)/shard_map/psum | solution.py:185
  1313.0 60.5 %all-reduce.102.cloned.1.call-start = ((), (), s32[]{:S(2)}) async-start(), calls=%async_computation.14 | async-start | bytes 786432 | tf_op jit(solution)/shard_map/psum | solution.py:219
  1337.6 3.4 collective-permute-start.13
  1345.9 114.9 %all-gather.61.cloned.1.call-start = ((), (), s32[]{:S(2)}) async-start(), calls=%async_computation.32 | async-start | bytes 7077888 | tf_op jit(solution)/shard_map/all_gather | solution.py:26
  1377.2 22.0 %collective-permute-start.14 = (bf16[128,1536]{1,0:T(8,128)(2,1)S(1)}, bf16[128,1536]{1,0:T(8,128)(2,1)S(1)}, u32[]{:S(2)}, u32[]{:S(2)}) collective-permute-start(bf16[128,1536]{1,0:T(8,128)(2,1)S(1)} %fusion.888), channel_id=1, source_target_pairs={{16,0},{17,1},{18,2},{19,3},{20,4},{21,5},{22,6},{23,7},{24,8},{25... | collective-permute-start | bytes 1179656 | tf_op jit(solution)/shard_map/ppermute | solution.py:19
  1416.9 105.0 %all-reduce.104.cloned.1.call-start = ((), (), s32[]{:S(2)}) async-start(), calls=%async_computation.15 | async-start | bytes 131072 | tf_op jit(solution)/shard_map/psum | solution.py:185
  1501.3 60.6 %all-reduce.106.cloned.1.call-start = ((), (), s32[]{:S(2)}) async-start(), calls=%async_computation.16 | async-start | bytes 786432 | tf_op jit(solution)/shard_map/psum | solution.py:219
  1525.9 3.4 collective-permute-start.15
  1534.2 118.8 %all-gather.63.cloned.1.call-start = ((), (), s32[]{:S(2)}) async-start(), calls=%async_computation.33 | async-start | bytes 7077888 | tf_op jit(solution)/shard_map/all_gather | solution.py:26
  1566.2 22.3 %collective-permute-start.16 = (bf16[128,1536]{1,0:T(8,128)(2,1)}, bf16[128,1536]{1,0:T(8,128)(2,1)}, u32[]{:S(2)}, u32[]{:S(2)}) collective-permute-start(bf16[128,1536]{1,0:T(8,128)(2,1)} %fusion.889), channel_id=1, source_target_pairs={{16,0},{17,1},{18,2},{19,3},{20,4},{21,5},{22,6},{23,7},{24,8},{25... | collective-permute-start | bytes 1179656 | tf_op jit(solution)/shard_map/ppermute | solution.py:19
  1609.0 180.2 %all-reduce.108.cloned.1.call-start = ((), (), s32[]{:S(2)}) async-start(), calls=%async_computation.17 | async-start | bytes 131072 | tf_op jit(solution)/shard_map/psum | solution.py:185
  1700.5 123.0 %all-reduce.90.cloned.1.call-start = ((), (), s32[]{:S(2)}) async-start(), calls=%async_computation.8 | async-start | bytes 1572864 | tf_op jit(solution)/shard_map/psum | solution.py:136
  1705.5 134.3 %reduce-scatter.15.cloned.1.call-start = ((), (), s32[]{:S(2)}) async-start(), calls=%async_computation.35 | async-start | bytes 5308416
  1732.0 142.2 %reduce-scatter.9.cloned.1.call-start = ((), (), s32[]{:S(2)}) async-start(), calls=%async_computation.19 | async-start | bytes 5308416 | tf_op jit(solution)/shard_map/reduce_scatter | solution.py:242
  1752.5 158.7 %reduce-scatter.13.cloned.1.call-start = ((), (), s32[]{:S(2)}) async-start(), calls=%async_computation.34 | async-start | bytes 442368
  1789.1 151.5 %all-reduce.110.cloned.1.call-start = ((), (), s32[]{:S(2)}) async-start(), calls=%async_computation.18 | async-start | bytes 786432 | tf_op jit(solution)/shard_map/psum | solution.py:219
  1795.3 3.4 collective-permute-start.17
  1803.5 198.4 %reduce-scatter.11.cloned.1.call-start = ((), (), s32[]{:S(2)}) async-start(), calls=%async_computation.20 | async-start | bytes 6193152 | tf_op jit(solution)/shard_map/reduce_scatter | solution.py:245
  (306 other events, 11843.8 us)
Sparse Core Ops, SparseCore 0:
  9.9 41.9 all-gather.38
  53.8 39.2 all-gather.42
  95.6 45.5 all-gather.40
  142.9 38.9 all-gather.44
  187.1 34.9 all-reduce.81
  256.7 57.9 all-gather.46
  334.6 43.1 all-reduce.83
  410.2 57.8 all-gather.48
  484.9 43.1 all-reduce.85
  564.4 57.8 all-gather.50
  642.2 43.1 all-reduce.87
  724.2 57.8 all-gather.52
  827.1 59.5 all-gather.54
  920.4 20.4 all-reduce.91
  952.5 27.4 all-reduce.93
  1024.0 43.7 all-gather.56
  1125.5 20.4 all-reduce.95
  1157.6 27.4 all-reduce.97
  1228.6 43.7 all-gather.58
  1313.1 20.4 all-reduce.99
  1346.0 27.4 all-reduce.101
  1417.0 43.7 all-gather.60
  1501.4 20.4 all-reduce.103
  1534.3 27.4 all-reduce.105
  1609.2 43.7 all-gather.62
  1700.6 20.4 all-reduce.107
  1723.9 34.8 all-reduce.89
  1762.7 54.0 reduce-scatter.14
  1820.3 53.8 reduce-scatter.8
  1877.4 33.7 reduce-scatter.12
  1914.3 26.2 all-reduce.109
  1944.1 57.8 reduce-scatter.10
where the time goes:
time: 2030 us; the launch traced here: 2010 us
  waiting for transfers between devices  912 us (45%)
  matrix products  385 us (19%)
  other arithmetic  254 us (13%)
  blocking collectives  217 us (11%)
  local copies, waits for them, and re-layouts  181 us (9%)
  starting transfers between devices  41.8 us (2%)
    all_gather x10, waiting for transfers between devices, entering(): gathered = jax.tree.map(lambda a: lax.all_gather(a, axis), part)  270 us
    psum x5, waiting for transfers between devices, forward_layer(): branch = lax.psum(partial_out, 'tensor')  165 us
    psum x5, waiting for transfers between devices, backward_layer(): lax.psum(back_in.astype(jnp.bfloat16), 'tensor').astype(jnp.float32)  136 us
    all_gather x10, blocking collectives, entering(): gathered = jax.tree.map(lambda a: lax.all_gather(a, axis), part)  120 us
    ppermute x18, waiting for transfers between devices, from_behind(): return lax.ppermute(block, axis, route)  118 us
    psum x5, waiting for transfers between devices, backward_layer(): lax.psum(grad_mixed[:, mix_width:].astype(jnp.bfloat16), 'tensor')  77.9 us
    dot_general x15, matrix products, outputs(): inside = jnp.einsum('tsh,shp->thp', mixing, values, precision=highest)  65.9 us
    unnamed x45, other arithmetic  58.4 us
  transfers between devices with their start and end apart: 50, of which 47 were waited for; matrix products, arithmetic and copies ran while one was open for 16% of the time, Pallas kernels for 0%

commit v1 on v0

v1 whole, which is shorter than its diff:
```python
import functools

import jax
import jax.numpy as jnp
from jax import lax
from jax.experimental import pallas as pl
from jax.experimental.pallas import tpu as pltpu
from jax.sharding import PartitionSpec as P

HEAD_DIM = 64
STATE = 128
CONV = 4
MAPS = 2 * STATE
CHUNK = 128
LANES = 128
PIECES = 2

epsilon = 1e-05
bf16 = jnp.bfloat16
f32 = jnp.float32


def low_dot(a, b, contract):
    return lax.dot_general(
        a.astype(bf16), b.astype(bf16), ((contract[0], contract[1]), ((), ())), preferred_element_type=f32
    )


def mm(a, b):
    return low_dot(a, b, ((1,), (0,)))


def mm_nt(a, b):
    return low_dot(a, b, ((1,), (1,)))


def mm_tn(a, b):
    return low_dot(a, b, ((0,), (0,)))


def softplus(v):
    return jnp.maximum(v, 0.0) + jnp.log(1.0 + jnp.exp(-jnp.abs(v)))


def groups_of(width):
    return [
        (at, min(LANES, width - at), at // HEAD_DIM, min(LANES, width - at) // HEAD_DIM)
        for at in range(0, width, LANES)
    ]


def head_rows(width):
    return -(-(width // HEAD_DIM) // 16) * 16


def column(cols, head):
    return jnp.broadcast_to(cols[:, head : head + 1], (cols.shape[0], LANES))


def choose(first, second, lanes):
    if second is None:
        return first[:, :lanes]
    lane = lax.broadcasted_iota(jnp.int32, (first.shape[0], lanes), 1)
    return jnp.where(lane < HEAD_DIM, first, second)


def only(value, which, count):
    if count == 1:
        return value
    lane = lax.broadcasted_iota(jnp.int32, value.shape, 1)
    return jnp.where((lane < HEAD_DIM) == (which == 0), value, jnp.zeros_like(value))


def pieces_of(value, count):
    terms = []
    for _ in range(count):
        term = value.astype(bf16)
        terms.append(term)
        value = value - term.astype(f32)
    return terms


def mm3(a, b):
    (a_hi, a_lo), (b_hi, b_lo) = pieces_of(a, 2), pieces_of(b, 2)
    return mm(jnp.concatenate([a_hi, a_lo, a_hi], axis=1), jnp.concatenate([b_hi, b_hi, b_lo], axis=0))


def mm3_nt(a, b):
    (a_hi, a_lo), (b_hi, b_lo) = pieces_of(a, 2), pieces_of(b, 2)
    return mm_nt(jnp.concatenate([a_hi, a_lo, a_hi], axis=1), jnp.concatenate([b_hi, b_hi, b_lo], axis=1))


def sum_dot(value, zero_one, count):
    return sum(mm(term, zero_one) for term in pieces_of(value, count))


def iotas():
    row = lax.broadcasted_iota(jnp.int32, (CHUNK, CHUNK), 0)
    col = lax.broadcasted_iota(jnp.int32, (CHUNK, CHUNK), 1)
    return row, col


def conv_rows(pad, taps_ref, at, lanes):
    here = slice(at, at + lanes)
    pre = taps_ref[CONV : CONV + 1, here] + taps_ref[CONV - 1 : CONV, here] * pad[8 : 8 + CHUNK, here]
    for k in range(CONV - 1):
        first = 8 - (CONV - 1) + k
        pre = pre + taps_ref[k : k + 1, here] * pad[first : first + CHUNK, here]
    return pre


def decay_terms(dt_pre, heads_ref, rows, row, col):
    wide = dt_pre.T[:rows] + heads_ref[0:rows, :]
    dt = softplus(wide)
    log_decay = sum_dot(-heads_ref[rows : 2 * rows, :] * dt, (row <= col).astype(bf16), 3)
    cols = jnp.concatenate([log_decay, dt, jnp.zeros((CHUNK - 2 * rows, CHUNK), f32)], axis=0).T
    return wide, dt, log_decay, cols


def as_row(value):
    return jnp.sum(value.T, axis=0, keepdims=True)


def filled(value):
    rows, lanes = value.shape
    if lanes == LANES:
        return value
    return jnp.concatenate([value, jnp.zeros((rows, LANES - lanes), f32)], axis=1)


def as_column(row):
    return jnp.broadcast_to(row, (CHUNK, LANES)).T


def deal(part, parts, first, count, total, own_ref, send_ref):
    def one(c, _):
        index = first + c
        distance = (index % parts) ^ part
        rows = total[pl.ds(pl.multiple_of(c * CHUNK, CHUNK), CHUNK), :]

        @pl.when(distance == 0)
        def _():
            own_ref[index // parts] = rows

        @pl.when(distance != 0)
        def _():
            send_ref[jnp.maximum(distance - 1, 0), index // parts] = rows.astype(send_ref.dtype)

        return 0

    lax.fori_loop(0, count, one, 0)


def forward_kernel(keep, width, parts, per_step, part_ref, h_ref, w1_ref, wg_ref, wo_ref, norm_ref, taps_ref, heads_ref, inner_ref, s0_ref, tail0_ref, *rest):
    if keep:
        dn_ref, own_ref, send_ref, sums_ref, st_ref, tail_ref, xn_ref, vbd_ref, z_ref, y_ref, sin_ref, pad, gg, total = rest
    else:
        g_ref, sums_ref, st_ref, tail_ref, xn_ref, vbd_ref, z_ref, pad = rest
    mixed = width + MAPS
    rows = head_rows(width)
    step = pl.program_id(0)

    @pl.when(step == 0)
    def _():
        st_ref[...] = s0_ref[...]
        tail_ref[...] = tail0_ref[...]

    def norm(c, _):
        here = pl.ds(pl.multiple_of(c * 64, 64), 64)
        hf = h_ref[here, :].astype(f32)
        scale = lax.rsqrt(jnp.mean(hf * hf, axis=1, keepdims=True) + epsilon)
        xn_ref[here, :] = (hf * scale * norm_ref[...]).astype(bf16)
        return 0

    lax.fori_loop(0, per_step * 2, norm, 0)
    vbd_ref[...] = jnp.dot(xn_ref[...], w1_ref[...], preferred_element_type=f32)
    z_ref[...] = jnp.dot(xn_ref[...], wg_ref[...], preferred_element_type=f32)
    row, col = iotas()

    def chunk(c, _):
        here = pl.ds(pl.multiple_of(c * CHUNK, CHUNK), CHUNK)
        pad[0:8, :] = tail_ref[...]
        pad[8 : 8 + CHUNK, :] = vbd_ref[here, :mixed]
        tail_ref[...] = pad[CHUNK : CHUNK + 8, :]
        pre = conv_rows(pad, taps_ref, width, MAPS)
        maps = pre * jax.nn.sigmoid(pre)
        b, c_map = maps[:, :STATE], maps[:, STATE:]
        b_rows = b.T
        _, _, log_row, cols = decay_terms(vbd_ref[here, mixed:], heads_ref, rows, row, col)
        contact = jnp.where(row >= col, mm3(c_map, b_rows), 0.0)
        if keep:
            sin_ref[c] = st_ref[...]
        carried = mm3(c_map, st_ref[...])
        squares = jnp.zeros((CHUNK, LANES), f32)
        pulls = jnp.zeros((CHUNK, LANES), f32)
        for at, lanes, head, count in groups_of(width):
            span = slice(at, at + lanes)
            pre = conv_rows(pad, taps_ref, at, lanes)
            own = pre * jax.nn.sigmoid(pre)
            logs = [column(cols, head + j) for j in range(count)]
            steps = [column(cols, rows + head + j) for j in range(count)]
            log_x = choose(logs[0], logs[-1] if count == 2 else None, lanes)
            step_x = choose(steps[0], steps[-1] if count == 2 else None, lanes)
            last_x = log_x[CHUNK - 1 : CHUNK, :]
            xd = own * step_x
            mixing = [
                jnp.exp(jnp.minimum(logs[j] - log_row[head + j : head + j + 1, :], 0.0)) * contact
                for j in range(count)
            ]
            inside = mm3(
                jnp.concatenate(mixing, axis=1),
                jnp.concatenate([only(xd, j, count) for j in range(count)], axis=0),
            )
            y = inside + jnp.exp(log_x) * carried[:, span] + inner_ref[0:1, span] * own
            st_ref[:, span] = jnp.exp(last_x) * st_ref[:, span] + mm3(b_rows, jnp.exp(last_x - log_x) * xd)
            z = z_ref[here, span]
            g = y * (z * jax.nn.sigmoid(z))
            if keep:
                gg[here, span] = (g * inner_ref[1:2, span]).astype(bf16)
                y_ref[here, span] = y
            else:
                g_ref[here, span] = g
            squares = squares + filled(g * g)
            if keep:
                pulls = pulls + filled(dn_ref[here, span] * inner_ref[1:2, span] * g)
        sums_ref[0, c] = as_row(squares)
        if keep:
            sums_ref[1, c] = as_row(pulls)
        return 0

    lax.fori_loop(0, per_step, chunk, 0)
    if keep:
        total[...] = lax.dot_general(
            gg[...], wo_ref[...], (((1,), (1,)), ((), ())), preferred_element_type=f32
        )
        deal(part_ref[0], parts, step * per_step, per_step, total, own_ref, send_ref)


def out_kernel(parts, per_step, part_ref, g_ref, q_ref, inner_ref, wo_ref, own_ref, send_ref, n, total):
    def chunk(c, _):
        here = pl.ds(pl.multiple_of(c * CHUNK, CHUNK), CHUNK)
        q = as_column(q_ref[c])
        for at, lanes, _, _ in groups_of(n.shape[1]):
            span = slice(at, at + lanes)
            n[here, span] = (g_ref[here, span] * q[:, :lanes] * inner_ref[1:2, span]).astype(bf16)
        return 0

    lax.fori_loop(0, per_step, chunk, 0)
    total[...] = lax.dot_general(n[...], wo_ref[...], (((1,), (1,)), ((), ())), preferred_element_type=f32)
    deal(part_ref[0], parts, pl.program_id(0) * per_step, per_step, total, own_ref, send_ref)


def out_call(place, g, q, weights, inner):
    wo = weights[2]
    tokens, width = g.shape
    depth = wo.shape[0]
    chunks = tokens // CHUNK
    per_step = min(STEP, chunks)
    steps = chunks // per_step
    count = per_step * CHUNK
    blocks = chunks // place.parts
    shapes = [(blocks, CHUNK, depth), (place.parts - 1, blocks, CHUNK, depth)]
    return pl.pallas_call(
        functools.partial(out_kernel, place.parts, per_step),
        grid_spec=pltpu.PrefetchScalarGridSpec(
            num_scalar_prefetch=1,
            grid=(steps,),
            in_specs=[
                block(steps, (count, width), lambda i, _: (i, 0)),
                block(steps, (per_step, 1, LANES), lambda i, _: (i, 0, 0)),
                once(inner.shape),
                once(wo.shape),
            ],
            out_specs=[once(shape) for shape in shapes],
            scratch_shapes=[pltpu.VMEM((count, width), bf16), pltpu.VMEM((count, depth), f32)],
        ),
        out_shape=[jax.ShapeDtypeStruct(shape, f32) for shape in shapes],
        compiler_params=kernel_params(steps, 8),
        cost_estimate=pl.CostEstimate(
            flops=tokens * width * 6000, bytes_accessed=tokens * depth * 8, transcendentals=0
        ),
        name="out_forward",
    )(place.part.reshape(1), g, q[:, None], inner, wo)


STEP = 4
GAIN_ROW = CONV + 1
HEAD_ROW = CONV + 2


def kernel_params(steps, megabytes):
    return pltpu.CompilerParams(vmem_limit_bytes=(megabytes if steps == 1 else 40) * 1024 * 1024)


def once(shape):
    return pl.BlockSpec(memory_space=pltpu.VMEM)


def block(steps, shape, index_map):
    return once(shape) if steps == 1 else pl.BlockSpec(shape, index_map)


def forward_call(place, h, weights, small, s0, tail0, dn=None):
    w1, wg, wo = weights
    norm_gain, taps, heads, inner = small
    keep = dn is not None
    tokens, depth = h.shape
    width = inner.shape[1]
    mixed = width + MAPS
    chunks = tokens // CHUNK
    per_step = min(STEP, chunks)
    steps = chunks // per_step
    count = per_step * CHUNK
    blocks = chunks // place.parts
    rows = lambda lanes: block(steps, (count, lanes), lambda i, _: (i, 0))
    if keep:
        shapes = [((blocks, CHUNK, depth), f32), ((place.parts - 1, blocks, CHUNK, depth), bf16)]
        out_shape = [jax.ShapeDtypeStruct(*item) for item in shapes]
        out_specs = [once(shape) for shape, _ in shapes]
    else:
        out_shape = [jax.ShapeDtypeStruct((tokens, width), f32)]
        out_specs = [rows(width)]
    out_shape += [
        jax.ShapeDtypeStruct((2, chunks, 1, LANES), f32),
        jax.ShapeDtypeStruct((STATE, width), f32),
        jax.ShapeDtypeStruct((8, mixed), f32),
    ]
    out_specs += [
        block(steps, (2, per_step, 1, LANES), lambda i, _: (0, i, 0, 0)),
        once((STATE, width)),
        once((8, mixed)),
    ]
    in_specs = [
        rows(depth),
        once(w1.shape),
        once(wg.shape),
        once(wo.shape),
        once((1, depth)),
        once(taps.shape),
        once(heads.shape),
        once(inner.shape),
        once(s0.shape),
        once(tail0.shape),
    ]
    args = [h, w1, wg, wo, norm_gain[None], taps, heads, inner, s0, tail0]
    held = [((tokens, depth), bf16), ((tokens, w1.shape[1]), f32), ((tokens, width), f32)]
    scratch = []
    if keep:
        in_specs.append(rows(width))
        args.append(dn)
        held.append(((tokens, width), f32))
        out_shape += [jax.ShapeDtypeStruct(*item) for item in held]
        out_specs += [rows(shape[1]) for shape, _ in held]
        out_shape.append(jax.ShapeDtypeStruct((chunks, STATE, width), f32))
        out_specs.append(block(steps, (per_step, STATE, width), lambda i, _: (i, 0, 0)))
    else:
        scratch = [pltpu.VMEM((count, shape[1]), kind) for shape, kind in held]
    scratch.append(pltpu.VMEM((CHUNK + 8, mixed), f32))
    if keep:
        scratch += [pltpu.VMEM((count, width), bf16), pltpu.VMEM((count, depth), f32)]
    return pl.pallas_call(
        functools.partial(forward_kernel, keep, width, place.parts, per_step),
        grid_spec=pltpu.PrefetchScalarGridSpec(
            num_scalar_prefetch=1, grid=(steps,), in_specs=in_specs, out_specs=out_specs, scratch_shapes=scratch
        ),
        out_shape=out_shape,
        compiler_params=kernel_params(steps, 10 if keep else 11),
        cost_estimate=pl.CostEstimate(
            flops=tokens * width * 40000, bytes_accessed=tokens * depth * 16, transcendentals=0
        ),
        name="section_forward",
    )(place.part.reshape(1), *args)


def normal_kernel(full, width, per_step, e_ref, wo_ref, z_ref, y_ref, q_ref, inner_ref, dn_ref, pull_ref, n_ref, gain_ref, gains):
    dn_ref[...] = jnp.dot(e_ref[...], wo_ref[...], preferred_element_type=f32)

    @pl.when(pl.program_id(0) == 0)
    def _():
        gains[...] = jnp.zeros_like(gains)

    def chunk(c, _):
        here = pl.ds(pl.multiple_of(c * CHUNK, CHUNK), CHUNK)
        q = as_column(q_ref[c])
        pulls = jnp.zeros((CHUNK, LANES), f32)
        for at, lanes, _, _ in groups_of(width):
            span = slice(at, at + lanes)
            z, dn_x, gain = z_ref[here, span], dn_ref[here, span], inner_ref[1:2, span]
            g = y_ref[here, span] * (z * jax.nn.sigmoid(z))
            gq = g * q[:, :lanes]
            pulls = pulls + filled(dn_x * gain * g)
            n_ref[here, span] = (gq * gain).astype(bf16)
            gains[:, span] += fold(dn_x * gq)
        pull_ref[c] = as_row(pulls)
        return 0

    lax.fori_loop(0, per_step, chunk, 0)
    gain_ref[...] = jnp.broadcast_to(jnp.sum(gains[...], axis=0, keepdims=True), gains.shape)


def gate_kernel(width, per_step, total, dn_ref, z_ref, y_ref, q_ref, pull_ref, inner_ref, dy_ref, dz_ref):
    def chunk(c, _):
        here = pl.ds(pl.multiple_of(c * CHUNK, CHUNK), CHUNK)
        q = as_column(q_ref[c])
        pull = as_column(pull_ref[c]) * (q * q * q) * (1.0 / total)
        for at, lanes, _, _ in groups_of(width):
            span = slice(at, at + lanes)
            z, y = z_ref[here, span], y_ref[here, span]
            sig = jax.nn.sigmoid(z)
            silu = z * sig
            dg = q[:, :lanes] * (dn_ref[here, span] * inner_ref[1:2, span]) - y * silu * pull[:, :lanes]
            dy_ref[here, span] = dg * silu
            dz_ref[here, span] = (dg * y * (sig + silu * (1.0 - sig))).astype(bf16)
        return 0

    lax.fori_loop(0, per_step, chunk, 0)


def normal_call(e, weights, z, y, q, inner):
    wo = weights[2]
    tokens, depth = e.shape
    width = inner.shape[1]
    chunks = tokens // CHUNK
    per_step = min(STEP, chunks)
    steps = chunks // per_step
    rows = lambda lanes: block(steps, (per_step * CHUNK, lanes), lambda i: (i, 0))
    lines = block(steps, (per_step, 1, LANES), lambda i: (i, 0, 0))
    return pl.pallas_call(
        functools.partial(normal_kernel, True, width, per_step),
        grid=(steps,),
        in_specs=[rows(depth), once(wo.shape), rows(width), rows(width), lines, once(inner.shape)],
        out_specs=[rows(width), lines, rows(width), once((8, width))],
        out_shape=[
            jax.ShapeDtypeStruct((tokens, width), f32),
            jax.ShapeDtypeStruct((chunks, 1, LANES), f32),
            jax.ShapeDtypeStruct((tokens, width), bf16),
            jax.ShapeDtypeStruct((8, width), f32),
        ],
        scratch_shapes=[pltpu.VMEM((8, width), f32)],
        compiler_params=kernel_params(steps, 4),
        cost_estimate=pl.CostEstimate(
            flops=tokens * width * 9000, bytes_accessed=tokens * depth * 16, transcendentals=0
        ),
        name="norm_backward",
    )(e, wo, z, y, q, inner)


def gate_call(place, dn, z, y, q, pull, inner):
    tokens, width = dn.shape
    chunks = tokens // CHUNK
    per_step = min(STEP, chunks)
    steps = chunks // per_step
    rows = lambda lanes: block(steps, (per_step * CHUNK, lanes), lambda i: (i, 0))
    lines = block(steps, (per_step, 1, LANES), lambda i: (i, 0, 0))
    return pl.pallas_call(
        functools.partial(gate_kernel, width, per_step, place.tensors * place.parts * width),
        grid=(steps,),
        in_specs=[rows(width), rows(width), rows(width), lines, lines, once(inner.shape)],
        out_specs=[rows(width), rows(width)],
        out_shape=[jax.ShapeDtypeStruct((tokens, width), f32), jax.ShapeDtypeStruct((tokens, width), bf16)],
        compiler_params=kernel_params(steps, 4),
        cost_estimate=pl.CostEstimate(
            flops=tokens * width * 6000, bytes_accessed=tokens * width * 16, transcendentals=0
        ),
        name="gate_backward",
    )(dn, z, y, q, pull, inner)


def fold(value):
    return jnp.sum(value.reshape(CHUNK // 8, 8, value.shape[1]), axis=0)


def backward_kernel(
    exact,
    width,
    parts,
    per_step,
    steps,
    part_ref,
    dy_ref,
    dz_ref,
    vbd_ref,
    before_ref,
    sin_ref,
    w1_ref,
    wg_ref,
    taps_ref,
    heads_ref,
    inner_ref,
    g0_ref,
    du0_ref,
    own_ref,
    send_ref,
    dvbd_ref,
    gt_ref,
    dut_ref,
    tapg_ref,
    pad,
    dpad,
    sums,
    y_in,
    dxd_out,
    dy_in_all,
    xd_out_all,
    total,
    taps_sum,
    headg_ref,
    skipg_ref,
    back_all,
):
    mixed = width + MAPS
    rows = head_rows(width)
    step = steps - 1 - pl.program_id(0)

    @pl.when(pl.program_id(0) == 0)
    def _():
        gt_ref[...] = g0_ref[...]
        dut_ref[...] = du0_ref[...]
        taps_sum[...] = jnp.zeros_like(taps_sum)
        headg_ref[...] = jnp.zeros_like(headg_ref)
        skipg_ref[...] = jnp.zeros_like(skipg_ref)

    row, col = iotas()
    causal = col >= row
    strict = col > row
    onward = (row >= col).astype(bf16)
    head_of = lax.broadcasted_iota(jnp.int32, (rows, width), 1) // HEAD_DIM
    ones = (head_of == lax.broadcasted_iota(jnp.int32, (rows, width), 0)).astype(bf16)

    def conv_back(here, at, lanes, du):
        span = slice(at, at + lanes)
        dpad[0:CHUNK, span] = du
        m = pad[8 : 8 + CHUNK, span]
        taps_sum[CONV * 8 : CONV * 8 + 8, span] += fold(du)
        taps_sum[CONV * 8 - 8 : CONV * 8, span] += fold(m * du)
        dm = taps_ref[CONV - 1 : CONV, span] * du
        for k in range(CONV - 1):
            first = CONV - 1 - k
            moved = dpad[first : first + CHUNK, span]
            dm = dm + taps_ref[k : k + 1, span] * moved
            taps_sum[k * 8 : k * 8 + 8, span] += fold(m * moved)
        dvbd_ref[here, span] = dm.astype(bf16)

    def chunk(reverse, _):
        c = per_step - 1 - reverse
        here = pl.ds(pl.multiple_of(c * CHUNK, CHUNK), CHUNK)
        dpad[CHUNK : CHUNK + 8, :] = dut_ref[...]
        pad[8 : 8 + CHUNK, :] = vbd_ref[here, :mixed]

        @pl.when(c == 0)
        def _():
            pad[0:8, :] = before_ref[0]

        @pl.when(c != 0)
        def _():
            pad[0:8, :] = vbd_ref[pl.ds(pl.multiple_of(jnp.maximum(c * CHUNK - 8, 0), 8), 8), :mixed]

        pre = conv_rows(pad, taps_ref, width, MAPS)
        sig = jax.nn.sigmoid(pre)
        maps = pre * sig
        maps_slope = sig + maps * (1.0 - sig)
        b_maps, c_maps = maps[:, :STATE], maps[:, STATE:]
        b_low, c_low = b_maps.astype(bf16), c_maps.astype(bf16)
        wide, dt, log_row, cols = decay_terms(vbd_ref[here, mixed:], heads_ref, rows, row, col)
        contact = jnp.where(causal, mm_nt(b_low, c_low), 0.0)
        back_low = gt_ref[...].astype(bf16)
        if exact:
            back_all[...] = gt_ref[...]
        c_rows = c_low.T
        y_in[...] = mm(c_low, sin_ref[c])
        dxd_out[...] = mm(b_low, back_low)
        dcontact = jnp.zeros((CHUNK, CHUNK), f32)
        log_rows, through = [], []
        for at, lanes, head, count in groups_of(width):
            span = slice(at, at + lanes)
            pre = conv_rows(pad, taps_ref, at, lanes)
            sig = jax.nn.sigmoid(pre)
            own = pre * sig
            slope = sig + own * (1.0 - sig)
            logs = [column(cols, head + j) for j in range(count)]
            steps_of = [column(cols, rows + head + j) for j in range(count)]
            log_x = choose(logs[0], logs[-1] if count == 2 else None, lanes)
            step_x = choose(steps_of[0], steps_of[-1] if count == 2 else None, lanes)
            last_x = log_x[CHUNK - 1 : CHUNK, :]
            dy = dy_ref[here, span]
            xd = own * step_x
            xd_low = xd.astype(bf16)
            dy_low = dy.astype(bf16)
            to_end = jnp.exp(last_x - log_x)
            dy_in = jnp.exp(log_x) * dy
            dy_in_low = dy_in.astype(bf16)
            if exact:
                dy_in_all[:, span] = dy_in
                xd_out_all[:, span] = to_end * xd
                dmix = mm3_nt(jnp.concatenate([only(xd, j, count) for j in range(count)], axis=0), dy)
            else:
                dy_in_all[:, span] = dy_in_low
                xd_out_all[:, span] = (to_end * xd).astype(bf16)
                dmix = mm_nt(jnp.concatenate([only(xd_low, j, count) for j in range(count)], axis=0), dy_low)
            mixing, products = [], []
            for j in range(count):
                decay = jnp.exp(jnp.minimum(log_row[head + j : head + j + 1, :] - logs[j], 0.0))
                one = decay * contact
                d_one = dmix[j * CHUNK : (j + 1) * CHUNK]
                dcontact = dcontact + decay * d_one
                mixing.append(one.astype(bf16))
                products.append((one * d_one).astype(bf16))
            dxd_in = mm(
                jnp.concatenate(mixing, axis=1),
                jnp.concatenate([only(dy_low, j, count) for j in range(count)], axis=0),
            )
            later = mm(jnp.concatenate(products, axis=0), onward)
            for j in range(count):
                log_rows.append(
                    jnp.sum(jnp.where(strict, later[j * CHUNK : (j + 1) * CHUNK], 0.0), axis=0, keepdims=True)
                )
            from_end = to_end * dxd_out[:, span]
            dxd = dxd_in + from_end
            sums[0:CHUNK, span] = (dy_in * y_in[:, span]).astype(bf16)
            sums[CHUNK : 2 * CHUNK, span] = (xd * from_end).astype(bf16)
            sums[2 * CHUNK : 3 * CHUNK, span] = (own * dxd).astype(bf16)
            carried = jnp.exp(last_x)
            back = gt_ref[:, span]
            through.append(
                jnp.sum(carried * sin_ref[c, :, span].astype(f32) * back, axis=0, keepdims=True)
            )
            skipg_ref[:, span] += fold(dy * own)
            gt_ref[:, span] = carried * back + mm(c_rows, dy_in_low)
            conv_back(here, at, lanes, (step_x * dxd + inner_ref[0:1, span] * dy) * slope)
        dcontact = jnp.where(causal, dcontact, 0.0)
        if exact:
            db = mm3_nt(xd_out_all[...], back_all[...]) + mm3(dcontact, c_maps)
            dc = mm3_nt(dy_in_all[...], sin_ref[c]) + mm3(dcontact.T, b_maps)
        else:
            db = mm_nt(xd_out_all[...], back_low) + mm(dcontact, c_low)
            dc = mm_nt(dy_in_all[...], sin_ref[c]) + mm_tn(dcontact, b_low)
        conv_back(here, width, STATE, db * maps_slope[:, :STATE])
        conv_back(here, width + STATE, STATE, dc * maps_slope[:, STATE:])
        dut_ref[...] = dpad[0:8, :]

        by_token = mm_nt(ones, sums[...])
        entering = by_token[:, :CHUNK]
        leaving = by_token[:, CHUNK : 2 * CHUNK]
        direct = by_token[:, 2 * CHUNK :]
        ends = jnp.broadcast_to(jnp.concatenate(through, axis=1), (CHUNK, width))
        ends = sum(mm_nt(ones, term) for term in pieces_of(ends, 2))
        inside = log_rows
        if rows > len(log_rows):
            inside = log_rows + [jnp.zeros((rows - len(log_rows), CHUNK), f32)]
        dlog = (
            jnp.concatenate(inside, axis=0)
            + sum_dot(entering, onward, 2)
            + sum_dot(leaving, (row < col).astype(bf16), 2)
            + ends
        )
        rate = heads_ref[rows : 2 * rows, :]
        ddt_pre = (direct - rate * dlog) * jax.nn.sigmoid(wide)
        headg_ref[0:rows, :] += ddt_pre
        headg_ref[rows : 2 * rows, :] += -rate * dt * dlog
        ddt_cols = jnp.concatenate([ddt_pre, jnp.zeros((CHUNK - rows, CHUNK), f32)], axis=0).T
        dvbd_ref[here, mixed:] = ddt_cols.astype(bf16)
        return 0

    lax.fori_loop(0, per_step, chunk, 0)
    nt = (((1,), (1,)), ((), ()))
    total[...] = lax.dot_general(dvbd_ref[...], w1_ref[...], nt, preferred_element_type=f32)
    total[...] += lax.dot_general(dz_ref[...], wg_ref[...], nt, preferred_element_type=f32)

    @pl.when(pl.program_id(0) == steps - 1)
    def _():
        tapg_ref[...] = jnp.zeros_like(tapg_ref)
        for k in range(CONV + 1):
            tapg_ref[k : k + 1, :] = jnp.sum(taps_sum[k * 8 : k * 8 + 8, :], axis=0, keepdims=True)
        skips = jnp.broadcast_to(jnp.sum(skipg_ref[...], axis=0, keepdims=True), (CHUNK, width))
        skips = sum(mm_nt(ones, term) for term in pieces_of(skips, 3))
        by_head = jnp.broadcast_to(jnp.sum(headg_ref[...], axis=1, keepdims=True), (2 * rows, LANES))
        columns = jnp.concatenate([by_head, skips, jnp.zeros((CHUNK - 3 * rows, LANES), f32)], axis=0)
        tapg_ref[HEAD_ROW : HEAD_ROW + 1, 0:LANES] = columns.T[0:1]

    deal(part_ref[0], parts, step * per_step, per_step, total, own_ref, send_ref)


def backward_call(place, exact, dy, dz, vbd, before, states, weights, small, g0, du0):
    w1, wg, _ = weights
    _, taps, heads, inner = small
    tokens, width = dy.shape
    depth = w1.shape[0]
    mixed = width + MAPS
    chunks = tokens // CHUNK
    per_step = min(STEP, chunks)
    steps = chunks // per_step
    count = per_step * CHUNK
    blocks = chunks // place.parts
    rows = lambda lanes: block(steps, (count, lanes), lambda i, _: (steps - 1 - i, 0))
    deep = lambda number, height, lanes: block(
        steps, (number, height, lanes), lambda i, _: (steps - 1 - i, 0, 0)
    )
    shapes = [
        ((STATE, width), f32),
        ((8, mixed), f32),
        ((8, mixed), f32),
    ]
    results = pl.pallas_call(
        functools.partial(backward_kernel, exact, width, place.parts, per_step, steps),
        grid_spec=pltpu.PrefetchScalarGridSpec(
            num_scalar_prefetch=1,
            grid=(steps,),
            in_specs=[
                rows(width),
                rows(width),
                rows(vbd.shape[1]),
                deep(1, 8, mixed),
                deep(per_step, STATE, width),
                once(w1.shape),
                once(wg.shape),
                once(taps.shape),
                once(heads.shape),
                once(inner.shape),
                once(g0.shape),
                once(du0.shape),
            ],
            out_specs=[
                once((blocks, CHUNK, depth)),
                once((place.parts - 1, blocks, CHUNK, depth)),
                rows(vbd.shape[1]),
            ]
            + [once(shape) for shape, _ in shapes],
            scratch_shapes=[
                pltpu.VMEM((CHUNK + 8, mixed), f32),
                pltpu.VMEM((CHUNK + 8, mixed), f32),
                pltpu.VMEM((3 * CHUNK, width), bf16),
                pltpu.VMEM((CHUNK, width), f32),
                pltpu.VMEM((CHUNK, width), f32),
                pltpu.VMEM((CHUNK, width), f32 if exact else bf16),
                pltpu.VMEM((CHUNK, width), f32 if exact else bf16),
                pltpu.VMEM((count, depth), f32),
                pltpu.VMEM((8 * (CONV + 1), mixed), f32),
                pltpu.VMEM((2 * head_rows(width), LANES), f32),
                pltpu.VMEM((8, width), f32),
                pltpu.VMEM((STATE, width), f32),
            ],
        ),
        out_shape=[
            jax.ShapeDtypeStruct((blocks, CHUNK, depth), f32),
            jax.ShapeDtypeStruct((place.parts - 1, blocks, CHUNK, depth), bf16),
            jax.ShapeDtypeStruct(vbd.shape, bf16),
        ]
        + [jax.ShapeDtypeStruct(*item) for item in shapes],
        compiler_params=kernel_params(steps, 12),
        cost_estimate=pl.CostEstimate(
            flops=tokens * width * 60000, bytes_accessed=tokens * depth * 16, transcendentals=0
        ),
        name="section_backward",
    )(place.part.reshape(1), dy, dz, vbd, before, states, w1, wg, taps, heads, inner, g0, du0)
    own, send, dvbd, gt, dut, sums = results
    return own, send, dvbd, gt, dut, sums


def unpack_kernel(parts, heads, rows, part_ref, both_ref, *refs):
    locals_ref, outs = refs[:parts], refs[parts:]
    wide_ref, bias_ref, gain_ref, maps_ref, maps_bias_ref, norm_ref, heads_ref = outs
    width = wide_ref.shape[1] // parts
    part = part_ref[0]
    lane = lax.broadcasted_iota(jnp.int32, (1, LANES), 1)
    by_head = [jnp.zeros((1, LANES), f32) for _ in range(3)]
    for d in range(parts):
        owner = part ^ d
        here = pl.ds(pl.multiple_of(owner * width, HEAD_DIM), width)
        ref = locals_ref[d]
        if width % LANES == 0:
            wide_ref[:, here] = ref[0:CONV, 0:width]
            bias_ref[:, here] = ref[CONV : CONV + 1, 0:width]
            gain_ref[:, here] = ref[GAIN_ROW : GAIN_ROW + 1, 0:width]
        else:
            for p in range(parts):

                @pl.when(owner == p)
                def _():
                    there = slice(p * width, (p + 1) * width)
                    wide_ref[:, there] = ref[0:CONV, 0:width]
                    bias_ref[:, there] = ref[CONV : CONV + 1, 0:width]
                    gain_ref[:, there] = ref[GAIN_ROW : GAIN_ROW + 1, 0:width]

        for k in range(3):
            values = ref[HEAD_ROW : HEAD_ROW + 1, 0:LANES]
            for p in range(parts):
                moved = pltpu.roll(values, (p * heads - k * rows) % LANES, 1)
                chosen = (owner == p) & (lane >= p * heads) & (lane < (p + 1) * heads)
                by_head[k] = jnp.where(chosen, moved, by_head[k])
    heads_ref[...] = jnp.concatenate(by_head + [jnp.zeros((5, LANES), f32)], axis=0)
    maps_ref[...] = both_ref[0:CONV, width : width + MAPS]
    maps_bias_ref[...] = both_ref[CONV : CONV + 1, width : width + MAPS]
    norm_ref[...] = both_ref[8:9, 0 : norm_ref.shape[1]]


def unpack(place, both, by_part, width, heads, depth):
    total = place.parts * width
    shapes = [(CONV, total), (1, total), (1, total), (CONV, MAPS), (1, MAPS), (1, depth), (8, LANES)]
    return pl.pallas_call(
        functools.partial(unpack_kernel, place.parts, heads, head_rows(width)),
        grid_spec=pltpu.PrefetchScalarGridSpec(
            num_scalar_prefetch=1,
            grid=(1,),
            in_specs=[once(both.shape)] * (1 + place.parts),
            out_specs=[once(shape) for shape in shapes],
        ),
        out_shape=[jax.ShapeDtypeStruct(shape, f32) for shape in shapes],
        compiler_params=pltpu.CompilerParams(vmem_limit_bytes=4 * 1024 * 1024),
        name="unpack_small",
    )(place.part.reshape(1), both, *by_part)


class Place:
    def __init__(self, micro_count):
        self.context = lax.axis_size("context")
        self.micros = micro_count
        self.parts = self.context // micro_count
        self.tensors = lax.axis_size("tensor")
        index = lax.axis_index("context")
        self.micro = index // self.parts
        self.part = index % self.parts
        self.tensor = lax.axis_index("tensor")

    def swap_part(self, block, mask):
        return lax.ppermute(block, "context", [(i, i ^ mask) for i in range(self.context)])

    def swap_micro(self, block, mask):
        return self.swap_part(block, mask * self.parts)

    def swap_tensor(self, block, mask):
        return lax.ppermute(block, "tensor", [(i, i ^ mask) for i in range(self.tensors)])

    def next_section(self, block, step, flip):
        count, tensors = lax.axis_size("section"), self.tensors
        return lax.ppermute(
            block,
            ("section", "tensor"),
            [
                (i * tensors + t, (i + step) * tensors + (t ^ flip))
                for i in range(count)
                if 0 <= i + step < count
                for t in range(tensors)
            ],
        )


def pick(array, index, axis):
    return lax.dynamic_index_in_dim(array, index, axis, False)


def tie(*items):
    return lax.optimization_barrier(items)


def bits_of(count):
    masks = []
    mask = 1
    while mask < count:
        masks.append(mask)
        mask *= 2
    return masks


def order(blocks, index, axis):
    count = len(blocks)
    shape = list(blocks[0].shape)
    shape.insert(axis, count)
    place = lax.broadcasted_iota(jnp.int32, shape, axis) ^ index
    result = jnp.expand_dims(blocks[0], axis)
    for d in range(1, count):
        result = jnp.where(place == d, jnp.expand_dims(blocks[d], axis), result)
    return jnp.broadcast_to(result, shape)


def beside(blocks, index):
    count = len(blocks)
    if count == 2:
        return jnp.where(
            index == 0, jnp.concatenate(blocks, axis=-1), jnp.concatenate(blocks[::-1], axis=-1)
        )
    return jnp.concatenate(
        [pick(order(blocks, index, 0), i, 0) for i in range(count)], axis=-1
    )


def sum_all(place, block, micro=True, part=True, tensor=True):
    if part:
        for mask in bits_of(place.parts):
            block = block + place.swap_part(block, mask)
    if tensor:
        for mask in bits_of(place.tensors):
            block = block + place.swap_tensor(block, mask)
    if micro:
        for mask in bits_of(place.micros):
            block = block + place.swap_micro(block, mask)
    return block


def lay_kernel(sizes, widths, places_ref, *refs):
    pieces, outs, sems = refs[: len(sizes)], refs[len(sizes) : -1], refs[-1]
    copies, number = [], 0
    for piece, size in zip(pieces, sizes):
        for row in range(size):
            at = 0
            for k, lanes in enumerate(widths):
                copies.append(
                    pltpu.make_async_copy(
                        piece.at[row, :, pl.ds(at, lanes)], outs[k].at[places_ref[number]], sems.at[number, k]
                    )
                )
                at += lanes
            number += 1
    for one in copies:
        one.start()
    for one in copies:
        one.wait()


def lay_rows(pieces, places, widths):
    rows = pieces[0].shape[1]
    sizes = [piece.shape[0] for piece in pieces]
    count = sum(sizes)
    if any(lanes % LANES for lanes in widths):
        whole = jnp.zeros((count,) + pieces[0].shape[1:], pieces[0].dtype)
        for i, row in enumerate(row for piece in pieces for row in piece):
            whole = lax.dynamic_update_index_in_dim(whole, row, places[i], 0)
        whole = whole.reshape(count * rows, -1)
        starts = [sum(widths[:k]) for k in range(len(widths))]
        return [whole[:, at : at + lanes] for at, lanes in zip(starts, widths)]
    results = pl.pallas_call(
        functools.partial(lay_kernel, sizes, widths),
        grid_spec=pltpu.PrefetchScalarGridSpec(
            num_scalar_prefetch=1,
            grid=(1,),
            in_specs=[pl.BlockSpec(memory_space=pl.ANY)] * len(pieces),
            out_specs=[pl.BlockSpec(memory_space=pltpu.VMEM)] * len(widths),
            scratch_shapes=[pltpu.SemaphoreType.DMA((count, len(widths)))],
        ),
        out_shape=[jax.ShapeDtypeStruct((count, rows, lanes), pieces[0].dtype) for lanes in widths],
        compiler_params=pltpu.CompilerParams(vmem_limit_bytes=4 * 1024 * 1024),
        name="lay_rows",
    )(jnp.stack(places).astype(jnp.int32), *pieces)
    return [result.reshape(count * rows, -1) for result in results]


def gather_weights(place, w_gate, w_value, w_bc, w_dt, w_out):
    parts = place.parts
    columns = w_gate.shape[1]
    width = columns // parts
    heads = w_dt.shape[1] // parts
    out_t = w_out.T

    def columns_of(part):
        steps = lax.dynamic_slice_in_dim(w_dt, part * heads, heads, 1)
        steps = jnp.pad(steps, ((0, 0), (0, LANES - heads)))
        cuts = [lax.dynamic_slice_in_dim(array, part * width, width, 1) for array in (w_value, w_gate, out_t)]
        return jnp.concatenate([cuts[0], w_bc, steps, cuts[1], cuts[2]], axis=1)[None]

    pieces, places = [], []
    for p in range(parts):
        block = columns_of(place.part ^ p)
        if p:
            block = place.swap_part(block, p)
        masks = bits_of(place.micros)
        if p % 2:
            masks = masks[::-1]
        found, distances = [block], [0]
        for mask in masks:
            whole = found[0] if len(found) == 1 else jnp.concatenate(found, axis=0)
            found.append(place.swap_micro(whole, mask))
            distances += [distance ^ mask for distance in distances]
        pieces += found
        places += [(place.micro ^ distance) * parts + (place.part ^ p) for distance in distances]
    return lay_rows(pieces, places, [width + MAPS + LANES, width, width])


def whole_tokens(place, rows):
    return [pick(rows, place.micro, 0)] + [
        place.swap_micro(pick(rows, place.micro ^ d, 0), d) for d in range(1, place.micros)
    ]


def lay_tokens(place, blocks):
    held = order(blocks, place.micro, 0)
    whole = order([held] + [place.swap_part(held, d) for d in range(1, place.parts)], place.part, 1)
    size = place.micros // PIECES
    return [whole[i * size : (i + 1) * size].reshape(-1, held.shape[-1]) for i in range(PIECES)]


def spread_tokens(place, rows):
    micros, count, width = rows.shape
    view = rows.reshape(micros, place.tensors, count // place.tensors, width)
    got = [
        place.swap_micro(pick(pick(view, place.micro ^ d, 0), place.tensor, 0), d) for d in range(1, micros)
    ]
    shares = jnp.stack(got)
    both = [shares] + [place.swap_tensor(shares, d) for d in range(1, place.tensors)]
    own = pick(rows, place.micro, 0)
    return lay_tokens(
        place,
        [own]
        + [
            order([part[d] for part in both], place.tensor, 0).reshape(count, width)
            for d in range(micros - 1)
        ],
    )


def blocks_of(place, array):
    return array.reshape(place.micros // PIECES, place.parts, place.tensors, -1, array.shape[-1])


def own_share(place, array, flip=0):
    return pick(pick(blocks_of(place, array), place.part, 1), place.tensor ^ flip, 1)


def cut(place, block):
    return block.reshape(block.shape[:-2] + (place.tensors, -1, block.shape[-1]))


class Reduction:
    def __init__(self, place, own, send, kind=bf16):
        self.place, self.kind = place, kind
        sends = [send.reshape(own.shape)] if place.parts == 2 else [send[d] for d in range(place.parts - 1)]
        self.came = [place.swap_part(cut(place, block), d + 1) for d, block in enumerate(sends)]
        self.own = cut(place, own)

    def launch(self, others=None):
        place = self.place

        def side(tensor):
            return pick(self.own, tensor, 1) + sum(pick(block, tensor, 1).astype(f32) for block in self.came)

        going = [side(place.tensor ^ d).astype(self.kind) for d in range(1, place.tensors)]
        going, others = tie(going, others)
        self.kept = side(place.tensor)
        self.sent = [place.swap_tensor(block, d + 1) for d, block in enumerate(going)]
        return others

    def land(self, others):
        self.sent, others = tie(self.sent, others)
        return others

    def result(self):
        return self.kept + sum(block.astype(f32) for block in self.sent)


class Gathering:
    def __init__(self, place, shares, flip=0):
        self.place, self.shares, self.flip = place, shares, flip
        self.came = None

    def launch(self):
        place = self.place
        self.came = [[place.swap_tensor(share, d) for share in self.shares] for d in range(1, place.tensors)]

    def result(self):
        place = self.place
        came = tie(self.came)[0]
        held = [order(list(group), place.tensor ^ self.flip, 1) for group in zip(self.shares, *came)]
        came = tie([[place.swap_part(block, d) for block in held] for d in range(1, place.parts)])[0]
        whole = [order(list(group), place.part, 1) for group in zip(held, *came)]
        return [block.reshape((-1,) + share.shape[2:]) for block, share in zip(whole, self.shares)]


def gather_shares(place, shares, flip=0):
    gathering = Gathering(place, shares, flip)
    gathering.launch()
    return gathering.result()


class Homing:
    def __init__(self, place, own):
        self.place = place
        self.own = pick(own, place.micro, 0)
        self.sends = [pick(own, place.micro ^ d, 0) for d in range(1, place.micros)]

    def launch(self):
        self.came = [self.place.swap_micro(block, d + 1) for d, block in enumerate(self.sends)]

    def turn(self, others=None):
        place = self.place
        self.rows, others = tie(order([self.own] + self.came, place.micro, 0), others)
        self.swapped = [place.swap_tensor(self.rows, d) for d in range(1, place.tensors)]
        return others

    def result(self):
        return order([self.rows] + self.swapped, self.place.tensor, 1)


def rows_dot(a, b):
    return jnp.dot(a, b, preferred_element_type=f32)


def columns_dot(a, b):
    return lax.dot_general(a, b, (((0,), (0,)), ((), ())), preferred_element_type=f32)


def forward_piece(place, h, weights, small, carry, dn=None):
    results = forward_call(place, h, weights, small, carry[0], carry[1], dn)
    if dn is None:
        return results[:2], (results[2], results[3])
    kept = (h, carry[1]) + tuple(results[5:])
    return results[:3], (results[3], results[4]), kept


def forward_start(place, small):
    width = small[3].shape[1]
    return jnp.zeros((STATE, width), f32), jnp.zeros((8, width + MAPS), f32)


def factor_of(place, small, squares):
    return lax.rsqrt(squares / (place.tensors * place.parts * small[3].shape[1]) + epsilon)


def out_share(place, h, branch):
    return (own_share(place, h).astype(f32) + branch).astype(bf16)


def gates_piece(place, dn, q, pull, kept, small):
    _, _, _, _, z, y, _ = kept
    return gate_call(place, dn, z, y, q[:, None], pull[:, None], small[3])


def normal_piece(e, q, kept, weights, small):
    _, _, _, _, z, y, _ = kept
    dn, pull, n, gain = normal_call(e, weights, z, y, q[:, None], small[3])
    return dn, pull[:, 0], n, gain


def backward_piece(place, exact, gates, kept, weights, small, carry):
    _, before, _, vbd, _, _, states = kept
    mixed = small[3].shape[1] + MAPS
    count = min(STEP * CHUNK, vbd.shape[0])
    tails = vbd.reshape(-1, count, vbd.shape[1])[:-1, count - 8 :, :mixed]
    before = jnp.concatenate([before[None], tails], axis=0)
    own, send, dvbd, adjoint, du, sums = backward_call(
        place, exact, gates[0], gates[1], vbd, before, states, weights, small, carry[0], carry[1]
    )
    return (own, send), (adjoint, du), dvbd, sums


def input_grad(place, e, h, norm_gain, dxn):
    ho = own_share(place, h).astype(f32)
    eo = own_share(place, e).astype(f32)
    r = lax.rsqrt(jnp.mean(ho * ho, axis=2, keepdims=True) + epsilon)
    scaled = dxn * norm_gain
    grad = eo + r * scaled - ho * (r * r * r * jnp.mean(scaled * ho, axis=2, keepdims=True))
    return grad.astype(bf16), jnp.sum(dxn * ho * r, axis=(0, 1))


class Scatter:
    def __init__(self, place, arrays):
        self.place = place
        parts = place.parts
        shape = [2] * len(bits_of(place.micros))
        views = [array.reshape(place.micros, parts, -1, array.shape[1]) for array in arrays]
        self.held = [[view[:, p].reshape(shape + list(view.shape[2:])) for view in views] for p in range(parts)]
        self.came = [[] for _ in range(parts)]
        self.left = [sorted(bits_of(place.micros), reverse=True) for _ in range(parts)]

    def prepare(self):
        place = self.place
        self.out, self.masks = [], []
        for p, left in enumerate(self.left):
            mask = left[0] if p % 2 else left[-1]
            axis = left.index(mask)
            mine = (place.micro // mask) % 2

            def side(bit):
                total = jnp.concatenate([pick(block, bit, axis) for block in self.held[p]], axis=-1)
                for block in self.came[p]:
                    total = total.astype(f32) + pick(block, bit, axis).astype(f32)
                return total.astype(bf16)

            self.out.append(side(1 - mine))
            self.masks.append(mask)
            self.held[p] = [pick(block, mine, axis) for block in self.held[p]]
            self.came[p] = [pick(block, mine, axis) for block in self.came[p]]
            left.remove(mask)

    def launch(self):
        self.next = [self.place.swap_micro(block, mask) for block, mask in zip(self.out, self.masks)]

    def land(self):
        for p, block in enumerate(self.next):
            self.came[p].append(block)

    def trade(self):
        place = self.place
        chip = []
        for held, came in zip(self.held, self.came):
            total = jnp.concatenate(held, axis=-1).astype(f32)
            for block in came:
                total = total + block.astype(f32)
            chip.append(total)

        def chosen(index):
            result = chip[0]
            for p in range(1, place.parts):
                result = jnp.where(index == p, chip[p], result)
            return result

        result = [chosen(place.part)]
        for d in range(1, place.parts):
            result.append(place.swap_part(chosen(place.part ^ d).astype(bf16), d).astype(f32))
        return result


def body(
    block_input,
    norm_gain,
    w_gate,
    w_value,
    w_bc,
    w_dt,
    conv_value,
    conv_bc,
    conv_value_bias,
    conv_bc_bias,
    dt_bias,
    decay_log,
    skip,
    gate_gain,
    w_out,
    cotangent,
):
    sections = lax.axis_size("section")
    section = lax.axis_index("section")
    place = Place(block_input.shape[0])
    parts, part = place.parts, place.part
    width = w_gate.shape[2] // parts
    heads_here = w_dt.shape[2] // parts
    mixed = width + MAPS

    def share(vector, size):
        return lax.dynamic_slice_in_dim(vector, part * size, size, vector.ndim - 1)

    def padded(vector):
        return jnp.pad(vector, (0, head_rows(width) - heads_here))

    h0 = spread_tokens(place, block_input)
    weights = gather_weights(place, w_gate[0], w_value[0], w_bc[0], w_dt[0], w_out[0])
    taps = jnp.concatenate(
        [
            jnp.concatenate([share(conv_value[0], width), conv_bc[0]], axis=1),
            jnp.concatenate([share(conv_value_bias[0], width), conv_bc_bias[0]])[None],
            jnp.zeros((8 - CONV - 1, mixed), f32),
        ],
        axis=0,
    )
    own_skip = share(skip[0], heads_here)
    rate = jnp.exp(share(decay_log[0], heads_here))
    heads = jnp.concatenate([padded(share(dt_bias[0], heads_here)), padded(rate)])
    heads = jnp.broadcast_to(heads[:, None], (heads.size, LANES))
    inner = jnp.stack([jnp.repeat(own_skip, HEAD_DIM), share(gate_gain[0], width)])
    inner = jnp.concatenate([inner, jnp.zeros((6, width), f32)], axis=0)
    small = (norm_gain[0], taps, heads, inner)

    span = range(PIECES)
    first, last = section == 0, section == sections - 1
    flip = 1 if place.tensors > 1 else 0

    def leave(place_of, block, came, step, others):
        if came:
            newest = list(came)[-1]
            block, came[newest], others = tie(block, came[newest], others)
        else:
            block, others = tie(block, others)
        came[place_of] = place.next_section(block, step, flip if step > 0 else 0)
        return others

    def arrive(i, came, stays, originals, others, flip):
        block, others = tie(came[i], others)
        return jnp.where(stays, own_share(place, originals[i], flip), block), others

    came = None
    for turn in range(sections - 1):
        carry = forward_start(place, small)
        shares_in, came = came, {}
        pieces, halves, terms, e_blocks = list(h0), [], None, None
        for i in span:
            if shares_in is not None:
                share, terms = arrive(i, shares_in, first, h0, terms, flip)
                pieces[i] = gather_shares(place, [share], flip)[0]
            if i:
                pieces[i], halves[-1][1], cotangent = tie(pieces[i], halves[-1][1], cotangent)
                crossing = [place.swap_tensor(halves[-1][1], mask) for mask in bits_of(place.tensors)]
                if turn == 0 and i == 1:
                    e_blocks = whole_tokens(place, cotangent)
            terms, carry = forward_piece(place, pieces[i], weights, small, carry)
            if i:
                terms, crossing, e_blocks = tie(terms, crossing, e_blocks)
                halves[-1][1] = halves[-1][1] + sum(crossing)
            halves.append([terms[0], sum_all(place, terms[1][0, :, 0], micro=False, tensor=False)])
        halves[-1][1] = sum_all(place, halves[-1][1], micro=False, part=False)
        if turn == 0 and e_blocks is None:
            e_blocks = whole_tokens(place, cotangent)
        red = []
        for g, squares in halves:
            own, send = out_call(place, g, factor_of(place, small, squares), weights, small[3])
            red.append(Reduction(place, own, send, jnp.float16))
            red[-1].launch()
        if turn == 0:
            e0 = lay_tokens(place, e_blocks)
            e0, dn0 = red[0].land((e0, [rows_dot(e, weights[2]) for e in e0]))
        for i, item in enumerate(red):
            leave(i, out_share(place, pieces[i], item.result()), came, 1, None)
    if sections == 1:
        e0 = lay_tokens(place, whole_tokens(place, cotangent))
        dn0 = [rows_dot(e, weights[2]) for e in e0]

    carry = forward_start(place, small)
    kept, sums, lines, terms = [], [], [], None
    for i in span:
        h = h0[i]
        if came is not None:
            block, terms = arrive(i, came, first, h0, terms, flip)
            h = gather_shares(place, [block], flip)[0]
        terms, carry, keep = forward_piece(place, h, weights, small, carry, dn0[i])
        kept.append(keep)
        lines.append(terms[2][:, :, 0])
        sums.append(Reduction(place, terms[0], terms[1]))
    lines = sum_all(place, jnp.stack(lines), micro=False)
    qs = [factor_of(place, small, lines[i, 0]) for i in span]
    dots = [lines[i, 1] for i in span]

    def gradient_of(i, came, others):
        share, others = arrive(i, came, last, e0, others, 0)
        gathering = Gathering(place, [share])
        gathering.launch()
        return gathering, others

    def outputs_of():
        outs = []
        for k in span:
            branch = sums[k].result() * own_share(place, qs[k].reshape(-1, 1))
            outs.append(out_share(place, kept[k][0], branch))
        return Homing(place, jnp.concatenate(outs, axis=0))

    came, homing, ready = None, None, None
    es = list(e0)
    for turn in range(sections - 1):
        carry = forward_start(place, small)
        shares_in, came = came, {}
        es, terms = list(e0), None
        for i in reversed(span):
            dn, pull = dn0[i], dots[i]
            if shares_in is not None:
                ready, terms = gradient_of(i, shares_in, terms)
                es[i] = ready.result()[0]
                dn, pull, _, _ = normal_piece(es[i], qs[i], kept[i], weights, small)
                pull = sum_all(place, pull, micro=False)
            elif homing is None:
                for item in sums:
                    dn = item.launch(dn)
            gates = gates_piece(place, dn, qs[i], pull, kept[i], small)
            if i + 1 < PIECES:
                gates = leave(i + 1, share, came, -1, gates)
            terms, carry, _, _ = backward_piece(place, False, gates, kept[i], weights, small, carry)
            if i + 1 < PIECES:
                terms, came[i + 1] = tie(terms, came[i + 1])
            if homing is None:
                for item in sums:
                    terms = item.land(terms)
            red = Reduction(place, terms[0], terms[1])
            red.launch()
            if homing is None:
                homing = outputs_of()
            if not i and turn == sections - 2 and PIECES > 1:
                ready, _ = gradient_of(PIECES - 1, came, None)
                ready.came = red.land(ready.came)
            share, _ = input_grad(place, es[i], kept[i][0], norm_gain[0], red.result())
        leave(0, share, came, -1, None)
    if homing is None:
        for item in sums:
            item.launch()
        homing = outputs_of()

    carry = forward_start(place, small)
    red, matrix, small_sums, terms = [], [None] * 3, None, None

    def add(old, a, b):
        now = columns_dot(a, b)
        return now if old is None else old + now

    for i in reversed(span):
        if came is not None:
            if red or ready is None:
                ready, terms = gradient_of(i, came, terms)
            es[i] = ready.result()[0]
        dn, pull, n, gain_grad = normal_piece(es[i], qs[i], kept[i], weights, small)
        pull = sum_all(place, pull, micro=False)
        matrix[0] = add(matrix[0], es[i], n)
        pull, matrix[0] = tie(pull, matrix[0])
        if red:
            pull = homing.turn(red[-1].launch(pull))
        else:
            pull, homing.sends = tie(pull, homing.sends)
            homing.launch()
        gates = gates_piece(place, dn, qs[i], pull, kept[i], small)
        if not i:
            scatter = Scatter(place, [matrix[0].astype(bf16), add(matrix[1], kept[i][2], gates[1]).astype(bf16)])
            scatter.prepare()
            gates, scatter.out = tie(gates, scatter.out)
            scatter.launch()
        terms, carry, dvbd, now = backward_piece(place, True, gates, kept[i], weights, small, carry)
        if red:
            terms = red[-1].land(terms)
        else:
            homing.came, terms, gates, dvbd, now = tie(homing.came, terms, gates, dvbd, now)
            if PIECES == 1:
                homing.turn()
        now = [now, gain_grad]
        if i:
            red.append(Reduction(place, terms[0], terms[1]))
            for k, b in ((1, gates[1]), (2, dvbd)):
                matrix[k] = add(matrix[k], kept[i][2], b)
        else:
            ahead = Reduction(place, terms[0], terms[1])
            ahead.own, dvbd, now, scatter.next, homing.swapped = tie(
                ahead.own, dvbd, now, scatter.next, homing.swapped
            )
            scatter.land()
            red.append(ahead)
        small_sums = now if small_sums is None else [a + b for a, b in zip(small_sums, now)]
    outputs = homing.result().reshape(block_input.shape)
    mixes = Scatter(place, [add(matrix[2], kept[0][2], dvbd).astype(bf16)])
    grads, norm_grad = [], 0.0
    for i, item in zip(reversed(span), red[:-1]):
        block, now = input_grad(place, es[i], kept[i][0], norm_gain[0], item.result())
        grads.insert(0, block)
        norm_grad = norm_grad + now
    for one in (mixes, scatter):
        one.prepare()
    mixes.out, scatter.out = red[-1].launch((mixes.out, scatter.out))
    for one in (scatter, mixes):
        one.launch()
    scatter.next = red[-1].land(scatter.next)
    block, now = input_grad(place, es[0], kept[0][0], norm_gain[0], red[-1].result())
    norm_grad = norm_grad + now
    homing = Homing(place, jnp.concatenate([block] + grads, axis=0))
    homing.launch()
    homing.came, mixes.next = tie(homing.came, mixes.next)
    homing.turn()
    mixes.land()
    mixes.prepare()
    mixes.launch()
    for one in (scatter, mixes):
        one.land()
        while one.left[0]:
            one.prepare()
            one.launch()
            one.land()
    input_grads = homing.result().reshape(block_input.shape).astype(f32)
    scatter, mixes = scatter.trade(), mixes.trade()
    gates = [block[:, width:] for block in scatter]
    out_t = [block[:, :width] for block in scatter]
    gate_grad = beside(gates, part)
    out_grad = order([block.T for block in out_t], part, 0).reshape(-1, w_out.shape[2])
    value_grad = beside([block[:, :width] for block in mixes], part)
    step_grad = beside([block[:, mixed : mixed + heads_here] for block in mixes], part)
    maps_grad = sum(block[:, width:mixed] for block in mixes).astype(bf16)
    maps_sum = maps_grad.astype(f32)
    for mask in bits_of(place.tensors):
        maps_sum = maps_sum + place.swap_tensor(maps_sum, mask)

    packed, gain_grad = small_sums
    row = lax.broadcasted_iota(jnp.int32, (8, mixed), 0)
    packed = jnp.where(row == GAIN_ROW, jnp.pad(gain_grad, ((0, 0), (0, MAPS))), packed)
    lanes = max(mixed, norm_grad.size)
    packed = jnp.concatenate(
        [jnp.pad(packed, ((0, 0), (0, lanes - mixed))), jnp.pad(norm_grad[None], ((0, 7), (0, lanes - norm_grad.size)))],
        axis=0,
    )
    packed, homing.rows = tie(packed, homing.rows)
    packed = sum_all(place, packed, part=False, tensor=False)
    by_part = [packed] + [place.swap_part(packed, d) for d in range(1, parts)]
    both = by_part[0]
    for distance in range(1, parts):
        both = both + by_part[distance]
    both = sum_all(place, both, micro=False, part=False)
    wide, bias_grad, gain_grad, maps_small, maps_bias, norm_sum, by_head = unpack(
        place, both, by_part, width, heads_here, norm_grad.size
    )
    total_heads = parts * heads_here
    return (
        outputs[None],
        input_grads[None],
        norm_sum,
        gate_grad[None],
        value_grad[None],
        maps_sum[None],
        step_grad[None],
        wide[None],
        maps_small[None],
        bias_grad,
        maps_bias,
        by_head[0:1, :total_heads],
        by_head[1:2, :total_heads],
        by_head[2:3, :total_heads],
        gain_grad,
        out_grad[None],
    )


def solution(mesh):
    placed = (
        P(None, "context", None),
        P("section", None),
        P("section", "context", "tensor"),
        P("section", "context", "tensor"),
        P("section", "context", None),
        P("section", "context", "tensor"),
        P("section", None, "tensor"),
        P("section", None, None),
        P("section", "tensor"),
        P("section", None),
        P("section", "tensor"),
        P("section", "tensor"),
        P("section", "tensor"),
        P("section", "tensor"),
        P("section", "tensor", "context"),
        P(None, "context", None),
    )
    return jax.shard_map(
        body,
        mesh=mesh,
        in_specs=placed,
        out_specs=(
            P("section", None, "context", None),
            P("section", None, "context", None),
            P("section", None),
            P("section", "context", "tensor"),
            P("section", "context", "tensor"),
            P("section", "context", None),
            P("section", "context", "tensor"),
            P("section", None, "tensor"),
            P("section", None, None),
            P("section", "tensor"),
            P("section", None),
            P("section", "tensor"),
            P("section", "tensor"),
            P("section", "tensor"),
            P("section", "tensor"),
            P("section", "tensor", "context"),
        ),
        check_vma=False,
    )
```

time: 2030 us -> 557 us (0.27)
  waiting for transfers between devices: 912 us -> 156 us
  matrix products: 385 us -> 17.8 us
  blocking collectives: 217 us -> 0 us
  other arithmetic: 254 us -> 75 us
  Pallas kernels: 0 us -> 141 us
  local copies, waits for them, and re-layouts: 181 us -> 80.9 us
  starting transfers between devices: 41.8 us -> 78.5 us
    psum x15 -> x0, waiting for transfers between devices: 379 us -> none  [the longest x5 165 us: forward_layer(): branch = lax.psum(partial_out, 'tensor')]
    dot_general x135 -> x8, matrix products: 385 us -> 17.8 us  [the longest x6 12.7 us: columns_dot(): lax.dot_general(a, b, (((0,), (0,)), ((), ())), preferred_element_type=f32)]
    all_gather x13 -> x0, waiting for transfers between devices: 323 us -> none  [the longest x10 270 us: entering(): gathered = jax.tree.map(lambda a: lax.all_gather(a, axis), part)]
    all_gather x12 -> x0, blocking collectives: 143 us -> none  [the longest x10 120 us: entering(): gathered = jax.tree.map(lambda a: lax.all_gather(a, axis), part)]
    pallas_call x0 -> x18, Pallas kernels: none -> 141 us  [the longest x4 71.9 us: backward_call(): pl.pallas_call(functools.partial(backward_kernel, exact, width, place.par...]
    psum x11 -> x0, blocking collectives: 73.3 us -> none  [the longest x5 24.7 us: forward_layer(): squares = lax.psum(jnp.sum(gated * gated, axis=1), 'tensor')]
    reduce_sum x45 -> x3, other arithmetic: 71.4 us -> 7.62 us  [the longest x2 6.13 us: input_grad(): r = lax.rsqrt(jnp.mean(ho * ho, axis=2, keepdims=True) + epsilon)]
    unnamed x45 -> x2, other arithmetic: 58.4 us -> 1.3 us
  transfers between devices with their start and end apart: 50 -> 75, of which waited for: 47 -> 37; matrix products, arithmetic and copies ran while one was open for 16% -> 22% of each run, Pallas kernels for 0% -> 22%
where the time goes in v1:
time: 557 us; the launch traced here: 552 us
  waiting for transfers between devices  156 us (28%)
  Pallas kernels  141 us (25%)
  local copies, waits for them, and re-layouts  80.9 us (15%)
  starting transfers between devices  78.5 us (14%)
  other arithmetic  75 us (13%)
  matrix products  17.8 us (3%)
    ppermute x49, waiting for transfers between devices, swap_part(): lax.ppermute(block, 'context', [(i, i ^ mask) for i in range(self.context)])  82.5 us
    pallas_call x4, Pallas kernels, backward_call(): pl.pallas_call(functools.partial(backward_kernel, exact, width, place.par...  71.9 us
    ppermute x22, waiting for transfers between devices, swap_tensor(): lax.ppermute(block, 'tensor', [(i, i ^ mask) for i in range(self.tensors)])  63.8 us
    pallas_call x4, Pallas kernels, forward_call(): pl.pallas_call(functools.partial(forward_kernel, keep, width, place.parts...  51.2 us
    unnamed x404, local copies, waits for them, and re-layouts  38.5 us
    ppermute x49, starting transfers between devices, swap_part(): lax.ppermute(block, 'context', [(i, i ^ mask) for i in range(self.context)])  35.7 us
    ppermute x22, starting transfers between devices, swap_tensor(): lax.ppermute(block, 'tensor', [(i, i ^ mask) for i in range(self.tensors)])  29.7 us
    select_n x16, other arithmetic, order(): result = jnp.where(place == d, jnp.expand_dims(blocks[d], axis), result)  24.5 us
  transfers between devices with their start and end apart: 75, of which 37 were waited for; matrix products, arithmetic and copies ran while one was open for 22% of the time, Pallas kernels for 22%

profile of v1, /device:TPU:0, one launch (start us, length us, event | category | flops | bytes accessed | tf_op | source)
XLA Modules:
  0.0 552.3 jit_solution(519518696854493503)
XLA Ops:
  2.8 3.0 collective-permute-start.1
  15.1 2.5 collective-permute-done
  24.0 8.8 %collective-permute-done.3 = bf16[3,64,1536]{2,1,0:T(8,128)(2,1)} collective-permute-done((bf16[3,64,1536]{2,1,0:T(8,128)(2,1)}, bf16[3,64,1536]{2,1,0:T(8,128)(2,1)}, u32[]{:S(2)}, u32[]{:S(2)}) %collective-permute-start.3) | collective-permute-done | bytes 589856 | tf_op jit(solution)/shard_map/ppermute | solution.py:831
  41.8 5.4 collective-permute-done.8.refs_4_
  53.3 35.6 %collective-permute-done.6.refs_2_ = bf16[2,192,2688]{2,1,0:T(8,128)(2,1)} collective-permute-done((bf16[2,192,2688]{2,1,0:T(8,128)(2,1)}, bf16[2,192,2688]{2,1,0:T(8,128)(2,1)}, u32[]{:S(2)}, u32[]{:S(2)}) %collective-permute-start.6) | collective-permute-done | bytes 2064416 | tf_op jit(solution)/shard_map/ppermute | solution.py:825
  89.9 3.6 lay_rows.1
  93.7 11.4 %section_forward.4 = (f32[512,768]{1,0:T(8,128)S(1)}, f32[2,4,1,128]{3,2,1,0:T(1,128)S(1)}, f32[128,768]{1,0:T(8,128)S(1)}, f32[8,1024]{1,0:T(8,128)S(1)}) custom-call(s32[1]{0:T(128)} %bitcast.part_ref, bf16[512,1536]{1,0:T(8,128)(2,1)S(1)} %bitcast.551, bf16[1536,1152]{1,0:T(8,128)(2,1)S(1)} %bitcast.599, bf16[1536,768]{1,0:T(8,128)(2,1)S(1)} %bitcast.607, ...), custom_call_target="tpu_custom_call" | custom-call | flops 15728640000 | bytes 12582912 | tf_op jit(solution)/shard_map/section_forward/pallas_call | solution.py:361
  111.1 12.0 %section_forward.5 = (f32[512,768]{1,0:T(8,128)S(1)}, f32[2,4,1,128]{3,2,1,0:T(1,128)S(1)}, f32[128,768]{1,0:T(8,128)}, f32[8,1024]{1,0:T(8,128)}) custom-call(s32[1]{0:T(128)} %bitcast.part_ref, bf16[512,1536]{1,0:T(8,128)(2,1)S(1)} %bitcast.548, bf16[1536,1152]{1,0:T(8,128)(2,1)S(1)} %bitcast.600, bf16[1536,768]{1,0:T(8,128)(2,1)S(1)} %bitcast.608, ...), custom_call_target="tpu_custom_call" | custom-call | flops 15728640000 | bytes 12582912 | tf_op jit(solution)/shard_map/section_forward/pallas_call | solution.py:361
  123.2 4.7 collective-permute-done.13
  136.1 2.5 collective-permute-done.19
  141.7 2.5 out_forward.3
  149.2 2.6 copy-done.58
  151.8 2.5 fusion.111.rest_0_.dn_ref
  154.3 2.5 fusion.112.rest_0_.dn_ref
  159.6 4.9 collective-permute-start.22
  164.5 3.7 collective-permute-done.21
  169.2 6.0 %collective-permute-done.22 = bf16[2,64,1536]{2,1,0:T(8,128)(2,1)S(1)} collective-permute-done((bf16[2,64,1536]{2,1,0:T(8,128)(2,1)S(1)}, bf16[2,64,1536]{2,1,0:T(8,128)(2,1)S(1)}, u32[]{:S(2)}, u32[]{:S(2)}) %collective-permute-start.22) | collective-permute-done | bytes 393248 | tf_op jit(solution)/shard_map/ppermute | solution.py:835
  175.2 6.7 %collective-permute-start.24 = (bf16[2,64,1536]{2,1,0:T(8,128)(2,1)S(1)}, bf16[2,64,1536]{2,1,0:T(8,128)(2,1)S(1)}, u32[]{:S(2)}, u32[]{:S(2)}) collective-permute-start(bf16[2,64,1536]{2,1,0:T(8,128)(2,1)S(1)} %bitcast_select_fusion.6), channel_id=1, source_target_pairs={{0,1},{1,0},{2,3},{3,2},{4,5},{5,4},{6,7},{7,6},{8,9},{9,8},{10,11... | collective-permute-start | bytes 1179656 | tf_op jit(solution)/shard_map/ppermute | solution.py:831
  181.9 8.6 %collective-permute-done.24 = bf16[2,64,1536]{2,1,0:T(8,128)(2,1)S(1)} collective-permute-done((bf16[2,64,1536]{2,1,0:T(8,128)(2,1)S(1)}, bf16[2,64,1536]{2,1,0:T(8,128)(2,1)S(1)}, u32[]{:S(2)}, u32[]{:S(2)}) %collective-permute-start.24) | collective-permute-done | bytes 393248 | tf_op jit(solution)/shard_map/ppermute | solution.py:831
  192.9 5.4 collective-permute-start.23
  205.7 13.5 %section_forward.6 = (f32[2,128,1536]{2,1,0:T(8,128)S(1)}, bf16[1,2,128,1536]{3,2,1,0:T(8,128)(2,1)S(1)}, f32[2,4,1,128]{3,2,1,0:T(1,128)S(1)}, f32[128,768]{1,0...) custom-call(s32[1]{0:T(128)} %bitcast.part_ref, ...), custom_call_target="tpu_custom_call" | custom-call | flops 15728640000 | bytes 12582912 | tf_op jit(solution)/shard_map/section_forward/pallas_call | solution.py:361
  223.8 10.3 %collective-permute-done.26 = bf16[2,64,1536]{2,1,0:T(8,128)(2,1)S(1)} collective-permute-done((bf16[2,64,1536]{2,1,0:T(8,128)(2,1)S(1)}, bf16[2,64,1536]{2,1,0:T(8,128)(2,1)S(1)}, u32[]{:S(2)}, u32[]{:S(2)}) %collective-permute-start.26) | collective-permute-done | bytes 393248 | tf_op jit(solution)/shard_map/ppermute | solution.py:831
  237.8 14.3 %section_forward.7 = (f32[2,128,1536]{2,1,0:T(8,128)S(1)}, bf16[1,2,128,1536]{3,2,1,0:T(8,128)(2,1)S(1)}, f32[2,4,1,128]{3,2,1,0:T(1,128)S(1)}, f32[128,768]{1,0...) custom-call(s32[1]{0:T(128)} %bitcast.part_ref, ...), custom_call_target="tpu_custom_call" | custom-call | flops 15728640000 | bytes 12582912 | tf_op jit(solution)/shard_map/section_forward/pallas_call | solution.py:361
  260.7 17.0 %section_backward.4 = (f32[2,128,1536]{2,1,0:T(8,128)S(1)}, bf16[1,2,128,1536]{3,2,1,0:T(8,128)(2,1)S(1)}, bf16[512,1152]{1,0:T(8,128)(2,1)}, f32[128,768]{1,0:T...) custom-call(s32[1]{0:T(128)} %bitcast.part_ref, f32[512,768]{1,0:T(8,128)S(1)} %get-tuple-element.216.dy_ref, ...), custom_call_target="tpu_custom_call" | custom-call | flops 23592960000 | bytes 12582912 | tf_op jit(solution)/shard_map/section_backward/pallas_call | solution.py:703
  297.0 3.6 fusion.9
  300.6 2.5 fusion.12
  304.5 17.2 %section_backward.5 = (f32[2,128,1536]{2,1,0:T(8,128)S(1)}, bf16[1,2,128,1536]{3,2,1,0:T(8,128)(2,1)S(1)}, bf16[512,1152]{1,0:T(8,128)(2,1)}, f32[128,768]{1,0:T...) custom-call(s32[1]{0:T(128)} %bitcast.part_ref, f32[512,768]{1,0:T(8,128)S(1)} %get-tuple-element.230.dy_ref, ...), custom_call_target="tpu_custom_call" | custom-call | flops 23592960000 | bytes 12582912 | tf_op jit(solution)/shard_map/section_backward/pallas_call | solution.py:703
  321.8 3.7 collective-permute-done.36
  337.0 3.7 collective-permute-done.39
  340.6 8.0 %collective-permute-done.38 = bf16[2,64,1536]{2,1,0:T(8,128)(2,1)} collective-permute-done((bf16[2,64,1536]{2,1,0:T(8,128)(2,1)}, bf16[2,64,1536]{2,1,0:T(8,128)(2,1)}, u32[]{:S(2)}, u32[]{:S(2)}) %collective-permute-start.38) | collective-permute-done | bytes 393248 | tf_op jit(solution)/shard_map/ppermute | solution.py:831
  350.2 2.5 fusion.20
  353.3 2.8 fusion.23
  357.7 2.4 bitcast_select_fusion.1.e_ref
  364.7 3.6 fusion.113
  375.6 18.3 %section_backward.6 = (f32[2,128,1536]{2,1,0:T(8,128)S(1)}, bf16[1,2,128,1536]{3,2,1,0:T(8,128)(2,1)S(1)}, bf16[512,1152]{1,0:T(8,128)(2,1)S(1)}, f32[128,768]{1...) custom-call(s32[1]{0:T(128)} %bitcast.part_ref, f32[512,768]{1,0:T(8,128)S(1)} %get-tuple-element.253.dy_ref, ...), custom_call_target="tpu_custom_call" | custom-call | flops 23592960000 | bytes 12582912 | tf_op jit(solution)/shard_map/section_backward/pallas_call | solution.py:703
  402.8 6.1 %collective-permute-done.48 = bf16[2,64,1536]{2,1,0:T(8,128)(2,1)} collective-permute-done((bf16[2,64,1536]{2,1,0:T(8,128)(2,1)S(1)}, bf16[2,64,1536]{2,1,0:T(8,128)(2,1)}, u32[]{:S(2)}, u32[]{:S(2)}) %collective-permute-start.48) | collective-permute-done | bytes 393248 | tf_op jit(solution)/shard_map/ppermute | solution.py:831
  433.0 19.4 %section_backward.7 = (f32[2,128,1536]{2,1,0:T(8,128)S(1)}, bf16[1,2,128,1536]{3,2,1,0:T(8,128)(2,1)S(1)}, bf16[512,1152]{1,0:T(8,128)(2,1)S(1)}, f32[128,768]{1...) custom-call(s32[1]{0:T(128)} %bitcast.part_ref, f32[512,768]{1,0:T(8,128)S(1)} %get-tuple-element.282.dy_ref, ...), custom_call_target="tpu_custom_call" | custom-call | flops 23592960000 | bytes 12582912 | tf_op jit(solution)/shard_map/section_backward/pallas_call | solution.py:703
  452.7 4.1 collective-permute-done.53
  460.3 2.5 fusion
  472.2 4.9 collective-permute-done.57
  477.1 5.7 %collective-permute-done.58 = bf16[192,1536]{1,0:T(8,128)(2,1)S(1)} collective-permute-done((bf16[192,1536]{1,0:T(8,128)(2,1)S(1)}, bf16[192,1536]{1,0:T(8,128)(2,1)S(1)}, u32[]{:S(2)}, u32[]{:S(2)}) %collective-permute-start.58) | collective-permute-done | bytes 589856 | tf_op jit(solution)/shard_map/ppermute | solution.py:825
  494.7 2.4 broadcast_in_dim.541
  497.1 9.3 %collective-permute-done.62 = bf16[64,1536]{1,0:T(8,128)(2,1)S(1)} collective-permute-done((bf16[64,1536]{1,0:T(8,128)(2,1)}, bf16[64,1536]{1,0:T(8,128)(2,1)S(1)}, u32[]{:S(2)}, u32[]{:S(2)}) %collective-permute-start.62) | collective-permute-done | bytes 196640 | tf_op jit(solution)/shard_map/ppermute | solution.py:825
  523.2 3.1 broadcast_in_dim.539
  526.3 2.5 broadcast_select_fusion.7
  535.3 2.7 fusion.59
  542.0 2.6 select_convert_fusion
  548.4 3.0 collective-permute-done.74
  (711 shorter events, 222.1 us)
Async XLA Ops:
  2.8 12.3 %collective-permute-start.1 = (bf16[64,1536]{1,0:T(8,128)(2,1)}, bf16[64,1536]{1,0:T(8,128)(2,1)S(1)}, u32[]{:S(2)}, u32[]{:S(2)}) collective-permute-start(bf16[64,1536]{1,0:T(8,128)(2,1)} %get-tuple-element.388), channel_id=1, source_target_pairs={{0,8},{2,10},{4,12},{6,14},{8,0},{10,2},{12,4},{14,6},{1,9},{3,11}... | collective-permute-start | bytes 589832 | tf_op jit(solution)/shard_map/ppermute | solution.py:825
  11.9 10.6 %collective-permute-start.7 = (bf16[1,192,2688]{2,1,0:T(8,128)(2,1)}, bf16[1,192,2688]{2,1,0:T(8,128)(2,1)S(1)}, u32[]{:S(2)}, u32[]{:S(2)}) collective-permute-start(bf16[1,192,2688]{2,1,0:T(8,128)(2,1)} %bitcast.39), channel_id=1, source_target_pairs={{0,2},{2,0},{4,6},{6,4},{8,10},{10,8},{12,14},{14,12},{1,3},{3,1},... | collective-permute-start | bytes 3096584 | tf_op jit(solution)/shard_map/ppermute | solution.py:825
  11.9 26.6 %collective-permute-start.5 = (bf16[1,192,2688]{2,1,0:T(8,128)(2,1)S(1)}, bf16[1,192,2688]{2,1,0:T(8,128)(2,1)S(1)}, u32[]{:S(2)}, u32[]{:S(2)}) collective-permute-start(bf16[1,192,2688]{2,1,0:T(8,128)(2,1)S(1)} %bitcast.539), channel_id=1, source_target_pairs={{0,4},{2,6},{4,0},{6,2},{8,12},{10,14},{12,8},{14,10},{1,5},{3,7},... | collective-permute-start | bytes 3096584 | tf_op jit(solution)/shard_map/ppermute | solution.py:825
  19.3 13.5 %collective-permute-start.3 = (bf16[3,64,1536]{2,1,0:T(8,128)(2,1)}, bf16[3,64,1536]{2,1,0:T(8,128)(2,1)}, u32[]{:S(2)}, u32[]{:S(2)}) collective-permute-start(bf16[3,64,1536]{2,1,0:T(8,128)(2,1)} %pad_maximum_fusion.4), channel_id=1, source_target_pairs={{0,1},{1,0},{2,3},{3,2},{4,5},{5,4},{6,7},{7,6},{8,9},{9,8},{10,11... | collective-permute-start | bytes 1769480 | tf_op jit(solution)/shard_map/ppermute | solution.py:831
  22.4 24.7 %collective-permute-start.8 = (bf16[1,192,2688]{2,1,0:T(8,128)(2,1)S(1)}, bf16[1,192,2688]{2,1,0:T(8,128)(2,1)S(1)}, u32[]{:S(2)}, u32[]{:S(2)}) collective-permute-start(bf16[1,192,2688]{2,1,0:T(8,128)(2,1)S(1)} %collective-permute-done.7.refs_3_), channel_id=1, source_target_pairs={{0,8},{2,10},{4,12},{6,14},{8,0},{10,2},{12,4},{14,6},{1,9},{3,11}... | collective-permute-start | bytes 3096584 | tf_op jit(solution)/shard_map/ppermute | solution.py:825
  36.8 14.0 %collective-permute-start.4 = (bf16[4,128,1536]{2,1,0:T(8,128)(2,1)}, bf16[4,128,1536]{2,1,0:T(8,128)(2,1)}, u32[]{:S(2)}, u32[]{:S(2)}) collective-permute-start(bf16[4,128,1536]{2,1,0:T(8,128)(2,1)} %select_select_fusion.1), channel_id=1, source_target_pairs={{0,2},{2,0},{4,6},{6,4},{8,10},{10,8},{12,14},{14,12},{1,3},{3,1},... | collective-permute-start | bytes 4718600 | tf_op jit(solution)/shard_map/ppermute | solution.py:825
  40.0 49.0 %collective-permute-start.6 = (bf16[2,192,2688]{2,1,0:T(8,128)(2,1)}, bf16[2,192,2688]{2,1,0:T(8,128)(2,1)}, u32[]{:S(2)}, u32[]{:S(2)}) collective-permute-start(bf16[2,192,2688]{2,1,0:T(8,128)(2,1)} %pad_maximum_fusion), channel_id=1, source_target_pairs={{0,8},{2,10},{4,12},{6,14},{8,0},{10,2},{12,4},{14,6},{1,9},{3,11}... | collective-permute-start | bytes 6193160 | tf_op jit(solution)/shard_map/ppermute | solution.py:825
  48.9 41.1 %collective-permute-start.9 = (bf16[2,192,2688]{2,1,0:T(8,128)(2,1)}, bf16[2,192,2688]{2,1,0:T(8,128)(2,1)}, u32[]{:S(2)}, u32[]{:S(2)}) collective-permute-start(bf16[2,192,2688]{2,1,0:T(8,128)(2,1)} %pad_maximum_fusion.1), channel_id=1, source_target_pairs={{0,4},{2,6},{4,0},{6,2},{8,12},{10,14},{12,8},{14,10},{1,5},{3,7},... | collective-permute-start | bytes 6193160 | tf_op jit(solution)/shard_map/ppermute | solution.py:825
  106.4 16.8 %collective-permute-start.11 = (f32[4,128]{1,0:T(4,128)S(1)}, f32[4,128]{1,0:T(4,128)S(1)}, u32[]{:S(2)}, u32[]{:S(2)}) collective-permute-start(f32[4,128]{1,0:T(4,128)S(1)} %fusion.100), channel_id=1, source_target_pairs={{0,1},{1,0},{2,3},{3,2},{4,5},{5,4},{6,7},{7,6},{8,9},{9,8},{10,11... | collective-permute-start | bytes 6152 | tf_op jit(solution)/shard_map/ppermute | solution.py:831
  107.6 15.6 %collective-permute-start.14 = (bf16[128,1536]{1,0:T(8,128)(2,1)S(1)}, bf16[128,1536]{1,0:T(8,128)(2,1)S(1)}, u32[]{:S(2)}, u32[]{:S(2)}) collective-permute-start(bf16[128,1536]{1,0:T(8,128)(2,1)S(1)} %get-tuple-element.384), channel_id=1, source_target_pairs={{0,12},{2,14},{4,8},{6,10},{8,4},{10,6},{12,0},{14,2},{1,13},{3,15... | collective-permute-start | bytes 1179656 | tf_op jit(solution)/shard_map/ppermute | solution.py:825
  109.5 18.4 %collective-permute-start.13 = (bf16[128,1536]{1,0:T(8,128)(2,1)S(1)}, bf16[128,1536]{1,0:T(8,128)(2,1)S(1)}, u32[]{:S(2)}, u32[]{:S(2)}) collective-permute-start(bf16[128,1536]{1,0:T(8,128)(2,1)S(1)} %get-tuple-element.385), channel_id=1, source_target_pairs={{0,8},{2,10},{4,12},{6,14},{8,0},{10,2},{12,4},{14,6},{1,9},{3,11}... | collective-permute-start | bytes 1179656 | tf_op jit(solution)/shard_map/ppermute | solution.py:825
  110.6 17.3 %collective-permute-start.12 = (bf16[128,1536]{1,0:T(8,128)(2,1)S(1)}, bf16[128,1536]{1,0:T(8,128)(2,1)S(1)}, u32[]{:S(2)}, u32[]{:S(2)}) collective-permute-start(bf16[128,1536]{1,0:T(8,128)(2,1)S(1)} %get-tuple-element.386), channel_id=1, source_target_pairs={{0,4},{2,6},{4,0},{6,2},{8,12},{10,14},{12,8},{14,10},{1,5},{3,7},... | collective-permute-start | bytes 1179656 | tf_op jit(solution)/shard_map/ppermute | solution.py:825
  131.6 12.8 %collective-permute-start.15 = (f32[2,2,64,1536]{3,2,0,1:T(8,128)}, f32[2,2,64,1536]{3,2,0,1:T(8,128)}, u32[]{:S(2)}, u32[]{:S(2)}) collective-permute-start(f32[2,2,64,1536]{3,2,0,1:T(8,128)} %copy.145), channel_id=1, source_target_pairs={{0,2},{2,0},{4,6},{6,4},{8,10},{10,8},{12,14},{14,12},{1,3},{3,1},... | collective-permute-start | bytes 4718600 | tf_op jit(solution)/shard_map/ppermute | solution.py:825
  133.3 13.5 %collective-permute-start.17 = (bf16[4,128,1536]{2,1,0:T(8,128)(2,1)}, bf16[4,128,1536]{2,1,0:T(8,128)(2,1)}, u32[]{:S(2)}, u32[]{:S(2)}) collective-permute-start(bf16[4,128,1536]{2,1,0:T(8,128)(2,1)} %select_select_fusion), channel_id=1, source_target_pairs={{0,2},{2,0},{4,6},{6,4},{8,10},{10,8},{12,14},{14,12},{1,3},{3,1},... | collective-permute-start | bytes 4718600 | tf_op jit(solution)/shard_map/ppermute | solution.py:825
  144.3 12.5 %collective-permute-start.20 = (f32[2,2,64,1536]{3,2,0,1:T(8,128)S(1)}, f32[2,2,64,1536]{3,2,0,1:T(8,128)S(1)}, u32[]{:S(2)}, u32[]{:S(2)}) collective-permute-start(f32[2,2,64,1536]{3,2,0,1:T(8,128)S(1)} %copy.150), channel_id=1, source_target_pairs={{0,2},{2,0},{4,6},{6,4},{8,10},{10,8},{12,14},{14,12},{1,3},{3,1},... | collective-permute-start | bytes 4718600 | tf_op jit(solution)/shard_map/ppermute | solution.py:825
  145.6 12.3 %collective-permute-start.16 = (f16[2,64,1536]{2,1,0:T(8,128)(2,1)S(1)}, f16[2,64,1536]{2,1,0:T(8,128)(2,1)S(1)}, u32[]{:S(2)}, u32[]{:S(2)}) collective-permute-start(f16[2,64,1536]{2,1,0:T(8,128)(2,1)S(1)} %fusion.62), channel_id=1, source_target_pairs={{0,1},{1,0},{2,3},{3,2},{4,5},{5,4},{6,7},{7,6},{8,9},{9,8},{10,11... | collective-permute-start | bytes 1179656 | tf_op jit(solution)/shard_map/ppermute | solution.py:831
  156.9 11.3 %collective-permute-start.21 = (f16[2,64,1536]{2,1,0:T(8,128)(2,1)S(1)}, f16[2,64,1536]{2,1,0:T(8,128)(2,1)S(1)}, u32[]{:S(2)}, u32[]{:S(2)}) collective-permute-start(f16[2,64,1536]{2,1,0:T(8,128)(2,1)S(1)} %fusion.61), channel_id=1, source_target_pairs={{0,1},{1,0},{2,3},{3,2},{4,5},{5,4},{6,7},{7,6},{8,9},{9,8},{10,11... | collective-permute-start | bytes 1179656 | tf_op jit(solution)/shard_map/ppermute | solution.py:831
  159.6 15.6 %collective-permute-start.22 = (bf16[2,64,1536]{2,1,0:T(8,128)(2,1)S(1)}, bf16[2,64,1536]{2,1,0:T(8,128)(2,1)S(1)}, u32[]{:S(2)}, u32[]{:S(2)}) collective-permute-start(bf16[2,64,1536]{2,1,0:T(8,128)(2,1)S(1)} %fusion.52), channel_id=1, source_target_pairs={{0,17},{1,16},{2,19},{3,18},{4,21},{5,20},{6,23},{7,22},{8,25},{9,... | collective-permute-start | bytes 1179656 | tf_op jit(solution)/shard_map/ppermute | solution.py:835
  175.2 15.3 %collective-permute-start.24 = (bf16[2,64,1536]{2,1,0:T(8,128)(2,1)S(1)}, bf16[2,64,1536]{2,1,0:T(8,128)(2,1)S(1)}, u32[]{:S(2)}, u32[]{:S(2)}) collective-permute-start(bf16[2,64,1536]{2,1,0:T(8,128)(2,1)S(1)} %bitcast_select_fusion.6), channel_id=1, source_target_pairs={{0,1},{1,0},{2,3},{3,2},{4,5},{5,4},{6,7},{7,6},{8,9},{9,8},{10,11... | collective-permute-start | bytes 1179656 | tf_op jit(solution)/shard_map/ppermute | solution.py:831
  192.9 30.0 %collective-permute-start.23 = (bf16[2,64,1536]{2,1,0:T(8,128)(2,1)}, bf16[2,64,1536]{2,1,0:T(8,128)(2,1)S(1)}, u32[]{:S(2)}, u32[]{:S(2)}) collective-permute-start(bf16[2,64,1536]{2,1,0:T(8,128)(2,1)} %fusion.57), channel_id=1, source_target_pairs={{0,17},{1,16},{2,19},{3,18},{4,21},{5,20},{6,23},{7,22},{8,25},{9,... | collective-permute-start | bytes 1179656 | tf_op jit(solution)/shard_map/ppermute | solution.py:835
  222.9 11.2 %collective-permute-start.26 = (bf16[2,64,1536]{2,1,0:T(8,128)(2,1)S(1)}, bf16[2,64,1536]{2,1,0:T(8,128)(2,1)S(1)}, u32[]{:S(2)}, u32[]{:S(2)}) collective-permute-start(bf16[2,64,1536]{2,1,0:T(8,128)(2,1)S(1)} %bitcast_select_fusion.4), channel_id=1, source_target_pairs={{0,1},{1,0},{2,3},{3,2},{4,5},{5,4},{6,7},{7,6},{8,9},{9,8},{10,11... | collective-permute-start | bytes 1179656 | tf_op jit(solution)/shard_map/ppermute | solution.py:831
  234.5 19.7 %collective-permute-start.29 = (bf16[2,2,64,1536]{3,2,0,1:T(8,128)(2,1)S(1)}, bf16[2,2,64,1536]{3,2,0,1:T(8,128)(2,1)S(1)}, u32[]{:S(2)}, u32[]{:S(2)}) collective-permute-start(bf16[2,2,64,1536]{3,2,0,1:T(8,128)(2,1)S(1)} %copy.160), channel_id=1, source_target_pairs={{0,2},{2,0},{4,6},{6,4},{8,10},{10,8},{12,14},{14,12},{1,3},{3,1},... | collective-permute-start | bytes 2359304 | tf_op jit(solution)/shard_map/ppermute | solution.py:825
  254.3 23.4 %collective-permute-start.31 = (bf16[2,64,1536]{2,1,0:T(8,128)(2,1)S(1)}, bf16[2,64,1536]{2,1,0:T(8,128)(2,1)S(1)}, u32[]{:S(2)}, u32[]{:S(2)}) collective-permute-start(bf16[2,64,1536]{2,1,0:T(8,128)(2,1)S(1)} %fusion.64), channel_id=1, source_target_pairs={{0,1},{1,0},{2,3},{3,2},{4,5},{5,4},{6,7},{7,6},{8,9},{9,8},{10,11... | collective-permute-start | bytes 1179656 | tf_op jit(solution)/shard_map/ppermute | solution.py:831
  257.8 20.0 %collective-permute-start.30 = (bf16[2,64,1536]{2,1,0:T(8,128)(2,1)S(1)}, bf16[2,64,1536]{2,1,0:T(8,128)(2,1)S(1)}, u32[]{:S(2)}, u32[]{:S(2)}) collective-permute-start(bf16[2,64,1536]{2,1,0:T(8,128)(2,1)S(1)} %fusion.63), channel_id=1, source_target_pairs={{0,1},{1,0},{2,3},{3,2},{4,5},{5,4},{6,7},{7,6},{8,9},{9,8},{10,11... | collective-permute-start | bytes 1179656 | tf_op jit(solution)/shard_map/ppermute | solution.py:831
  284.6 11.7 %collective-permute-start.35 = (bf16[2,64,1536]{2,1,0:T(8,128)(2,1)}, bf16[2,64,1536]{2,1,0:T(8,128)(2,1)}, u32[]{:S(2)}, u32[]{:S(2)}) collective-permute-start(bf16[2,64,1536]{2,1,0:T(8,128)(2,1)} %fusion.65), channel_id=1, source_target_pairs={{0,1},{1,0},{2,3},{3,2},{4,5},{5,4},{6,7},{7,6},{8,9},{9,8},{10,11... | collective-permute-start | bytes 1179656 | tf_op jit(solution)/shard_map/ppermute | solution.py:831
  303.1 22.3 %collective-permute-start.36 = (bf16[2,64,1536]{2,1,0:T(8,128)(2,1)S(1)}, bf16[2,64,1536]{2,1,0:T(8,128)(2,1)S(1)}, u32[]{:S(2)}, u32[]{:S(2)}) collective-permute-start(bf16[2,64,1536]{2,1,0:T(8,128)(2,1)S(1)} %fusion.12), channel_id=1, source_target_pairs={{16,0},{17,1},{18,2},{19,3},{20,4},{21,5},{22,6},{23,7},{24,8},{25... | collective-permute-start | bytes 1179656 | tf_op jit(solution)/shard_map/ppermute | solution.py:835
  328.4 12.2 %collective-permute-start.39 = (bf16[2,64,1536]{2,1,0:T(8,128)(2,1)}, bf16[2,64,1536]{2,1,0:T(8,128)(2,1)}, u32[]{:S(2)}, u32[]{:S(2)}) collective-permute-start(bf16[2,64,1536]{2,1,0:T(8,128)(2,1)} %bitcast_select_fusion.7), channel_id=1, source_target_pairs={{0,1},{1,0},{2,3},{3,2},{4,5},{5,4},{6,7},{7,6},{8,9},{9,8},{10,11... | collective-permute-start | bytes 1179656 | tf_op jit(solution)/shard_map/ppermute | solution.py:831
  330.9 17.8 %collective-permute-start.38 = (bf16[2,64,1536]{2,1,0:T(8,128)(2,1)}, bf16[2,64,1536]{2,1,0:T(8,128)(2,1)}, u32[]{:S(2)}, u32[]{:S(2)}) collective-permute-start(bf16[2,64,1536]{2,1,0:T(8,128)(2,1)} %fusion.66), channel_id=1, source_target_pairs={{0,1},{1,0},{2,3},{3,2},{4,5},{5,4},{6,7},{7,6},{8,9},{9,8},{10,11... | collective-permute-start | bytes 1179656 | tf_op jit(solution)/shard_map/ppermute | solution.py:831
  356.2 41.6 %collective-permute-start.47 = (bf16[2,64,1536]{2,1,0:T(8,128)(2,1)S(1)}, bf16[2,64,1536]{2,1,0:T(8,128)(2,1)S(1)}, u32[]{:S(2)}, u32[]{:S(2)}) collective-permute-start(bf16[2,64,1536]{2,1,0:T(8,128)(2,1)S(1)} %get-tuple-element.263), channel_id=1, source_target_pairs={{16,0},{17,1},{18,2},{19,3},{20,4},{21,5},{22,6},{23,7},{24,8},{25... | collective-permute-start | bytes 1179656 | tf_op jit(solution)/shard_map/ppermute | solution.py:835
  368.3 29.4 %collective-permute-start.43 = (bf16[64,1536]{1,0:T(8,128)(2,1)S(1)}, bf16[64,1536]{1,0:T(8,128)(2,1)S(1)}, u32[]{:S(2)}, u32[]{:S(2)}) collective-permute-start(bf16[64,1536]{1,0:T(8,128)(2,1)S(1)} %get-tuple-element.248), channel_id=1, source_target_pairs={{0,4},{2,6},{4,0},{6,2},{8,12},{10,14},{12,8},{14,10},{1,5},{3,7},... | collective-permute-start | bytes 589832 | tf_op jit(solution)/shard_map/ppermute | solution.py:825
  369.8 27.9 %collective-permute-start.44 = (bf16[64,1536]{1,0:T(8,128)(2,1)S(1)}, bf16[64,1536]{1,0:T(8,128)(2,1)S(1)}, u32[]{:S(2)}, u32[]{:S(2)}) collective-permute-start(bf16[64,1536]{1,0:T(8,128)(2,1)S(1)} %get-tuple-element.249), channel_id=1, source_target_pairs={{0,8},{2,10},{4,12},{6,14},{8,0},{10,2},{12,4},{14,6},{1,9},{3,11}... | collective-permute-start | bytes 589832 | tf_op jit(solution)/shard_map/ppermute | solution.py:825
  370.5 27.2 %collective-permute-start.45 = (bf16[64,1536]{1,0:T(8,128)(2,1)S(1)}, bf16[64,1536]{1,0:T(8,128)(2,1)S(1)}, u32[]{:S(2)}, u32[]{:S(2)}) collective-permute-start(bf16[64,1536]{1,0:T(8,128)(2,1)S(1)} %get-tuple-element.250), channel_id=1, source_target_pairs={{0,12},{2,14},{4,8},{6,10},{8,4},{10,6},{12,0},{14,2},{1,13},{3,15... | collective-permute-start | bytes 589832 | tf_op jit(solution)/shard_map/ppermute | solution.py:825
  422.6 30.0 %collective-permute-start.52 = (bf16[2,64,1536]{2,1,0:T(8,128)(2,1)}, bf16[2,64,1536]{2,1,0:T(8,128)(2,1)S(1)}, u32[]{:S(2)}, u32[]{:S(2)}) collective-permute-start(bf16[2,64,1536]{2,1,0:T(8,128)(2,1)} %fusion.67), channel_id=1, source_target_pairs={{0,1},{1,0},{2,3},{3,2},{4,5},{5,4},{6,7},{7,6},{8,9},{9,8},{10,11... | collective-permute-start | bytes 1179656 | tf_op jit(solution)/shard_map/ppermute | solution.py:831
  424.1 28.6 %collective-permute-start.55 = (bf16[4,64,1536]{2,1,0:T(8,128)(2,1)S(1)}, bf16[4,64,1536]{2,1,0:T(8,128)(2,1)S(1)}, u32[]{:S(2)}, u32[]{:S(2)}) collective-permute-start(bf16[4,64,1536]{2,1,0:T(8,128)(2,1)S(1)} %select_select_fusion.3), channel_id=1, source_target_pairs={{0,1},{1,0},{2,3},{3,2},{4,5},{5,4},{6,7},{7,6},{8,9},{9,8},{10,11... | collective-permute-start | bytes 2359304 | tf_op jit(solution)/shard_map/ppermute | solution.py:831
  429.5 27.3 %collective-permute-start.53 = (bf16[2,192,1536]{2,1,0:T(8,128)(2,1)S(1)}, bf16[2,192,1536]{2,1,0:T(8,128)(2,1)S(1)}, u32[]{:S(2)}, u32[]{:S(2)}) collective-permute-start(bf16[2,192,1536]{2,1,0:T(8,128)(2,1)S(1)} %pad_maximum_fusion.2), channel_id=1, source_target_pairs={{0,4},{2,6},{4,0},{6,2},{8,12},{10,14},{12,8},{14,10},{1,5},{3,7},... | collective-permute-start | bytes 3538952 | tf_op jit(solution)/shard_map/ppermute | solution.py:825
  431.1 27.0 %collective-permute-start.54 = (bf16[2,192,1536]{2,1,0:T(8,128)(2,1)S(1)}, bf16[2,192,1536]{2,1,0:T(8,128)(2,1)S(1)}, u32[]{:S(2)}, u32[]{:S(2)}) collective-permute-start(bf16[2,192,1536]{2,1,0:T(8,128)(2,1)S(1)} %pad_maximum_fusion.3), channel_id=1, source_target_pairs={{0,8},{2,10},{4,12},{6,14},{8,0},{10,2},{12,4},{14,6},{1,9},{3,11}... | collective-permute-start | bytes 3538952 | tf_op jit(solution)/shard_map/ppermute | solution.py:825
  452.6 13.7 %collective-permute-start.56 = (bf16[2,2,64,1536]{3,2,1,0:T(8,128)(2,1)S(1)}, bf16[2,2,64,1536]{3,2,1,0:T(8,128)(2,1)S(1)}, u32[]{:S(2)}, u32[]{:S(2)}) collective-permute-start(bf16[2,2,64,1536]{3,2,1,0:T(8,128)(2,1)S(1)} %bitcast.625), channel_id=1, source_target_pairs={{0,2},{2,0},{4,6},{6,4},{8,10},{10,8},{12,14},{14,12},{1,3},{3,1},... | collective-permute-start | bytes 2359304 | tf_op jit(solution)/shard_map/ppermute | solution.py:825
  466.4 16.3 %collective-permute-start.58 = (bf16[192,1536]{1,0:T(8,128)(2,1)S(1)}, bf16[192,1536]{1,0:T(8,128)(2,1)S(1)}, u32[]{:S(2)}, u32[]{:S(2)}) collective-permute-start(bf16[192,1536]{1,0:T(8,128)(2,1)S(1)} %fusion.4), channel_id=1, source_target_pairs={{0,8},{2,10},{4,12},{6,14},{8,0},{10,2},{12,4},{14,6},{1,9},{3,11}... | collective-permute-start | bytes 1769480 | tf_op jit(solution)/shard_map/ppermute | solution.py:825
  467.2 16.3 %collective-permute-start.59 = (bf16[192,1536]{1,0:T(8,128)(2,1)S(1)}, bf16[192,1536]{1,0:T(8,128)(2,1)S(1)}, u32[]{:S(2)}, u32[]{:S(2)}) collective-permute-start(bf16[192,1536]{1,0:T(8,128)(2,1)S(1)} %fusion.3), channel_id=1, source_target_pairs={{0,4},{2,6},{4,0},{6,2},{8,12},{10,14},{12,8},{14,10},{1,5},{3,7},... | collective-permute-start | bytes 1769480 | tf_op jit(solution)/shard_map/ppermute | solution.py:825
  469.3 38.5 %collective-permute-start.63 = (bf16[2,192,1152]{2,1,0:T(8,128)(2,1)}, bf16[2,192,1152]{2,1,0:T(8,128)(2,1)}, u32[]{:S(2)}, u32[]{:S(2)}) collective-permute-start(bf16[2,192,1152]{2,1,0:T(8,128)(2,1)} %dynamic-slice_bitcast_fusion.1), channel_id=1, source_target_pairs={{0,4},{2,6},{4,0},{6,2},{8,12},{10,14},{12,8},{14,10},{1,5},{3,7},... | collective-permute-start | bytes 2654216 | tf_op jit(solution)/shard_map/ppermute | solution.py:825
  470.2 37.7 %collective-permute-start.64 = (bf16[2,192,1152]{2,1,0:T(8,128)(2,1)}, bf16[2,192,1152]{2,1,0:T(8,128)(2,1)}, u32[]{:S(2)}, u32[]{:S(2)}) collective-permute-start(bf16[2,192,1152]{2,1,0:T(8,128)(2,1)} %dynamic-slice_bitcast_fusion), channel_id=1, source_target_pairs={{0,8},{2,10},{4,12},{6,14},{8,0},{10,2},{12,4},{14,6},{1,9},{3,11}... | collective-permute-start | bytes 2654216 | tf_op jit(solution)/shard_map/ppermute | solution.py:825
  487.4 19.0 %collective-permute-start.62 = (bf16[64,1536]{1,0:T(8,128)(2,1)}, bf16[64,1536]{1,0:T(8,128)(2,1)S(1)}, u32[]{:S(2)}, u32[]{:S(2)}) collective-permute-start(bf16[64,1536]{1,0:T(8,128)(2,1)} %get-tuple-element.403), channel_id=1, source_target_pairs={{0,12},{2,14},{4,8},{6,10},{8,4},{10,6},{12,0},{14,2},{1,13},{3,15... | collective-permute-start | bytes 589832 | tf_op jit(solution)/shard_map/ppermute | solution.py:825
  488.7 19.1 %collective-permute-start.60 = (bf16[64,1536]{1,0:T(8,128)(2,1)}, bf16[64,1536]{1,0:T(8,128)(2,1)}, u32[]{:S(2)}, u32[]{:S(2)}) collective-permute-start(bf16[64,1536]{1,0:T(8,128)(2,1)} %get-tuple-element.404), channel_id=1, source_target_pairs={{0,4},{2,6},{4,0},{6,2},{8,12},{10,14},{12,8},{14,10},{1,5},{3,7},... | collective-permute-start | bytes 589832 | tf_op jit(solution)/shard_map/ppermute | solution.py:825
  490.2 17.6 %collective-permute-start.61 = (bf16[64,1536]{1,0:T(8,128)(2,1)}, bf16[64,1536]{1,0:T(8,128)(2,1)}, u32[]{:S(2)}, u32[]{:S(2)}) collective-permute-start(bf16[64,1536]{1,0:T(8,128)(2,1)} %get-tuple-element.405), channel_id=1, source_target_pairs={{0,8},{2,10},{4,12},{6,14},{8,0},{10,2},{12,4},{14,6},{1,9},{3,11}... | collective-permute-start | bytes 589832 | tf_op jit(solution)/shard_map/ppermute | solution.py:825
  506.4 14.3 %collective-permute-start.70 = (bf16[192,1536]{1,0:T(8,128)(2,1)}, bf16[192,1536]{1,0:T(8,128)(2,1)S(1)}, u32[]{:S(2)}, u32[]{:S(2)}) collective-permute-start(bf16[192,1536]{1,0:T(8,128)(2,1)} %get-tuple-element.373), channel_id=1, source_target_pairs={{0,2},{2,0},{4,6},{6,4},{8,10},{10,8},{12,14},{14,12},{1,3},{3,1},... | collective-permute-start | bytes 1769480 | tf_op jit(solution)/shard_map/ppermute | solution.py:825
  510.0 28.1 %collective-permute-start.65 = (bf16[4,64,1536]{2,1,0:T(8,128)(2,1)}, bf16[4,64,1536]{2,1,0:T(8,128)(2,1)}, u32[]{:S(2)}, u32[]{:S(2)}) collective-permute-start(bf16[4,64,1536]{2,1,0:T(8,128)(2,1)} %select_select_fusion.2), channel_id=1, source_target_pairs={{0,1},{1,0},{2,3},{3,2},{4,5},{5,4},{6,7},{7,6},{8,9},{9,8},{10,11... | collective-permute-start | bytes 2359304 | tf_op jit(solution)/shard_map/ppermute | solution.py:831
  518.4 16.9 %collective-permute-start.72 = (bf16[192,1152]{1,0:T(8,128)(2,1)}, bf16[192,1152]{1,0:T(8,128)(2,1)}, u32[]{:S(2)}, u32[]{:S(2)}) collective-permute-start(bf16[192,1152]{1,0:T(8,128)(2,1)} %fusion.5), channel_id=1, source_target_pairs={{0,8},{2,10},{4,12},{6,14},{8,0},{10,2},{12,4},{14,6},{1,9},{3,11}... | collective-permute-start | bytes 1327112 | tf_op jit(solution)/shard_map/ppermute | solution.py:825
  519.0 16.2 %collective-permute-start.71 = (bf16[192,1152]{1,0:T(8,128)(2,1)}, bf16[192,1152]{1,0:T(8,128)(2,1)}, u32[]{:S(2)}, u32[]{:S(2)}) collective-permute-start(bf16[192,1152]{1,0:T(8,128)(2,1)} %fusion.7), channel_id=1, source_target_pairs={{0,4},{2,6},{4,0},{6,2},{8,12},{10,14},{12,8},{14,10},{1,5},{3,7},... | collective-permute-start | bytes 1327112 | tf_op jit(solution)/shard_map/ppermute | solution.py:825
  (227 other events, 1764.3 us)

commit v2 on v1

--- a/solution.py
+++ b/solution.py
@@ -151,9 +151,9 @@
     lax.fori_loop(0, count, one, 0)
 
 
-def forward_kernel(keep, width, parts, per_step, part_ref, h_ref, w1_ref, wg_ref, wo_ref, norm_ref, taps_ref, heads_ref, inner_ref, s0_ref, tail0_ref, *rest):
+def forward_kernel(keep, width, parts, per_step, part_ref, h_ref, w1_ref, wg_ref, norm_ref, taps_ref, heads_ref, inner_ref, s0_ref, tail0_ref, *rest):
     if keep:
-        dn_ref, own_ref, send_ref, sums_ref, st_ref, tail_ref, xn_ref, vbd_ref, z_ref, y_ref, sin_ref, pad, gg, total = rest
+        wo_ref, dn_ref, own_ref, send_ref, sums_ref, st_ref, tail_ref, xn_ref, vbd_ref, z_ref, y_ref, sin_ref, pad, gg, total = rest
     else:
         g_ref, sums_ref, st_ref, tail_ref, xn_ref, vbd_ref, z_ref, pad = rest
     mixed = width + MAPS
@@ -301,7 +301,7 @@
 
 
 def forward_call(place, h, weights, small, s0, tail0, dn=None):
-    w1, wg, wo = weights
+    w1, wg = weights[:2]
     norm_gain, taps, heads, inner = small
     keep = dn is not None
     tokens, depth = h.shape
@@ -334,7 +334,6 @@
         rows(depth),
         once(w1.shape),
         once(wg.shape),
-        once(wo.shape),
         once((1, depth)),
         once(taps.shape),
         once(heads.shape),
@@ -342,12 +341,12 @@
         once(s0.shape),
         once(tail0.shape),
     ]
-    args = [h, w1, wg, wo, norm_gain[None], taps, heads, inner, s0, tail0]
+    args = [h, w1, wg, norm_gain[None], taps, heads, inner, s0, tail0]
     held = [((tokens, depth), bf16), ((tokens, w1.shape[1]), f32), ((tokens, width), f32)]
     scratch = []
     if keep:
-        in_specs.append(rows(width))
-        args.append(dn)
+        in_specs += [once(weights[2].shape), rows(width)]
+        args += [weights[2], dn]
         held.append(((tokens, width), f32))
         out_shape += [jax.ShapeDtypeStruct(*item) for item in held]
         out_specs += [rows(shape[1]) for shape, _ in held]
@@ -861,10 +860,38 @@
     return masks
 
 
-def order(blocks, index, axis):
+def order_kernel(count, axis, index_ref, *refs):
+    blocks, out, sems = refs[:count], refs[count], refs[count + 1]
+    copies = []
+    for d, one in enumerate(blocks):
+        there = (slice(None),) * axis + (index_ref[0] ^ d,)
+        copies.append(pltpu.make_async_copy(one, out.at[there], sems.at[d]))
+    for one in copies:
+        one.start()
+    for one in copies:
+        one.wait()
+
+
+def order(blocks, index, axis, copies=True):
     count = len(blocks)
     shape = list(blocks[0].shape)
     shape.insert(axis, count)
+    if count == 1:
+        return blocks[0].reshape(shape)
+    if copies and axis <= blocks[0].ndim - 2 and shape[-2] % 16 == 0 and shape[-1] >= LANES:
+        return pl.pallas_call(
+            functools.partial(order_kernel, count, axis),
+            grid_spec=pltpu.PrefetchScalarGridSpec(
+                num_scalar_prefetch=1,
+                grid=(1,),
+                in_specs=[pl.BlockSpec(memory_space=pl.ANY)] * count,
+                out_specs=pl.BlockSpec(memory_space=pltpu.VMEM),
+                scratch_shapes=[pltpu.SemaphoreType.DMA((count,))],
+            ),
+            out_shape=jax.ShapeDtypeStruct(tuple(shape), blocks[0].dtype),
+            compiler_params=pltpu.CompilerParams(vmem_limit_bytes=4 * 1024 * 1024),
+            name="order_blocks",
+        )(index.reshape(1).astype(jnp.int32), *blocks)
     place = lax.broadcasted_iota(jnp.int32, shape, axis) ^ index
     result = jnp.expand_dims(blocks[0], axis)
     for d in range(1, count):
@@ -943,35 +970,59 @@
     return [result.reshape(count * rows, -1) for result in results]
 
 
+class Collect:
+    def __init__(self, place, blocks):
+        self.place = place
+        self.found = [[block] for block in blocks]
+        self.distances = [[0] for _ in blocks]
+        self.masks = [bits_of(place.micros)[:: -1 if p % 2 else 1] for p in range(len(blocks))]
+
+    def prepare(self):
+        self.out = [found[0] if len(found) == 1 else jnp.concatenate(found, axis=0) for found in self.found]
+
+    def launch(self):
+        self.next = [self.place.swap_micro(block, masks[0]) for block, masks in zip(self.out, self.masks)]
+
+    def land(self):
+        for p, block in enumerate(self.next):
+            mask = self.masks[p].pop(0)
+            self.found[p].append(block)
+            self.distances[p] += [distance ^ mask for distance in self.distances[p]]
+
+    def finish(self):
+        while self.masks[0]:
+            self.prepare()
+            self.launch()
+            self.land()
+
+    def result(self, widths):
+        place, pieces, places = self.place, [], []
+        for p, found in enumerate(self.found):
+            pieces += found
+            places += [(place.micro ^ distance) * place.parts + (place.part ^ p) for distance in self.distances[p]]
+        return lay_rows(pieces, places, widths)
+
+
 def gather_weights(place, w_gate, w_value, w_bc, w_dt, w_out):
     parts = place.parts
-    columns = w_gate.shape[1]
-    width = columns // parts
+    width = w_gate.shape[1] // parts
     heads = w_dt.shape[1] // parts
-    out_t = w_out.T
+
+    def cut_of(array, part):
+        return lax.dynamic_slice_in_dim(array, part * width, width, 1)
 
     def columns_of(part):
         steps = lax.dynamic_slice_in_dim(w_dt, part * heads, heads, 1)
         steps = jnp.pad(steps, ((0, 0), (0, LANES - heads)))
-        cuts = [lax.dynamic_slice_in_dim(array, part * width, width, 1) for array in (w_value, w_gate, out_t)]
-        return jnp.concatenate([cuts[0], w_bc, steps, cuts[1], cuts[2]], axis=1)[None]
-
-    pieces, places = [], []
-    for p in range(parts):
-        block = columns_of(place.part ^ p)
-        if p:
-            block = place.swap_part(block, p)
-        masks = bits_of(place.micros)
-        if p % 2:
-            masks = masks[::-1]
-        found, distances = [block], [0]
-        for mask in masks:
-            whole = found[0] if len(found) == 1 else jnp.concatenate(found, axis=0)
-            found.append(place.swap_micro(whole, mask))
-            distances += [distance ^ mask for distance in distances]
-        pieces += found
-        places += [(place.micro ^ distance) * parts + (place.part ^ p) for distance in distances]
-    return lay_rows(pieces, places, [width + MAPS + LANES, width, width])
+        return jnp.concatenate([cut_of(w_value, part), w_bc, steps, cut_of(w_gate, part)], axis=1)[None]
+
+    def collected(make):
+        blocks = [make(place.part ^ p) for p in range(parts)]
+        return Collect(place, blocks[:1] + [place.swap_part(block, p + 1) for p, block in enumerate(blocks[1:])])
+
+    first = collected(columns_of)
+    second = collected(lambda part: cut_of(w_out.T, part)[None])
+    return first, second
 
 
 def whole_tokens(place, rows):
@@ -981,29 +1032,30 @@
 
 
 def lay_tokens(place, blocks):
-    held = order(blocks, place.micro, 0)
-    whole = order([held] + [place.swap_part(held, d) for d in range(1, place.parts)], place.part, 1)
+    held = order(blocks, place.micro, 0, False)
+    whole = order([held] + [place.swap_part(held, d) for d in range(1, place.parts)], place.part, 1, False)
     size = place.micros // PIECES
     return [whole[i * size : (i + 1) * size].reshape(-1, held.shape[-1]) for i in range(PIECES)]
 
 
-def spread_tokens(place, rows):
-    micros, count, width = rows.shape
-    view = rows.reshape(micros, place.tensors, count // place.tensors, width)
-    got = [
-        place.swap_micro(pick(pick(view, place.micro ^ d, 0), place.tensor, 0), d) for d in range(1, micros)
-    ]
-    shares = jnp.stack(got)
-    both = [shares] + [place.swap_tensor(shares, d) for d in range(1, place.tensors)]
-    own = pick(rows, place.micro, 0)
-    return lay_tokens(
-        place,
-        [own]
-        + [
-            order([part[d] for part in both], place.tensor, 0).reshape(count, width)
-            for d in range(micros - 1)
-        ],
-    )
+class Spread:
+    def __init__(self, place, rows):
+        self.place, self.rows = place, rows
+        micros, count, width = rows.shape
+        view = rows.reshape(micros, place.tensors, count // place.tensors, width)
+        self.shares = jnp.stack(
+            [place.swap_micro(pick(pick(view, place.micro ^ d, 0), place.tensor, 0), d) for d in range(1, micros)]
+        )
+        self.came = [place.swap_tensor(self.shares, d) for d in range(1, place.tensors)]
+
+    def result(self):
+        place = self.place
+        both = [self.shares] + self.came
+        blocks = [pick(self.rows, place.micro, 0)]
+        for d in range(place.micros - 1):
+            whole = order([part[d] for part in both], place.tensor, 0, False)
+            blocks.append(whole.reshape(-1, self.rows.shape[2]))
+        return lay_tokens(place, blocks)
 
 
 def blocks_of(place, array):
@@ -1014,27 +1066,210 @@
     return pick(pick(blocks_of(place, array), place.part, 1), place.tensor ^ flip, 1)
 
 
+GROUP = 16
+
+
+def split_kernel(parts, tensors, tensor_ref, own_ref, *refs):
+    came, going_ref, kept_ref = refs[: parts - 1], refs[-2], refs[-1]
+    rows = kept_ref.shape[1]
+
+    def group(i, _):
+        here = pl.ds(pl.multiple_of(i * GROUP, GROUP), GROUP)
+        for d in range(tensors):
+            start = (tensor_ref[0] ^ d) * rows + i * GROUP
+            there = pl.ds(pl.multiple_of(start, GROUP), GROUP)
+            total = own_ref[0, there, :]
+            for one in came:
+                total = total + one[0, there, :].astype(f32)
+            if d:
+                going_ref[d - 1, 0, here, :] = total.astype(bf16)
+            else:
+                kept_ref[0, here, :] = total
+        return 0
+
+    lax.fori_loop(0, rows // GROUP, group, 0)
+
+
+def split_call(place, own, came):
+    blocks, tokens, depth = own.shape
+    rows = tokens // place.tensors
+    others = place.tensors - 1
+    return pl.pallas_call(
+        functools.partial(split_kernel, place.parts, place.tensors),
+        grid_spec=pltpu.PrefetchScalarGridSpec(
+            num_scalar_prefetch=1,
+            grid=(blocks,),
+            in_specs=[pl.BlockSpec((1, tokens, depth), lambda b, _: (b, 0, 0))] * place.parts,
+            out_specs=[
+                pl.BlockSpec((others, 1, rows, depth), lambda b, _: (0, b, 0, 0)),
+                pl.BlockSpec((1, rows, depth), lambda b, _: (b, 0, 0)),
+            ],
+        ),
+        out_shape=[
+            jax.ShapeDtypeStruct((others, blocks, rows, depth), bf16),
+            jax.ShapeDtypeStruct((blocks, rows, depth), f32),
+        ],
+        compiler_params=pltpu.CompilerParams(vmem_limit_bytes=8 * 1024 * 1024),
+        name="split_terms",
+    )(place.tensor.reshape(1), own, *came)
+
+
+def finish_kernel(places_ref, kept_ref, h_ref, e_ref, norm_ref, *refs):
+    sent, grad_ref, sum_ref = refs[:-2], refs[-2], refs[-1]
+    rows = kept_ref.shape[1]
+
+    @pl.when(pl.program_id(0) == 0)
+    def _():
+        sum_ref[...] = jnp.zeros_like(sum_ref)
+
+    def group(i, _):
+        here = pl.ds(pl.multiple_of(i * GROUP, GROUP), GROUP)
+        dxn = kept_ref[0, here, :]
+        for one in sent:
+            dxn = dxn + one[0, here, :].astype(f32)
+        h = h_ref[0, 0, 0, here, :].astype(f32)
+        r = lax.rsqrt(jnp.mean(h * h, axis=1, keepdims=True) + epsilon)
+        scaled = dxn * norm_ref[...]
+        pull = r * r * r * jnp.mean(scaled * h, axis=1, keepdims=True)
+        grad_ref[0, here, :] = (e_ref[0, 0, 0, here, :].astype(f32) + r * scaled - h * pull).astype(bf16)
+        found = dxn * h * r
+        sum_ref[...] += found[0:8] + found[8:16]
+        return 0
+
+    lax.fori_loop(0, rows // GROUP, group, 0)
+
+
+def finish_call(place, kept, sent, h, e, norm_gain):
+    blocks, rows, depth = kept.shape
+    share = pl.BlockSpec((1, rows, depth), lambda b, _: (b, 0, 0))
+    whole = pl.BlockSpec((1, 1, 1, rows, depth), lambda b, places: (b, places[0], places[1], 0, 0))
+    return pl.pallas_call(
+        finish_kernel,
+        grid_spec=pltpu.PrefetchScalarGridSpec(
+            num_scalar_prefetch=1,
+            grid=(blocks,),
+            in_specs=[share, whole, whole, pl.BlockSpec((1, depth), lambda b, _: (0, 0))] + [share] * len(sent),
+            out_specs=[share, pl.BlockSpec((8, depth), lambda b, _: (0, 0))],
+        ),
+        out_shape=[jax.ShapeDtypeStruct(kept.shape, bf16), jax.ShapeDtypeStruct((8, depth), f32)],
+        compiler_params=pltpu.CompilerParams(vmem_limit_bytes=8 * 1024 * 1024),
+        name="finish_gradient",
+    )(jnp.stack([place.part, place.tensor]), kept, blocks_of(place, h), blocks_of(place, e), norm_gain[None], *sent)
+
+
+def deal_kernel(parts, widths, rounds, part_ref, *refs):
+    mine_ref, send_ref = refs[-2], refs[-1]
+    each = len(widths) + rounds
+    rows = mine_ref.shape[0]
+
+    def group(i, _):
+        here = pl.ds(pl.multiple_of(i * GROUP, GROUP), GROUP)
+        for p in range(parts):
+            arrays = refs[p * each : (p + 1) * each]
+            total = jnp.concatenate([one[here, :].astype(f32) for one in arrays[: len(widths)]], axis=1)
+            for one in arrays[len(widths) :]:
+                total = total + one[here, :].astype(f32)
+            distance = part_ref[0] ^ p
+
+            @pl.when(distance == 0)
+            def _():
+                mine_ref[here, :] = total
+
+            @pl.when(distance != 0)
+            def _():
+                send_ref[jnp.maximum(distance - 1, 0), here, :] = total.astype(bf16)
+
+        return 0
+
+    lax.fori_loop(0, rows // GROUP, group, 0)
+
+
+def deal_call(place, groups, came):
+    widths = [block.shape[-1] for block in groups[0]]
+    rows, total = groups[0][0].shape[0], sum(widths)
+    args = [one for held, round_ in zip(groups, came) for one in list(held) + list(round_)]
+    others = place.parts - 1
+    step = 3 * GROUP
+    return pl.pallas_call(
+        functools.partial(deal_kernel, place.parts, widths, len(came[0])),
+        grid_spec=pltpu.PrefetchScalarGridSpec(
+            num_scalar_prefetch=1,
+            grid=(rows // step,),
+            in_specs=[pl.BlockSpec((step, one.shape[1]), lambda i, _: (i, 0)) for one in args],
+            out_specs=[
+                pl.BlockSpec((step, total), lambda i, _: (i, 0)),
+                pl.BlockSpec((others, step, total), lambda i, _: (0, i, 0)),
+            ],
+        ),
+        out_shape=[jax.ShapeDtypeStruct((rows, total), f32), jax.ShapeDtypeStruct((others, rows, total), bf16)],
+        compiler_params=pltpu.CompilerParams(vmem_limit_bytes=8 * 1024 * 1024),
+        name="deal_rows",
+    )(place.part.reshape(1), *args)
+
+
+def beside_kernel(parts, at, part_ref, *refs):
+    blocks, out_ref = refs[:parts], refs[-1]
+    rows, width = out_ref.shape[0], out_ref.shape[1] // parts
+
+    def group(i, _):
+        here = pl.ds(pl.multiple_of(i * GROUP, GROUP), GROUP)
+        for d, one in enumerate(blocks):
+            there = pl.ds(pl.multiple_of((part_ref[0] ^ d) * width, LANES), width)
+            out_ref[here, there] = one[here, at : at + width].astype(f32)
+        return 0
+
+    lax.fori_loop(0, rows // GROUP, group, 0)
+
+
+def columns_beside(place, blocks, at, width):
+    if width % LANES or at % LANES:
+        return beside([block[:, at : at + width].astype(f32) for block in blocks], place.part)
+    shape = (blocks[0].shape[0], place.parts * width)
+    step = 3 * GROUP
+    return pl.pallas_call(
+        functools.partial(beside_kernel, place.parts, at),
+        grid_spec=pltpu.PrefetchScalarGridSpec(
+            num_scalar_prefetch=1,
+            grid=(shape[0] // step,),
+            in_specs=[pl.BlockSpec((step, block.shape[1]), lambda i, _: (i, 0)) for block in blocks],
+            out_specs=pl.BlockSpec((step, shape[1]), lambda i, _: (i, 0)),
+        ),
+        out_shape=jax.ShapeDtypeStruct(shape, f32),
+        compiler_params=pltpu.CompilerParams(vmem_limit_bytes=8 * 1024 * 1024),
+        name="columns_beside",
+    )(place.part.reshape(1), *blocks)
+
+
 def cut(place, block):
     return block.reshape(block.shape[:-2] + (place.tensors, -1, block.shape[-1]))
 
 
 class Reduction:
     def __init__(self, place, own, send, kind=bf16):
-        self.place, self.kind = place, kind
+        self.place, self.kind, self.going = place, kind, None
         sends = [send.reshape(own.shape)] if place.parts == 2 else [send[d] for d in range(place.parts - 1)]
-        self.came = [place.swap_part(cut(place, block), d + 1) for d, block in enumerate(sends)]
-        self.own = cut(place, own)
+        self.came = [place.swap_part(block, d + 1) for d, block in enumerate(sends)]
+        self.own = own
+
+    def prepare(self):
+        place = self.place
+        if self.kind == bf16:
+            going, self.kept = split_call(place, self.own, self.came)
+            self.going = [going.reshape(self.kept.shape)] if place.tensors == 2 else list(going)
+        else:
+            own, came = cut(place, self.own), [cut(place, block) for block in self.came]
+
+            def side(tensor):
+                return pick(own, tensor, 1) + sum(pick(block, tensor, 1).astype(f32) for block in came)
+
+            self.going = [side(place.tensor ^ d).astype(self.kind) for d in range(1, place.tensors)]
+            self.kept = side(place.tensor)
 
     def launch(self, others=None):
-        place = self.place
-
-        def side(tensor):
-            return pick(self.own, tensor, 1) + sum(pick(block, tensor, 1).astype(f32) for block in self.came)
-
-        going = [side(place.tensor ^ d).astype(self.kind) for d in range(1, place.tensors)]
-        going, others = tie(going, others)
-        self.kept = side(place.tensor)
-        self.sent = [place.swap_tensor(block, d + 1) for d, block in enumerate(going)]
+        if self.going is None:
+            self.prepare()
+        self.going, others = tie(self.going, others)
+        self.sent = [self.place.swap_tensor(block, d + 1) for d, block in enumerate(self.going)]
         return others
 
     def land(self, others):
@@ -1072,15 +1307,21 @@
 class Homing:
     def __init__(self, place, own):
         self.place = place
+        self.rows = None
         self.own = pick(own, place.micro, 0)
         self.sends = [pick(own, place.micro ^ d, 0) for d in range(1, place.micros)]
 
     def launch(self):
         self.came = [self.place.swap_micro(block, d + 1) for d, block in enumerate(self.sends)]
 
+    def collect(self):
+        self.rows = order([self.own] + self.came, self.place.micro, 0)
+
     def turn(self, others=None):
         place = self.place
-        self.rows, others = tie(order([self.own] + self.came, place.micro, 0), others)
+        if self.rows is None:
+            self.collect()
+        self.rows, others = tie(self.rows, others)
         self.swapped = [place.swap_tensor(self.rows, d) for d in range(1, place.tensors)]
         return others
 
@@ -1140,13 +1381,8 @@
     return (own, send), (adjoint, du), dvbd, sums
 
 
-def input_grad(place, e, h, norm_gain, dxn):
-    ho = own_share(place, h).astype(f32)
-    eo = own_share(place, e).astype(f32)
-    r = lax.rsqrt(jnp.mean(ho * ho, axis=2, keepdims=True) + epsilon)
-    scaled = dxn * norm_gain
-    grad = eo + r * scaled - ho * (r * r * r * jnp.mean(scaled * ho, axis=2, keepdims=True))
-    return grad.astype(bf16), jnp.sum(dxn * ho * r, axis=(0, 1))
+def input_grad(place, e, h, norm_gain, item):
+    return finish_call(place, item.kept, item.sent, h, e, norm_gain)
 
 
 class Scatter:
@@ -1188,23 +1424,9 @@
 
     def trade(self):
         place = self.place
-        chip = []
-        for held, came in zip(self.held, self.came):
-            total = jnp.concatenate(held, axis=-1).astype(f32)
-            for block in came:
-                total = total + block.astype(f32)
-            chip.append(total)
-
-        def chosen(index):
-            result = chip[0]
-            for p in range(1, place.parts):
-                result = jnp.where(index == p, chip[p], result)
-            return result
-
-        result = [chosen(place.part)]
-        for d in range(1, place.parts):
-            result.append(place.swap_part(chosen(place.part ^ d).astype(bf16), d).astype(f32))
-        return result
+        mine, send = deal_call(place, self.held, self.came)
+        sends = [send.reshape(mine.shape)] if place.parts == 2 else list(send)
+        return [mine] + [place.swap_part(block, d + 1) for d, block in enumerate(sends)]
 
 
 def body(
@@ -1239,8 +1461,15 @@
     def padded(vector):
         return jnp.pad(vector, (0, head_rows(width) - heads_here))
 
-    h0 = spread_tokens(place, block_input)
-    weights = gather_weights(place, w_gate[0], w_value[0], w_bc[0], w_dt[0], w_out[0])
+    spread = Spread(place, block_input)
+    collected, second = gather_weights(place, w_gate[0], w_value[0], w_bc[0], w_dt[0], w_out[0])
+    collected.prepare()
+    collected.launch()
+    spread.came, collected.next = tie(spread.came, collected.next)
+    collected.land()
+    collected.finish()
+    weights = tuple(collected.result([mixed + LANES, width]))
+    h0 = spread.result()
     taps = jnp.concatenate(
         [
             jnp.concatenate([share(conv_value[0], width), conv_bc[0]], axis=1),
@@ -1278,46 +1507,75 @@
     for turn in range(sections - 1):
         carry = forward_start(place, small)
         shares_in, came = came, {}
-        pieces, halves, terms, e_blocks = list(h0), [], None, None
+        pieces, halves, terms, crossing = list(h0), [], None, []
         for i in span:
             if shares_in is not None:
                 share, terms = arrive(i, shares_in, first, h0, terms, flip)
                 pieces[i] = gather_shares(place, [share], flip)[0]
             if i:
-                pieces[i], halves[-1][1], cotangent = tie(pieces[i], halves[-1][1], cotangent)
+                pieces[i], halves[-1][1] = tie(pieces[i], halves[-1][1])
                 crossing = [place.swap_tensor(halves[-1][1], mask) for mask in bits_of(place.tensors)]
-                if turn == 0 and i == 1:
-                    e_blocks = whole_tokens(place, cotangent)
-            terms, carry = forward_piece(place, pieces[i], weights, small, carry)
+            if second.masks[0]:
+                second.prepare()
+                pieces[i], second.out = tie(pieces[i], second.out)
+                second.launch()
+                terms, carry = forward_piece(place, pieces[i], weights, small, carry)
+                terms, crossing, second.next = tie(terms, crossing, second.next)
+                second.land()
+            else:
+                terms, carry = forward_piece(place, pieces[i], weights, small, carry)
+                terms, crossing = tie(terms, crossing)
             if i:
-                terms, crossing, e_blocks = tie(terms, crossing, e_blocks)
                 halves[-1][1] = halves[-1][1] + sum(crossing)
             halves.append([terms[0], sum_all(place, terms[1][0, :, 0], micro=False, tensor=False)])
         halves[-1][1] = sum_all(place, halves[-1][1], micro=False, part=False)
-        if turn == 0 and e_blocks is None:
-            e_blocks = whole_tokens(place, cotangent)
+        second.finish()
+        if len(weights) == 2:
+            weights += tuple(second.result([width]))
         red = []
         for g, squares in halves:
+            if red:
+                g = red[-1].launch(g)
+            elif turn == 0:
+                g, cotangent = tie(g, cotangent)
+                e_blocks = whole_tokens(place, cotangent)
             own, send = out_call(place, g, factor_of(place, small, squares), weights, small[3])
             red.append(Reduction(place, own, send, jnp.float16))
-            red[-1].launch()
+        red[-1].launch()
         if turn == 0:
+            e_blocks = red[0].land(e_blocks)
             e0 = lay_tokens(place, e_blocks)
-            e0, dn0 = red[0].land((e0, [rows_dot(e, weights[2]) for e in e0]))
+            e0, dn0 = red[-1].land((e0, [rows_dot(e, weights[2]) for e in e0]))
         for i, item in enumerate(red):
             leave(i, out_share(place, pieces[i], item.result()), came, 1, None)
+    second.finish()
+    if len(weights) == 2:
+        weights += tuple(second.result([width]))
     if sections == 1:
         e0 = lay_tokens(place, whole_tokens(place, cotangent))
         dn0 = [rows_dot(e, weights[2]) for e in e0]
 
     carry = forward_start(place, small)
-    kept, sums, lines, terms = [], [], [], None
+    kept, sums, lines, terms, ahead = [], [], [], None, None
     for i in span:
         h = h0[i]
         if came is not None:
-            block, terms = arrive(i, came, first, h0, terms, flip)
-            h = gather_shares(place, [block], flip)[0]
+            if ahead is None:
+                share, terms = arrive(i, came, first, h0, terms, flip)
+                ahead = Gathering(place, [share], flip)
+                ahead.launch()
+                if i + 1 < PIECES:
+                    ahead.came, came[i + 1] = tie(ahead.came, came[i + 1])
+            h = ahead.result()[0]
+            ahead = None
+            if i + 1 < PIECES:
+                share, h = arrive(i + 1, came, first, h0, h, flip)
+                h, share = tie(h, share)
+                ahead = Gathering(place, [share], flip)
+                ahead.launch()
         terms, carry, keep = forward_piece(place, h, weights, small, carry, dn0[i])
+        if ahead is not None:
+            terms, ahead.came = tie(terms, ahead.came)
         kept.append(keep)
         lines.append(terms[2][:, :, 0])
         sums.append(Reduction(place, terms[0], terms[1]))
@@ -1370,7 +1628,7 @@
             if not i and turn == sections - 2 and PIECES > 1:
                 ready, _ = gradient_of(PIECES - 1, came, None)
                 ready.came = red.land(ready.came)
-            share, _ = input_grad(place, es[i], kept[i][0], norm_gain[0], red.result())
+            share, _ = input_grad(place, es[i], kept[i][0], norm_gain[0], red)
         leave(0, share, came, -1, None)
     if homing is None:
         for item in sums:
@@ -1388,6 +1646,10 @@
         if came is not None:
             if red or ready is None:
                 ready, terms = gradient_of(i, came, terms)
+            if red:
+                red[-1].prepare()
+                homing.collect()
+                ready.came, red[-1].going, homing.rows = tie(ready.came, red[-1].going, homing.rows)
             es[i] = ready.result()[0]
         dn, pull, n, gain_grad = normal_piece(es[i], qs[i], kept[i], weights, small)
         pull = sum_all(place, pull, micro=False)
@@ -1425,47 +1687,41 @@
             red.append(ahead)
         small_sums = now if small_sums is None else [a + b for a, b in zip(small_sums, now)]
     outputs = homing.result().reshape(block_input.shape)
+    scatter.prepare()
+    scatter.launch()
+    red[-1].prepare()
+    red[-1].going, dvbd = tie(red[-1].going, dvbd)
+    red[-1].launch()
     mixes = Scatter(place, [add(matrix[2], kept[0][2], dvbd).astype(bf16)])
-    grads, norm_grad = [], 0.0
+    mixes.prepare()
+    mixes.launch()
+    grads, norm_grad = [], jnp.zeros((8, norm_gain.shape[1]), f32)
     for i, item in zip(reversed(span), red[:-1]):
-        block, now = input_grad(place, es[i], kept[i][0], norm_gain[0], item.result())
+        block, now = input_grad(place, es[i], kept[i][0], norm_gain[0], item)
         grads.insert(0, block)
         norm_grad = norm_grad + now
-    for one in (mixes, scatter):
-        one.prepare()
-    mixes.out, scatter.out = red[-1].launch((mixes.out, scatter.out))
-    for one in (scatter, mixes):
-        one.launch()
     scatter.next = red[-1].land(scatter.next)
-    block, now = input_grad(place, es[0], kept[0][0], norm_gain[0], red[-1].result())
+    scatter.land()
+    while scatter.left[0]:
+        scatter.prepare()
+        scatter.launch()
+        scatter.land()
+    block, now = input_grad(place, es[0], kept[0][0], norm_gain[0], red[-1])
     norm_grad = norm_grad + now
     homing = Homing(place, jnp.concatenate([block] + grads, axis=0))
     homing.launch()
-    homing.came, mixes.next = tie(homing.came, mixes.next)
-    homing.turn()
+    scatter = scatter.trade()
+    gate_grad = columns_beside(place, scatter, width, width)
+    out_grad = order([block[:, :width].astype(f32).T for block in scatter], part, 0).reshape(-1, w_out.shape[2])
+    homing.came, mixes.next, gate_grad, out_grad = tie(homing.came, mixes.next, gate_grad, out_grad)
     mixes.land()
     mixes.prepare()
+    homing.collect()
+    mixes.out, homing.rows = tie(mixes.out, homing.rows)
+    homing.turn()
     mixes.launch()
-    for one in (scatter, mixes):
-        one.land()
-        while one.left[0]:
-            one.prepare()
-            one.launch()
-            one.land()
-    input_grads = homing.result().reshape(block_input.shape).astype(f32)
-    scatter, mixes = scatter.trade(), mixes.trade()
-    gates = [block[:, width:] for block in scatter]
-    out_t = [block[:, :width] for block in scatter]
-    gate_grad = beside(gates, part)
-    out_grad = order([block.T for block in out_t], part, 0).reshape(-1, w_out.shape[2])
-    value_grad = beside([block[:, :width] for block in mixes], part)
-    step_grad = beside([block[:, mixed : mixed + heads_here] for block in mixes], part)
-    maps_grad = sum(block[:, width:mixed] for block in mixes).astype(bf16)
-    maps_sum = maps_grad.astype(f32)
-    for mask in bits_of(place.tensors):
-        maps_sum = maps_sum + place.swap_tensor(maps_sum, mask)
-
     packed, gain_grad = small_sums
+    norm_grad = jnp.sum(norm_grad, axis=0)
     row = lax.broadcasted_iota(jnp.int32, (8, mixed), 0)
     packed = jnp.where(row == GAIN_ROW, jnp.pad(gain_grad, ((0, 0), (0, MAPS))), packed)
     lanes = max(mixed, norm_grad.size)
@@ -1473,9 +1729,23 @@
         [jnp.pad(packed, ((0, 0), (0, lanes - mixed))), jnp.pad(norm_grad[None], ((0, 7), (0, lanes - norm_grad.size)))],
         axis=0,
     )
-    packed, homing.rows = tie(packed, homing.rows)
+    packed, mixes.next = tie(packed, mixes.next)
+    mixes.land()
+    while mixes.left[0]:
+        mixes.prepare()
+        mixes.launch()
+        mixes.land()
     packed = sum_all(place, packed, part=False, tensor=False)
     by_part = [packed] + [place.swap_part(packed, d) for d in range(1, parts)]
+    input_grads = homing.result().reshape(block_input.shape).astype(f32)
+    mixes = mixes.trade()
+    value_grad = columns_beside(place, mixes, 0, width)
+    step_grad = beside([block[:, mixed : mixed + heads_here].astype(f32) for block in mixes], part)
+    maps_grad = sum(block[:, width:mixed].astype(f32) for block in mixes).astype(bf16)
+    maps_sum = maps_grad.astype(f32)
+    for mask in bits_of(place.tensors):
+        maps_sum = maps_sum + place.swap_tensor(maps_sum, mask)
+
     both = by_part[0]
     for distance in range(1, parts):
         both = both + by_part[distance]

time: 557 us -> 540 us (0.969)
  other arithmetic: 75 us -> 37.8 us
  Pallas kernels: 141 us -> 172 us
  local copies, waits for them, and re-layouts: 80.9 us -> 66.1 us
    pallas_call x0 -> x27, Pallas kernels: none -> 28.2 us  [the longest x13 9.5 us: order(): pl.pallas_call(functools.partial(order_kernel, count, axis), grid_spec=pl...]
    ppermute x49 -> x54, waiting for transfers between devices: 82.5 us -> 100 us  [swap_part(): lax.ppermute(block, 'context', [(i, i ^ mask) for i in range(self.context)])]
    ppermute x22, waiting for transfers between devices: 63.8 us -> 48.9 us  [swap_tensor(): lax.ppermute(block, 'tensor', [(i, i ^ mask) for i in range(self.tensors)])]
    select_n x16 -> x5, other arithmetic: 24.5 us -> 9.68 us  [order(): result = jnp.where(place == d, jnp.expand_dims(blocks[d], axis), result)]
    broadcast_in_dim x10 -> x2, local copies, waits for them, and re-layouts: 13.3 us -> 2.22 us  [order(): result = jnp.where(place == d, jnp.expand_dims(blocks[d], axis), result)]
    squeeze x12 -> x19, local copies, waits for them, and re-layouts: 4.46 us -> 15.4 us  [pick(): return lax.dynamic_index_in_dim(array, index, axis, False)]
    convert_element_type x13 -> x2, other arithmetic: 12.9 us -> 2.53 us  [prepare(): side(place.tensor ^ d).astype(self.kind)]
    reduce_sum x3 -> x1, other arithmetic: 7.62 us -> 0.02 us  [body(): norm_grad = jnp.sum(norm_grad, axis=0)]
  transfers between devices with their start and end apart: 75 -> 80, of which waited for: 37 -> 36; matrix products, arithmetic and copies ran while one was open for 22% -> 14% of each run, Pallas kernels for 22% -> 29%
where the time goes in v2:
time: 540 us; the launch traced here: 531 us
  Pallas kernels  172 us (32%)
  waiting for transfers between devices  159 us (29%)
  starting transfers between devices  76.4 us (14%)
  local copies, waits for them, and re-layouts  66.1 us (12%)
  other arithmetic  37.8 us (7%)
  matrix products  17 us (3%)
    ppermute x54, waiting for transfers between devices, swap_part(): lax.ppermute(block, 'context', [(i, i ^ mask) for i in range(self.context)])  100 us
    pallas_call x4, Pallas kernels, backward_call(): pl.pallas_call(functools.partial(backward_kernel, exact, width, place.par...  71.6 us
    pallas_call x4, Pallas kernels, forward_call(): pl.pallas_call(functools.partial(forward_kernel, keep, width, place.parts...  51.1 us
    ppermute x22, waiting for transfers between devices, swap_tensor(): lax.ppermute(block, 'tensor', [(i, i ^ mask) for i in range(self.tensors)])  48.9 us
    ppermute x54, starting transfers between devices, swap_part(): lax.ppermute(block, 'context', [(i, i ^ mask) for i in range(self.context)])  38.5 us
    unnamed x262, local copies, waits for them, and re-layouts  37.5 us
    ppermute x22, starting transfers between devices, swap_tensor(): lax.ppermute(block, 'tensor', [(i, i ^ mask) for i in range(self.tensors)])  28.1 us
    squeeze x19, local copies, waits for them, and re-layouts, pick(): return lax.dynamic_index_in_dim(array, index, axis, False)  15.4 us
  transfers between devices with their start and end apart: 80, of which 36 were waited for; matrix products, arithmetic and copies ran while one was open for 14% of the time, Pallas kernels for 29%

profile of v2, /device:TPU:0, one launch (start us, length us, event | category | flops | bytes accessed | tf_op | source)
XLA Modules:
  0.0 530.8 jit_solution(11673817751376455664)
XLA Ops:
  4.9 3.6 collective-permute-start.2
  14.3 4.0 collective-permute-done.1
  23.4 10.9 %collective-permute-done.4.refs_1_ = bf16[1,192,1920]{2,1,0:T(8,128)(2,1)S(1)} collective-permute-done((bf16[1,192,1920]{2,1,0:T(8,128)(2,1)S(1)}, bf16[1,192,1920]{2,1,0:T(8,128)(2,1)S(1)}, u32[]{:S(2)}, u32[]{:S(2)}) %collective-permute-start.4) | collective-permute-done | bytes 737312 | tf_op jit(solution)/shard_map/ppermute | solution.py:824
  44.7 30.0 %collective-permute-done.9.refs_2_ = bf16[2,192,1920]{2,1,0:T(8,128)(2,1)} collective-permute-done((bf16[2,192,1920]{2,1,0:T(8,128)(2,1)}, bf16[2,192,1920]{2,1,0:T(8,128)(2,1)}, u32[]{:S(2)}, u32[]{:S(2)}) %collective-permute-start.9) | collective-permute-done | bytes 1474592 | tf_op jit(solution)/shard_map/ppermute | solution.py:824
  74.7 2.7 collective-permute-done.10.refs_5_
  77.4 2.8 lay_rows.2
  80.3 4.3 broadcast_select_fusion.1
  87.0 11.4 %section_forward.4 = (f32[512,768]{1,0:T(8,128)S(1)}, f32[2,4,1,128]{3,2,1,0:T(1,128)S(1)}, f32[128,768]{1,0:T(8,128)S(1)}, f32[8,1024]{1,0:T(8,128)S(1)}) custom-call(s32[1]{0:T(128)} %bitcast.1.part_ref.index_ref, bf16[512,1536]{1,0:T(8,128)(2,1)S(1)} %bitcast.401, bf16[1536,1152]{1,0:T(8,128)(2,1)S(1)} %bitcast.442, bf16[1536,768]{1,0:T(8,128)(2,1)S(1)} %bitcast.450, ...), custom_call_target="tpu_custom_call" | custom-call | flops 15728640000 | bytes 12582912 | tf_op jit(solution)/shard_map/section_forward/pallas_call | solution.py:360
  103.3 12.1 %section_forward.5 = (f32[512,768]{1,0:T(8,128)S(1)}, f32[2,4,1,128]{3,2,1,0:T(1,128)S(1)}, f32[128,768]{1,0:T(8,128)}, f32[8,1024]{1,0:T(8,128)}) custom-call(s32[1]{0:T(128)} %bitcast.1.part_ref.index_ref, bf16[512,1536]{1,0:T(8,128)(2,1)S(1)} %bitcast.398, bf16[1536,1152]{1,0:T(8,128)(2,1)S(1)} %bitcast.443, bf16[1536,768]{1,0:T(8,128)(2,1)S(1)} %bitcast.451, ...), custom_call_target="tpu_custom_call" | custom-call | flops 15728640000 | bytes 12582912 | tf_op jit(solution)/shard_map/section_forward/pallas_call | solution.py:360
  118.6 3.5 out_forward.2
  134.0 3.5 out_forward.3
  138.6 7.7 %collective-permute-done.24 = bf16[128,1536]{1,0:T(8,128)(2,1)S(1)} collective-permute-done((bf16[128,1536]{1,0:T(8,128)(2,1)S(1)}, bf16[128,1536]{1,0:T(8,128)(2,1)S(1)}, u32[]{:S(2)}, u32[]{:S(2)}) %collective-permute-start.24) | collective-permute-done | bytes 393248 | tf_op jit(solution)/shard_map/ppermute | solution.py:824
  150.5 4.4 collective-permute-start.27
  156.9 2.2 broadcast_select_fusion
  159.4 2.6 copy-done.12
  164.7 7.6 %collective-permute-done.21 = f16[2,64,1536]{2,1,0:T(8,128)(2,1)S(1)} collective-permute-done((f16[2,64,1536]{2,1,0:T(8,128)(2,1)S(1)}, f16[2,64,1536]{2,1,0:T(8,128)(2,1)S(1)}, u32[]{:S(2)}, u32[]{:S(2)}) %collective-permute-start.21) | collective-permute-done | bytes 393248 | tf_op jit(solution)/shard_map/ppermute | solution.py:830
  173.8 2.5 collective-permute-start.28
  176.3 2.8 collective-permute-start.29
  179.2 6.7 %collective-permute-done.28.refs_1_ = bf16[2,64,1536]{2,1,0:T(8,128)(2,1)S(1)} collective-permute-done((bf16[2,64,1536]{2,1,0:T(8,128)(2,1)S(1)}, bf16[2,64,1536]{2,1,0:T(8,128)(2,1)S(1)}, u32[]{:S(2)}, u32[]{:S(2)}) %collective-permute-start.28) | collective-permute-done | bytes 393248 | tf_op jit(solution)/shard_map/ppermute | solution.py:830
  185.9 7.2 %collective-permute-done.29 = bf16[2,64,1536]{2,1,0:T(8,128)(2,1)S(1)} collective-permute-done((bf16[2,64,1536]{2,1,0:T(8,128)(2,1)S(1)}, bf16[2,64,1536]{2,1,0:T(8,128)(2,1)S(1)}, u32[]{:S(2)}, u32[]{:S(2)}) %collective-permute-start.29) | collective-permute-done | bytes 393248 | tf_op jit(solution)/shard_map/ppermute | solution.py:834
  193.4 2.3 collective-permute-done.30.refs_1_
  195.9 3.5 collective-permute-start.31
  199.4 13.5 %section_forward.6 = (f32[2,128,1536]{2,1,0:T(8,128)S(1)}, bf16[1,2,128,1536]{3,2,1,0:T(8,128)(2,1)S(1)}, f32[2,4,1,128]{3,2,1,0:T(1,128)S(1)}, f32[128,768]{1,0...) custom-call(s32[1]{0:T(128)} %bitcast.1.part_ref.index_ref, ...), custom_call_target="tpu_custom_call" | custom-call | flops 15728640000 | bytes 12582912 | tf_op jit(solution)/shard_map/section_forward/pallas_call | solution.py:360
  215.6 14.2 %section_forward.7 = (f32[2,128,1536]{2,1,0:T(8,128)S(1)}, bf16[1,2,128,1536]{3,2,1,0:T(8,128)(2,1)S(1)}, f32[2,4,1,128]{3,2,1,0:T(1,128)S(1)}, f32[128,768]{1,0...) custom-call(s32[1]{0:T(128)} %bitcast.1.part_ref.index_ref, ...), custom_call_target="tpu_custom_call" | custom-call | flops 15728640000 | bytes 12582912 | tf_op jit(solution)/shard_map/section_forward/pallas_call | solution.py:360
  240.3 17.1 %section_backward.4 = (f32[2,128,1536]{2,1,0:T(8,128)S(1)}, bf16[1,2,128,1536]{3,2,1,0:T(8,128)(2,1)S(1)}, bf16[512,1152]{1,0:T(8,128)(2,1)}, f32[128,768]{1,0:T...) custom-call(s32[1]{0:T(128)} %bitcast.1.part_ref.index_ref, f32[512,768]{1,0:T(8,128)S(1)} %get-tuple-element.301.dy_ref, ...), custom_call_target="tpu_custom_call" | custom-call | flops 23592960000 | bytes 12582912 | tf_op jit(solution)/shard_map/section_backward/pallas_call | solution.py:702
  260.0 2.3 collective-permute-done.39.refs_0_
  265.6 8.4 %collective-permute-done.40.refs_0_ = bf16[2,64,1536]{2,1,0:T(8,128)(2,1)S(1)} collective-permute-done((bf16[2,64,1536]{2,1,0:T(8,128)(2,1)S(1)}, bf16[2,64,1536]{2,1,0:T(8,128)(2,1)S(1)}, u32[]{:S(2)}, u32[]{:S(2)}) %collective-permute-start.40) | collective-permute-done | bytes 393248 | tf_op jit(solution)/shard_map/ppermute | solution.py:830
  273.9 2.2 finish_gradient.4
  277.5 17.2 %section_backward.5 = (f32[2,128,1536]{2,1,0:T(8,128)S(1)}, bf16[1,2,128,1536]{3,2,1,0:T(8,128)(2,1)}, bf16[512,1152]{1,0:T(8,128)(2,1)}, f32[128,768]{1,0:T(8,1...) custom-call(s32[1]{0:T(128)} %bitcast.1.part_ref.index_ref, f32[512,768]{1,0:T(8,128)S(1)} %get-tuple-element.319.dy_ref, ...), custom_call_target="tpu_custom_call" | custom-call | flops 23592960000 | bytes 12582912 | tf_op jit(solution)/shard_map/section_backward/pallas_call | solution.py:702
  295.9 2.2 collective-permute-done.41
  307.2 5.8 %collective-permute-done.44.refs_1_ = bf16[2,64,1536]{2,1,0:T(8,128)(2,1)} collective-permute-done((bf16[2,64,1536]{2,1,0:T(8,128)(2,1)}, bf16[2,64,1536]{2,1,0:T(8,128)(2,1)}, u32[]{:S(2)}, u32[]{:S(2)}) %collective-permute-start.44) | collective-permute-done | bytes 393248 | tf_op jit(solution)/shard_map/ppermute | solution.py:830
  313.0 8.0 %collective-permute-done.43.refs_0_ = bf16[2,64,1536]{2,1,0:T(8,128)(2,1)} collective-permute-done((bf16[2,64,1536]{2,1,0:T(8,128)(2,1)}, bf16[2,64,1536]{2,1,0:T(8,128)(2,1)}, u32[]{:S(2)}, u32[]{:S(2)}) %collective-permute-start.43) | collective-permute-done | bytes 393248 | tf_op jit(solution)/shard_map/ppermute | solution.py:830
  328.6 3.1 finish_gradient.5
  333.4 3.6 fusion.64
  344.3 18.2 %section_backward.6 = (f32[2,128,1536]{2,1,0:T(8,128)S(1)}, bf16[1,2,128,1536]{3,2,1,0:T(8,128)(2,1)S(1)}, bf16[512,1152]{1,0:T(8,128)(2,1)S(1)}, f32[128,768]{1...) custom-call(s32[1]{0:T(128)} %bitcast.1.part_ref.index_ref, f32[512,768]{1,0:T(8,128)S(1)} %get-tuple-element.349.dy_ref, ...), custom_call_target="tpu_custom_call" | custom-call | flops 23592960000 | bytes 12582912 | tf_op jit(solution)/shard_map/section_backward/pallas_call | solution.py:702
  367.5 7.5 %collective-permute-done.52.refs_1_ = bf16[2,64,1536]{2,1,0:T(8,128)(2,1)S(1)} collective-permute-done((bf16[2,64,1536]{2,1,0:T(8,128)(2,1)S(1)}, bf16[2,64,1536]{2,1,0:T(8,128)(2,1)S(1)}, u32[]{:S(2)}, u32[]{:S(2)}) %collective-permute-start.52) | collective-permute-done | bytes 393248 | tf_op jit(solution)/shard_map/ppermute | solution.py:830
  375.4 2.3 collective-permute-done.54.refs_1_
  385.0 3.0 fusion.65
  388.0 3.1 add.530
  404.7 19.1 %section_backward.7 = (f32[2,128,1536]{2,1,0:T(8,128)S(1)}, bf16[1,2,128,1536]{3,2,1,0:T(8,128)(2,1)}, bf16[512,1152]{1,0:T(8,128)(2,1)S(1)}, f32[128,768]{1,0:T...) custom-call(s32[1]{0:T(128)} %bitcast.1.part_ref.index_ref, f32[512,768]{1,0:T(8,128)S(1)} %get-tuple-element.380.dy_ref, ...), custom_call_target="tpu_custom_call" | custom-call | flops 23592960000 | bytes 12582912 | tf_op jit(solution)/shard_map/section_backward/pallas_call | solution.py:702
  440.2 2.3 fusion.67
  442.5 2.4 fusion
  468.5 9.5 %collective-permute-done.65.refs_1_ = bf16[64,1536]{1,0:T(8,128)(2,1)} collective-permute-done((bf16[64,1536]{1,0:T(8,128)(2,1)}, bf16[64,1536]{1,0:T(8,128)(2,1)}, u32[]{:S(2)}, u32[]{:S(2)}) %collective-permute-start.65) | collective-permute-done | bytes 196640 | tf_op jit(solution)/shard_map/ppermute | solution.py:824
  478.0 4.3 collective-permute-done.67.refs_3_
  489.9 7.5 %collective-permute-done.72.refs_2_ = bf16[192,1152]{1,0:T(8,128)(2,1)S(1)} collective-permute-done((bf16[192,1152]{1,0:T(8,128)(2,1)S(1)}, bf16[192,1152]{1,0:T(8,128)(2,1)S(1)}, u32[]{:S(2)}, u32[]{:S(2)}) %collective-permute-start.72) | collective-permute-done | bytes 442400 | tf_op jit(solution)/shard_map/ppermute | solution.py:824
  500.7 2.5 order_blocks.22
  505.7 2.6 collective-permute-done.75
  527.0 2.9 collective-permute-done.79
  (558 shorter events, 204.7 us)
Async XLA Ops:
  9.1 25.2 %collective-permute-start.4 = (bf16[1,192,1920]{2,1,0:T(8,128)(2,1)S(1)}, bf16[1,192,1920]{2,1,0:T(8,128)(2,1)S(1)}, u32[]{:S(2)}, u32[]{:S(2)}) collective-permute-start(bf16[1,192,1920]{2,1,0:T(8,128)(2,1)S(1)} %get-tuple-element.515.refs_0_), channel_id=1, source_target_pairs={{0,4},{2,6},{4,0},{6,2},{8,12},{10,14},{12,8},{14,10},{1,5},{3,7},... | collective-permute-start | bytes 2211848 | tf_op jit(solution)/shard_map/ppermute | solution.py:824
  11.0 24.4 %collective-permute-start.6 = (bf16[1,192,1920]{2,1,0:T(8,128)(2,1)S(1)}, bf16[1,192,1920]{2,1,0:T(8,128)(2,1)S(1)}, u32[]{:S(2)}, u32[]{:S(2)}) collective-permute-start(bf16[1,192,1920]{2,1,0:T(8,128)(2,1)S(1)} %collective-permute-done.5.refs_3_), channel_id=1, source_target_pairs={{0,8},{2,10},{4,12},{6,14},{8,0},{10,2},{12,4},{14,6},{1,9},{3,11}... | collective-permute-start | bytes 2211848 | tf_op jit(solution)/shard_map/ppermute | solution.py:824
  20.5 14.9 %collective-permute-start.3 = (bf16[3,64,1536]{2,1,0:T(8,128)(2,1)}, bf16[3,64,1536]{2,1,0:T(8,128)(2,1)}, u32[]{:S(2)}, u32[]{:S(2)}) collective-permute-start(bf16[3,64,1536]{2,1,0:T(8,128)(2,1)} %pad_maximum_fusion.6), channel_id=1, source_target_pairs={{0,1},{1,0},{2,3},{3,2},{4,5},{5,4},{6,7},{7,6},{8,9},{9,8},{10,11... | collective-permute-start | bytes 1769480 | tf_op jit(solution)/shard_map/ppermute | solution.py:830
  38.3 41.9 %collective-permute-start.7 = (bf16[4,128,1536]{2,1,0:T(8,128)(2,1)}, bf16[4,128,1536]{2,1,0:T(8,128)(2,1)}, u32[]{:S(2)}, u32[]{:S(2)}) collective-permute-start(bf16[4,128,1536]{2,1,0:T(8,128)(2,1)} %select_select_fusion.1), channel_id=1, source_target_pairs={{0,2},{2,0},{4,6},{6,4},{8,10},{10,8},{12,14},{14,12},{1,3},{3,1},... | collective-permute-start | bytes 4718600 | tf_op jit(solution)/shard_map/ppermute | solution.py:824
  39.6 35.1 %collective-permute-start.9 = (bf16[2,192,1920]{2,1,0:T(8,128)(2,1)}, bf16[2,192,1920]{2,1,0:T(8,128)(2,1)}, u32[]{:S(2)}, u32[]{:S(2)}) collective-permute-start(bf16[2,192,1920]{2,1,0:T(8,128)(2,1)} %pad_maximum_fusion), channel_id=1, source_target_pairs={{0,8},{2,10},{4,12},{6,14},{8,0},{10,2},{12,4},{14,6},{1,9},{3,11}... | collective-permute-start | bytes 4423688 | tf_op jit(solution)/shard_map/ppermute | solution.py:824
  42.7 34.7 %collective-permute-start.10 = (bf16[2,192,1920]{2,1,0:T(8,128)(2,1)}, bf16[2,192,1920]{2,1,0:T(8,128)(2,1)}, u32[]{:S(2)}, u32[]{:S(2)}) collective-permute-start(bf16[2,192,1920]{2,1,0:T(8,128)(2,1)} %pad_maximum_fusion.1), channel_id=1, source_target_pairs={{0,4},{2,6},{4,0},{6,2},{8,12},{10,14},{12,8},{14,10},{1,5},{3,7},... | collective-permute-start | bytes 4423688 | tf_op jit(solution)/shard_map/ppermute | solution.py:824
  43.7 41.0 %collective-permute-start.8 = (bf16[1,192,768]{2,1,0:T(8,128)(2,1)}, bf16[1,192,768]{2,1,0:T(8,128)(2,1)}, u32[]{:S(2)}, u32[]{:S(2)}) collective-permute-start(bf16[1,192,768]{2,1,0:T(8,128)(2,1)} %get-tuple-element.505), channel_id=1, source_target_pairs={{0,2},{2,0},{4,6},{6,4},{8,10},{10,8},{12,14},{14,12},{1,3},{3,1},... | collective-permute-start | bytes 884744 | tf_op jit(solution)/shard_map/ppermute | solution.py:824
  84.8 13.6 %collective-permute-start.11 = (bf16[1,192,768]{2,1,0:T(8,128)(2,1)S(1)}, bf16[1,192,768]{2,1,0:T(8,128)(2,1)S(1)}, u32[]{:S(2)}, u32[]{:S(2)}) collective-permute-start(bf16[1,192,768]{2,1,0:T(8,128)(2,1)S(1)} %get-tuple-element.236.refs_0_), channel_id=1, source_target_pairs={{0,4},{2,6},{4,0},{6,2},{8,12},{10,14},{12,8},{14,10},{1,5},{3,7},... | collective-permute-start | bytes 884744 | tf_op jit(solution)/shard_map/ppermute | solution.py:824
  85.1 13.3 %collective-permute-start.12 = (bf16[1,192,768]{2,1,0:T(8,128)(2,1)}, bf16[1,192,768]{2,1,0:T(8,128)(2,1)S(1)}, u32[]{:S(2)}, u32[]{:S(2)}) collective-permute-start(bf16[1,192,768]{2,1,0:T(8,128)(2,1)} %collective-permute-done.8.refs_3_), channel_id=1, source_target_pairs={{0,8},{2,10},{4,12},{6,14},{8,0},{10,2},{12,4},{14,6},{1,9},{3,11}... | collective-permute-start | bytes 884744 | tf_op jit(solution)/shard_map/ppermute | solution.py:824
  99.7 15.7 %collective-permute-start.14 = (f32[4,128]{1,0:T(4,128)S(1)}, f32[4,128]{1,0:T(4,128)S(1)}, u32[]{:S(2)}, u32[]{:S(2)}) collective-permute-start(f32[4,128]{1,0:T(4,128)S(1)} %fusion.52), channel_id=1, source_target_pairs={{0,1},{1,0},{2,3},{3,2},{4,5},{5,4},{6,7},{7,6},{8,9},{9,8},{10,11... | collective-permute-start | bytes 6152 | tf_op jit(solution)/shard_map/ppermute | solution.py:830
  101.3 15.4 %collective-permute-start.15 = (bf16[2,192,768]{2,1,0:T(8,128)(2,1)S(1)}, bf16[2,192,768]{2,1,0:T(8,128)(2,1)S(1)}, u32[]{:S(2)}, u32[]{:S(2)}) collective-permute-start(bf16[2,192,768]{2,1,0:T(8,128)(2,1)S(1)} %pad_maximum_fusion.7), channel_id=1, source_target_pairs={{0,8},{2,10},{4,12},{6,14},{8,0},{10,2},{12,4},{14,6},{1,9},{3,11}... | collective-permute-start | bytes 1769480 | tf_op jit(solution)/shard_map/ppermute | solution.py:824
  101.6 15.2 %collective-permute-start.16 = (bf16[2,192,768]{2,1,0:T(8,128)(2,1)S(1)}, bf16[2,192,768]{2,1,0:T(8,128)(2,1)S(1)}, u32[]{:S(2)}, u32[]{:S(2)}) collective-permute-start(bf16[2,192,768]{2,1,0:T(8,128)(2,1)S(1)} %pad_maximum_fusion.8), channel_id=1, source_target_pairs={{0,4},{2,6},{4,0},{6,2},{8,12},{10,14},{12,8},{14,10},{1,5},{3,7},... | collective-permute-start | bytes 1769480 | tf_op jit(solution)/shard_map/ppermute | solution.py:824
  125.4 13.3 %collective-permute-start.23 = (bf16[128,1536]{1,0:T(8,128)(2,1)S(1)}, bf16[128,1536]{1,0:T(8,128)(2,1)S(1)}, u32[]{:S(2)}, u32[]{:S(2)}) collective-permute-start(bf16[128,1536]{1,0:T(8,128)(2,1)S(1)} %get-tuple-element.484), channel_id=1, source_target_pairs={{0,4},{2,6},{4,0},{6,2},{8,12},{10,14},{12,8},{14,10},{1,5},{3,7},... | collective-permute-start | bytes 1179656 | tf_op jit(solution)/shard_map/ppermute | solution.py:824
  127.2 19.2 %collective-permute-start.24 = (bf16[128,1536]{1,0:T(8,128)(2,1)S(1)}, bf16[128,1536]{1,0:T(8,128)(2,1)S(1)}, u32[]{:S(2)}, u32[]{:S(2)}) collective-permute-start(bf16[128,1536]{1,0:T(8,128)(2,1)S(1)} %get-tuple-element.483), channel_id=1, source_target_pairs={{0,8},{2,10},{4,12},{6,14},{8,0},{10,2},{12,4},{14,6},{1,9},{3,11}... | collective-permute-start | bytes 1179656 | tf_op jit(solution)/shard_map/ppermute | solution.py:824
  127.7 18.7 %collective-permute-start.25 = (bf16[128,1536]{1,0:T(8,128)(2,1)S(1)}, bf16[128,1536]{1,0:T(8,128)(2,1)S(1)}, u32[]{:S(2)}, u32[]{:S(2)}) collective-permute-start(bf16[128,1536]{1,0:T(8,128)(2,1)S(1)} %get-tuple-element.482), channel_id=1, source_target_pairs={{0,12},{2,14},{4,8},{6,10},{8,4},{10,6},{12,0},{14,2},{1,13},{3,15... | collective-permute-start | bytes 1179656 | tf_op jit(solution)/shard_map/ppermute | solution.py:824
  130.6 15.7 %collective-permute-start.22 = (f16[2,64,1536]{2,1,0:T(8,128)(2,1)S(1)}, f16[2,64,1536]{2,1,0:T(8,128)(2,1)S(1)}, u32[]{:S(2)}, u32[]{:S(2)}) collective-permute-start(f16[2,64,1536]{2,1,0:T(8,128)(2,1)S(1)} %fusion.26), channel_id=1, source_target_pairs={{0,1},{1,0},{2,3},{3,2},{4,5},{5,4},{6,7},{7,6},{8,9},{9,8},{10,11... | collective-permute-start | bytes 1179656 | tf_op jit(solution)/shard_map/ppermute | solution.py:830
  138.6 16.3 %collective-permute-start.20 = (f32[2,128,1536]{2,1,0:T(8,128)}, f32[2,128,1536]{2,1,0:T(8,128)}, u32[]{:S(2)}, u32[]{:S(2)}) collective-permute-start(f32[2,128,1536]{2,1,0:T(8,128)} %bitcast.68), channel_id=1, source_target_pairs={{0,2},{2,0},{4,6},{6,4},{8,10},{10,8},{12,14},{14,12},{1,3},{3,1},... | collective-permute-start | bytes 4718600 | tf_op jit(solution)/shard_map/ppermute | solution.py:824
  150.5 23.3 %collective-permute-start.27 = (bf16[2,64,1536]{2,1,0:T(8,128)(2,1)S(1)}, bf16[2,64,1536]{2,1,0:T(8,128)(2,1)S(1)}, u32[]{:S(2)}, u32[]{:S(2)}) collective-permute-start(bf16[2,64,1536]{2,1,0:T(8,128)(2,1)S(1)} %fusion.11), channel_id=1, source_target_pairs={{0,17},{1,16},{2,19},{3,18},{4,21},{5,20},{6,23},{7,22},{8,25},{9,... | collective-permute-start | bytes 1179656 | tf_op jit(solution)/shard_map/ppermute | solution.py:834
  156.2 16.2 %collective-permute-start.21 = (f16[2,64,1536]{2,1,0:T(8,128)(2,1)S(1)}, f16[2,64,1536]{2,1,0:T(8,128)(2,1)S(1)}, u32[]{:S(2)}, u32[]{:S(2)}) collective-permute-start(f16[2,64,1536]{2,1,0:T(8,128)(2,1)S(1)} %fusion.27), channel_id=1, source_target_pairs={{0,1},{1,0},{2,3},{3,2},{4,5},{5,4},{6,7},{7,6},{8,9},{9,8},{10,11... | collective-permute-start | bytes 1179656 | tf_op jit(solution)/shard_map/ppermute | solution.py:830
  173.8 12.1 %collective-permute-start.28 = (bf16[2,64,1536]{2,1,0:T(8,128)(2,1)S(1)}, bf16[2,64,1536]{2,1,0:T(8,128)(2,1)S(1)}, u32[]{:S(2)}, u32[]{:S(2)}) collective-permute-start(bf16[2,64,1536]{2,1,0:T(8,128)(2,1)S(1)} %bitcast_select_fusion.2.refs_0_), channel_id=1, source_target_pairs={{0,1},{1,0},{2,3},{3,2},{4,5},{5,4},{6,7},{7,6},{8,9},{9,8},{10,11... | collective-permute-start | bytes 1179656 | tf_op jit(solution)/shard_map/ppermute | solution.py:830
  176.3 16.7 %collective-permute-start.29 = (bf16[2,64,1536]{2,1,0:T(8,128)(2,1)S(1)}, bf16[2,64,1536]{2,1,0:T(8,128)(2,1)S(1)}, u32[]{:S(2)}, u32[]{:S(2)}) collective-permute-start(bf16[2,64,1536]{2,1,0:T(8,128)(2,1)S(1)} %fusion.16), channel_id=1, source_target_pairs={{0,17},{1,16},{2,19},{3,18},{4,21},{5,20},{6,23},{7,22},{8,25},{9,... | collective-permute-start | bytes 1179656 | tf_op jit(solution)/shard_map/ppermute | solution.py:834
  195.9 17.0 %collective-permute-start.31 = (bf16[2,64,1536]{2,1,0:T(8,128)(2,1)S(1)}, bf16[2,64,1536]{2,1,0:T(8,128)(2,1)S(1)}, u32[]{:S(2)}, u32[]{:S(2)}) collective-permute-start(bf16[2,64,1536]{2,1,0:T(8,128)(2,1)S(1)} %bitcast_select_fusion.1.refs_0_), channel_id=1, source_target_pairs={{0,1},{1,0},{2,3},{3,2},{4,5},{5,4},{6,7},{7,6},{8,9},{9,8},{10,11... | collective-permute-start | bytes 1179656 | tf_op jit(solution)/shard_map/ppermute | solution.py:830
  213.2 18.9 %collective-permute-start.34 = (bf16[2,128,1536]{2,1,0:T(8,128)(2,1)S(1)}, bf16[2,128,1536]{2,1,0:T(8,128)(2,1)S(1)}, u32[]{:S(2)}, u32[]{:S(2)}) collective-permute-start(bf16[2,128,1536]{2,1,0:T(8,128)(2,1)S(1)} %bitcast.458), channel_id=1, source_target_pairs={{0,2},{2,0},{4,6},{6,4},{8,10},{10,8},{12,14},{14,12},{1,3},{3,1},... | collective-permute-start | bytes 2359304 | tf_op jit(solution)/shard_map/ppermute | solution.py:824
  233.3 26.6 %collective-permute-start.36 = (bf16[2,64,1536]{2,1,0:T(8,128)(2,1)S(1)}, bf16[2,64,1536]{2,1,0:T(8,128)(2,1)S(1)}, u32[]{:S(2)}, u32[]{:S(2)}) collective-permute-start(bf16[2,64,1536]{2,1,0:T(8,128)(2,1)S(1)} %bitcast.464), channel_id=1, source_target_pairs={{0,1},{1,0},{2,3},{3,2},{4,5},{5,4},{6,7},{7,6},{8,9},{9,8},{10,11... | collective-permute-start | bytes 1179656 | tf_op jit(solution)/shard_map/ppermute | solution.py:830
  236.9 22.9 %collective-permute-start.35 = (bf16[2,64,1536]{2,1,0:T(8,128)(2,1)S(1)}, bf16[2,64,1536]{2,1,0:T(8,128)(2,1)S(1)}, u32[]{:S(2)}, u32[]{:S(2)}) collective-permute-start(bf16[2,64,1536]{2,1,0:T(8,128)(2,1)S(1)} %bitcast.466), channel_id=1, source_target_pairs={{0,1},{1,0},{2,3},{3,2},{4,5},{5,4},{6,7},{7,6},{8,9},{9,8},{10,11... | collective-permute-start | bytes 1179656 | tf_op jit(solution)/shard_map/ppermute | solution.py:830
  262.5 11.5 %collective-permute-start.40 = (bf16[2,64,1536]{2,1,0:T(8,128)(2,1)S(1)}, bf16[2,64,1536]{2,1,0:T(8,128)(2,1)S(1)}, u32[]{:S(2)}, u32[]{:S(2)}) collective-permute-start(bf16[2,64,1536]{2,1,0:T(8,128)(2,1)S(1)} %bitcast.467), channel_id=1, source_target_pairs={{0,1},{1,0},{2,3},{3,2},{4,5},{5,4},{6,7},{7,6},{8,9},{9,8},{10,11... | collective-permute-start | bytes 1179656 | tf_op jit(solution)/shard_map/ppermute | solution.py:830
  276.2 21.9 %collective-permute-start.41 = (bf16[2,64,1536]{2,1,0:T(8,128)(2,1)S(1)}, bf16[2,64,1536]{2,1,0:T(8,128)(2,1)S(1)}, u32[]{:S(2)}, u32[]{:S(2)}) collective-permute-start(bf16[2,64,1536]{2,1,0:T(8,128)(2,1)S(1)} %get-tuple-element.327), channel_id=1, source_target_pairs={{16,0},{17,1},{18,2},{19,3},{20,4},{21,5},{22,6},{23,7},{24,8},{25... | collective-permute-start | bytes 1179656 | tf_op jit(solution)/shard_map/ppermute | solution.py:834
  300.8 12.2 %collective-permute-start.44 = (bf16[2,64,1536]{2,1,0:T(8,128)(2,1)}, bf16[2,64,1536]{2,1,0:T(8,128)(2,1)}, u32[]{:S(2)}, u32[]{:S(2)}) collective-permute-start(bf16[2,64,1536]{2,1,0:T(8,128)(2,1)} %bitcast_select_fusion.refs_0_), channel_id=1, source_target_pairs={{0,1},{1,0},{2,3},{3,2},{4,5},{5,4},{6,7},{7,6},{8,9},{9,8},{10,11... | collective-permute-start | bytes 1179656 | tf_op jit(solution)/shard_map/ppermute | solution.py:830
  305.6 15.4 %collective-permute-start.43 = (bf16[2,64,1536]{2,1,0:T(8,128)(2,1)}, bf16[2,64,1536]{2,1,0:T(8,128)(2,1)}, u32[]{:S(2)}, u32[]{:S(2)}) collective-permute-start(bf16[2,64,1536]{2,1,0:T(8,128)(2,1)} %bitcast.111), channel_id=1, source_target_pairs={{0,1},{1,0},{2,3},{3,2},{4,5},{5,4},{6,7},{7,6},{8,9},{9,8},{10,11... | collective-permute-start | bytes 1179656 | tf_op jit(solution)/shard_map/ppermute | solution.py:830
  331.7 31.6 %collective-permute-start.45 = (bf16[2,64,1536]{2,1,0:T(8,128)(2,1)S(1)}, bf16[2,64,1536]{2,1,0:T(8,128)(2,1)S(1)}, u32[]{:S(2)}, u32[]{:S(2)}) collective-permute-start(bf16[2,64,1536]{2,1,0:T(8,128)(2,1)S(1)} %get-tuple-element.335), channel_id=1, source_target_pairs={{16,0},{17,1},{18,2},{19,3},{20,4},{21,5},{22,6},{23,7},{24,8},{25... | collective-permute-start | bytes 1179656 | tf_op jit(solution)/shard_map/ppermute | solution.py:834
  337.0 26.3 %collective-permute-start.49 = (bf16[64,1536]{1,0:T(8,128)(2,1)S(1)}, bf16[64,1536]{1,0:T(8,128)(2,1)S(1)}, u32[]{:S(2)}, u32[]{:S(2)}) collective-permute-start(bf16[64,1536]{1,0:T(8,128)(2,1)S(1)} %get-tuple-element.344), channel_id=1, source_target_pairs={{0,4},{2,6},{4,0},{6,2},{8,12},{10,14},{12,8},{14,10},{1,5},{3,7},... | collective-permute-start | bytes 589832 | tf_op jit(solution)/shard_map/ppermute | solution.py:824
  337.4 26.0 %collective-permute-start.50 = (bf16[64,1536]{1,0:T(8,128)(2,1)S(1)}, bf16[64,1536]{1,0:T(8,128)(2,1)S(1)}, u32[]{:S(2)}, u32[]{:S(2)}) collective-permute-start(bf16[64,1536]{1,0:T(8,128)(2,1)S(1)} %get-tuple-element.345), channel_id=1, source_target_pairs={{0,8},{2,10},{4,12},{6,14},{8,0},{10,2},{12,4},{14,6},{1,9},{3,11}... | collective-permute-start | bytes 589832 | tf_op jit(solution)/shard_map/ppermute | solution.py:824
  339.0 24.3 %collective-permute-start.51 = (bf16[64,1536]{1,0:T(8,128)(2,1)S(1)}, bf16[64,1536]{1,0:T(8,128)(2,1)S(1)}, u32[]{:S(2)}, u32[]{:S(2)}) collective-permute-start(bf16[64,1536]{1,0:T(8,128)(2,1)S(1)} %get-tuple-element.346), channel_id=1, source_target_pairs={{0,12},{2,14},{4,8},{6,10},{8,4},{10,6},{12,0},{14,2},{1,13},{3,15... | collective-permute-start | bytes 589832 | tf_op jit(solution)/shard_map/ppermute | solution.py:824
  363.5 11.6 %collective-permute-start.52 = (bf16[2,64,1536]{2,1,0:T(8,128)(2,1)S(1)}, bf16[2,64,1536]{2,1,0:T(8,128)(2,1)S(1)}, u32[]{:S(2)}, u32[]{:S(2)}) collective-permute-start(bf16[2,64,1536]{2,1,0:T(8,128)(2,1)S(1)} %bitcast_select_fusion.3.refs_0_), channel_id=1, source_target_pairs={{0,1},{1,0},{2,3},{3,2},{4,5},{5,4},{6,7},{7,6},{8,9},{9,8},{10,11... | collective-permute-start | bytes 1179656 | tf_op jit(solution)/shard_map/ppermute | solution.py:830
  391.2 34.8 %collective-permute-start.57 = (bf16[2,64,1536]{2,1,0:T(8,128)(2,1)S(1)}, bf16[2,64,1536]{2,1,0:T(8,128)(2,1)S(1)}, u32[]{:S(2)}, u32[]{:S(2)}) collective-permute-start(bf16[2,64,1536]{2,1,0:T(8,128)(2,1)S(1)} %bitcast.463), channel_id=1, source_target_pairs={{0,1},{1,0},{2,3},{3,2},{4,5},{5,4},{6,7},{7,6},{8,9},{9,8},{10,11... | collective-permute-start | bytes 1179656 | tf_op jit(solution)/shard_map/ppermute | solution.py:830
  401.3 30.8 %collective-permute-start.58 = (bf16[2,192,1536]{2,1,0:T(8,128)(2,1)}, bf16[2,192,1536]{2,1,0:T(8,128)(2,1)}, u32[]{:S(2)}, u32[]{:S(2)}) collective-permute-start(bf16[2,192,1536]{2,1,0:T(8,128)(2,1)} %pad_maximum_fusion.2), channel_id=1, source_target_pairs={{0,4},{2,6},{4,0},{6,2},{8,12},{10,14},{12,8},{14,10},{1,5},{3,7},... | collective-permute-start | bytes 3538952 | tf_op jit(solution)/shard_map/ppermute | solution.py:824
  401.7 30.5 %collective-permute-start.59 = (bf16[2,192,1536]{2,1,0:T(8,128)(2,1)}, bf16[2,192,1536]{2,1,0:T(8,128)(2,1)}, u32[]{:S(2)}, u32[]{:S(2)}) collective-permute-start(bf16[2,192,1536]{2,1,0:T(8,128)(2,1)} %pad_maximum_fusion.3), channel_id=1, source_target_pairs={{0,8},{2,10},{4,12},{6,14},{8,0},{10,2},{12,4},{14,6},{1,9},{3,11}... | collective-permute-start | bytes 3538952 | tf_op jit(solution)/shard_map/ppermute | solution.py:824
  403.3 28.8 %collective-permute-start.60 = (bf16[4,64,1536]{2,1,0:T(8,128)(2,1)}, bf16[4,64,1536]{2,1,0:T(8,128)(2,1)}, u32[]{:S(2)}, u32[]{:S(2)}) collective-permute-start(bf16[4,64,1536]{2,1,0:T(8,128)(2,1)} %order_blocks.19.refs_0_), channel_id=1, source_target_pairs={{0,1},{1,0},{2,3},{3,2},{4,5},{5,4},{6,7},{7,6},{8,9},{9,8},{10,11... | collective-permute-start | bytes 2359304 | tf_op jit(solution)/shard_map/ppermute | solution.py:830
  433.6 18.2 %collective-permute-start.62 = (bf16[2,64,1536]{2,1,0:T(8,128)(2,1)S(1)}, bf16[2,64,1536]{2,1,0:T(8,128)(2,1)S(1)}, u32[]{:S(2)}, u32[]{:S(2)}) collective-permute-start(bf16[2,64,1536]{2,1,0:T(8,128)(2,1)S(1)} %bitcast.465), channel_id=1, source_target_pairs={{0,1},{1,0},{2,3},{3,2},{4,5},{5,4},{6,7},{7,6},{8,9},{9,8},{10,11... | collective-permute-start | bytes 1179656 | tf_op jit(solution)/shard_map/ppermute | solution.py:830
  436.8 16.2 %collective-permute-start.63 = (bf16[192,1536]{1,0:T(8,128)(2,1)S(1)}, bf16[192,1536]{1,0:T(8,128)(2,1)S(1)}, u32[]{:S(2)}, u32[]{:S(2)}) collective-permute-start(bf16[192,1536]{1,0:T(8,128)(2,1)S(1)} %fusion.3), channel_id=1, source_target_pairs={{0,8},{2,10},{4,12},{6,14},{8,0},{10,2},{12,4},{14,6},{1,9},{3,11}... | collective-permute-start | bytes 1769480 | tf_op jit(solution)/shard_map/ppermute | solution.py:824
  438.5 16.3 %collective-permute-start.64 = (bf16[192,1536]{1,0:T(8,128)(2,1)S(1)}, bf16[192,1536]{1,0:T(8,128)(2,1)S(1)}, u32[]{:S(2)}, u32[]{:S(2)}) collective-permute-start(bf16[192,1536]{1,0:T(8,128)(2,1)S(1)} %fusion.2), channel_id=1, source_target_pairs={{0,4},{2,6},{4,0},{6,2},{8,12},{10,14},{12,8},{14,10},{1,5},{3,7},... | collective-permute-start | bytes 1769480 | tf_op jit(solution)/shard_map/ppermute | solution.py:824
  446.3 36.0 %collective-permute-start.68 = (bf16[2,192,1152]{2,1,0:T(8,128)(2,1)}, bf16[2,192,1152]{2,1,0:T(8,128)(2,1)}, u32[]{:S(2)}, u32[]{:S(2)}) collective-permute-start(bf16[2,192,1152]{2,1,0:T(8,128)(2,1)} %dynamic-slice_bitcast_fusion.1), channel_id=1, source_target_pairs={{0,4},{2,6},{4,0},{6,2},{8,12},{10,14},{12,8},{14,10},{1,5},{3,7},... | collective-permute-start | bytes 2654216 | tf_op jit(solution)/shard_map/ppermute | solution.py:824
  447.6 34.7 %collective-permute-start.69 = (bf16[2,192,1152]{2,1,0:T(8,128)(2,1)}, bf16[2,192,1152]{2,1,0:T(8,128)(2,1)}, u32[]{:S(2)}, u32[]{:S(2)}) collective-permute-start(bf16[2,192,1152]{2,1,0:T(8,128)(2,1)} %dynamic-slice_bitcast_fusion), channel_id=1, source_target_pairs={{0,8},{2,10},{4,12},{6,14},{8,0},{10,2},{12,4},{14,6},{1,9},{3,11}... | collective-permute-start | bytes 2654216 | tf_op jit(solution)/shard_map/ppermute | solution.py:824
  458.3 19.8 %collective-permute-start.65 = (bf16[64,1536]{1,0:T(8,128)(2,1)}, bf16[64,1536]{1,0:T(8,128)(2,1)}, u32[]{:S(2)}, u32[]{:S(2)}) collective-permute-start(bf16[64,1536]{1,0:T(8,128)(2,1)} %get-tuple-element.500), channel_id=1, source_target_pairs={{0,4},{2,6},{4,0},{6,2},{8,12},{10,14},{12,8},{14,10},{1,5},{3,7},... | collective-permute-start | bytes 589832 | tf_op jit(solution)/shard_map/ppermute | solution.py:824
  459.9 18.1 %collective-permute-start.66 = (bf16[64,1536]{1,0:T(8,128)(2,1)}, bf16[64,1536]{1,0:T(8,128)(2,1)}, u32[]{:S(2)}, u32[]{:S(2)}) collective-permute-start(bf16[64,1536]{1,0:T(8,128)(2,1)} %get-tuple-element.499), channel_id=1, source_target_pairs={{0,8},{2,10},{4,12},{6,14},{8,0},{10,2},{12,4},{14,6},{1,9},{3,11}... | collective-permute-start | bytes 589832 | tf_op jit(solution)/shard_map/ppermute | solution.py:824
  464.1 18.2 %collective-permute-start.67 = (bf16[64,1536]{1,0:T(8,128)(2,1)}, bf16[64,1536]{1,0:T(8,128)(2,1)}, u32[]{:S(2)}, u32[]{:S(2)}) collective-permute-start(bf16[64,1536]{1,0:T(8,128)(2,1)} %get-tuple-element.498), channel_id=1, source_target_pairs={{0,12},{2,14},{4,8},{6,10},{8,4},{10,6},{12,0},{14,2},{1,13},{3,15... | collective-permute-start | bytes 589832 | tf_op jit(solution)/shard_map/ppermute | solution.py:824
  486.6 11.5 %collective-permute-start.73 = (bf16[192,1152]{1,0:T(8,128)(2,1)S(1)}, bf16[192,1152]{1,0:T(8,128)(2,1)S(1)}, u32[]{:S(2)}, u32[]{:S(2)}) collective-permute-start(bf16[192,1152]{1,0:T(8,128)(2,1)S(1)} %fusion.6), channel_id=1, source_target_pairs={{0,4},{2,6},{4,0},{6,2},{8,12},{10,14},{12,8},{14,10},{1,5},{3,7},... | collective-permute-start | bytes 1327112 | tf_op jit(solution)/shard_map/ppermute | solution.py:824
  488.4 30.3 %collective-permute-start.71 = (bf16[4,64,1536]{2,1,0:T(8,128)(2,1)S(1)}, bf16[4,64,1536]{2,1,0:T(8,128)(2,1)}, u32[]{:S(2)}, u32[]{:S(2)}) collective-permute-start(bf16[4,64,1536]{2,1,0:T(8,128)(2,1)S(1)} %order_blocks.24.refs_0_), channel_id=1, source_target_pairs={{0,1},{1,0},{2,3},{3,2},{4,5},{5,4},{6,7},{7,6},{8,9},{9,8},{10,11... | collective-permute-start | bytes 2359304 | tf_op jit(solution)/shard_map/ppermute | solution.py:830
  (162 other events, 1359.9 us)

commit v3 on v2

--- a/solution.py
+++ b/solution.py
@@ -132,28 +132,40 @@
     return jnp.broadcast_to(row, (CHUNK, LANES)).T
 
 
-def deal(part, parts, first, count, total, own_ref, send_ref):
+def deal(part, parts, first, count, total, own_ref, send_ref, sems):
+    def own_copy(c):
+        rows = total.at[pl.ds(pl.multiple_of(c * CHUNK, CHUNK), CHUNK), :]
+        return pltpu.make_async_copy(rows, own_ref.at[(first + c) // parts], sems.at[c])
+
     def one(c, _):
         index = first + c
         distance = (index % parts) ^ part
-        rows = total[pl.ds(pl.multiple_of(c * CHUNK, CHUNK), CHUNK), :]
 
         @pl.when(distance == 0)
         def _():
-            own_ref[index // parts] = rows
+            own_copy(c).start()
 
         @pl.when(distance != 0)
         def _():
+            rows = total[pl.ds(pl.multiple_of(c * CHUNK, CHUNK), CHUNK), :]
             send_ref[jnp.maximum(distance - 1, 0), index // parts] = rows.astype(send_ref.dtype)
 
         return 0
 
+    def end(c, _):
+        @pl.when(((first + c) % parts) ^ part == 0)
+        def _():
+            own_copy(c).wait()
+
+        return 0
+
     lax.fori_loop(0, count, one, 0)
+    lax.fori_loop(0, count, end, 0)
 
 
 def forward_kernel(keep, width, parts, per_step, part_ref, h_ref, w1_ref, wg_ref, norm_ref, taps_ref, heads_ref, inner_ref, s0_ref, tail0_ref, *rest):
     if keep:
-        wo_ref, dn_ref, own_ref, send_ref, sums_ref, st_ref, tail_ref, xn_ref, vbd_ref, z_ref, y_ref, sin_ref, pad, gg, total = rest
+        wo_ref, dn_ref, own_ref, send_ref, sums_ref, st_ref, tail_ref, xn_ref, vbd_ref, z_ref, y_ref, sin_ref, pad, gg, total, sems = rest
     else:
         g_ref, sums_ref, st_ref, tail_ref, xn_ref, vbd_ref, z_ref, pad = rest
     mixed = width + MAPS
@@ -233,10 +245,10 @@
         total[...] = lax.dot_general(
             gg[...], wo_ref[...], (((1,), (1,)), ((), ())), preferred_element_type=f32
         )
-        deal(part_ref[0], parts, step * per_step, per_step, total, own_ref, send_ref)
-
-
-def out_kernel(parts, per_step, part_ref, g_ref, q_ref, inner_ref, wo_ref, own_ref, send_ref, n, total):
+        deal(part_ref[0], parts, step * per_step, per_step, total, own_ref, send_ref, sems)
+
+
+def out_kernel(parts, per_step, part_ref, g_ref, q_ref, inner_ref, wo_ref, own_ref, send_ref, n, total, sems):
     def chunk(c, _):
         here = pl.ds(pl.multiple_of(c * CHUNK, CHUNK), CHUNK)
         q = as_column(q_ref[c])
@@ -247,7 +259,7 @@
 
     lax.fori_loop(0, per_step, chunk, 0)
     total[...] = lax.dot_general(n[...], wo_ref[...], (((1,), (1,)), ((), ())), preferred_element_type=f32)
-    deal(part_ref[0], parts, pl.program_id(0) * per_step, per_step, total, own_ref, send_ref)
+    deal(part_ref[0], parts, pl.program_id(0) * per_step, per_step, total, own_ref, send_ref, sems)
 
 
 def out_call(place, g, q, weights, inner):
@@ -271,8 +283,12 @@
                 once(inner.shape),
                 once(wo.shape),
             ],
-            out_specs=[once(shape) for shape in shapes],
-            scratch_shapes=[pltpu.VMEM((count, width), bf16), pltpu.VMEM((count, depth), f32)],
+            out_specs=[pl.BlockSpec(memory_space=pl.ANY), once(shapes[1])],
+            scratch_shapes=[
+                pltpu.VMEM((count, width), bf16),
+                pltpu.VMEM((count, depth), f32),
+                pltpu.SemaphoreType.DMA((per_step,)),
+            ],
         ),
         out_shape=[jax.ShapeDtypeStruct(shape, f32) for shape in shapes],
         compiler_params=kernel_params(steps, 8),
@@ -316,7 +332,7 @@
     if keep:
         shapes = [((blocks, CHUNK, depth), f32), ((place.parts - 1, blocks, CHUNK, depth), bf16)]
         out_shape = [jax.ShapeDtypeStruct(*item) for item in shapes]
-        out_specs = [once(shape) for shape, _ in shapes]
+        out_specs = [pl.BlockSpec(memory_space=pl.ANY), once(shapes[1][0])]
     else:
         out_shape = [jax.ShapeDtypeStruct((tokens, width), f32)]
         out_specs = [rows(width)]
@@ -356,7 +372,11 @@
         scratch = [pltpu.VMEM((count, shape[1]), kind) for shape, kind in held]
     scratch.append(pltpu.VMEM((CHUNK + 8, mixed), f32))
     if keep:
-        scratch += [pltpu.VMEM((count, width), bf16), pltpu.VMEM((count, depth), f32)]
+        scratch += [
+            pltpu.VMEM((count, width), bf16),
+            pltpu.VMEM((count, depth), f32),
+            pltpu.SemaphoreType.DMA((per_step,)),
+        ]
     return pl.pallas_call(
         functools.partial(forward_kernel, keep, width, place.parts, per_step),
         grid_spec=pltpu.PrefetchScalarGridSpec(
@@ -506,6 +526,7 @@
     headg_ref,
     skipg_ref,
     back_all,
+    sems,
 ):
     mixed = width + MAPS
     rows = head_rows(width)
@@ -676,7 +697,7 @@
         columns = jnp.concatenate([by_head, skips, jnp.zeros((CHUNK - 3 * rows, LANES), f32)], axis=0)
         tapg_ref[HEAD_ROW : HEAD_ROW + 1, 0:LANES] = columns.T[0:1]
 
-    deal(part_ref[0], parts, step * per_step, per_step, total, own_ref, send_ref)
+    deal(part_ref[0], parts, step * per_step, per_step, total, own_ref, send_ref, sems)
 
 
 def backward_call(place, exact, dy, dz, vbd, before, states, weights, small, g0, du0):
@@ -719,7 +740,7 @@
                 once(du0.shape),
             ],
             out_specs=[
-                once((blocks, CHUNK, depth)),
+                pl.BlockSpec(memory_space=pl.ANY),
                 once((place.parts - 1, blocks, CHUNK, depth)),
                 rows(vbd.shape[1]),
             ]
@@ -737,6 +758,7 @@
                 pltpu.VMEM((2 * head_rows(width), LANES), f32),
                 pltpu.VMEM((8, width), f32),
                 pltpu.VMEM((STATE, width), f32),
+                pltpu.SemaphoreType.DMA((per_step,)),
             ],
         ),
         out_shape=[
@@ -1467,9 +1489,13 @@
     collected.launch()
     spread.came, collected.next = tie(spread.came, collected.next)
     collected.land()
-    collected.finish()
+    h0 = spread.result()
+    while collected.masks[0]:
+        collected.prepare()
+        collected.launch()
+        h0, collected.next = tie(h0, collected.next)
+        collected.land()
     weights = tuple(collected.result([mixed + LANES, width]))
-    h0 = spread.result()
     taps = jnp.concatenate(
         [
             jnp.concatenate([share(conv_value[0], width), conv_bc[0]], axis=1),

time: 540 us -> 532 us (0.985)
    unnamed x262 -> x274, local copies, waits for them, and re-layouts: 37.5 us -> 34.5 us
  transfers between devices with their start and end apart: 80 -> 80, of which waited for: 36 -> 39; matrix products, arithmetic and copies ran while one was open for 14% -> 14% of each run, Pallas kernels for 29% -> 29%
where the time goes in v3:
time: 532 us; the launch traced here: 522 us
  Pallas kernels  170 us (32%)
  waiting for transfers between devices  156 us (29%)
  starting transfers between devices  77.8 us (15%)
  local copies, waits for them, and re-layouts  64.5 us (12%)
  other arithmetic  33.5 us (6%)
  matrix products  17 us (3%)
    ppermute x54, waiting for transfers between devices, swap_part(): lax.ppermute(block, 'context', [(i, i ^ mask) for i in range(self.context)])  98.7 us
    pallas_call x4, Pallas kernels, backward_call(): pl.pallas_call(functools.partial(backward_kernel, exact, width, place.par...  71.3 us
    pallas_call x4, Pallas kernels, forward_call(): pl.pallas_call(functools.partial(forward_kernel, keep, width, place.parts...  51 us
    ppermute x22, waiting for transfers between devices, swap_tensor(): lax.ppermute(block, 'tensor', [(i, i ^ mask) for i in range(self.tensors)])  48.4 us
    ppermute x54, starting transfers between devices, swap_part(): lax.ppermute(block, 'context', [(i, i ^ mask) for i in range(self.context)])  39.1 us
    unnamed x274, local copies, waits for them, and re-layouts  34.5 us
    ppermute x22, starting transfers between devices, swap_tensor(): lax.ppermute(block, 'tensor', [(i, i ^ mask) for i in range(self.tensors)])  28.5 us
    squeeze x19, local copies, waits for them, and re-layouts, pick(): return lax.dynamic_index_in_dim(array, index, axis, False)  15.4 us
  transfers between devices with their start and end apart: 80, of which 39 were waited for; matrix products, arithmetic and copies ran while one was open for 14% of the time, Pallas kernels for 29%

profile of v3, /device:TPU:0, one launch (start us, length us, event | category | flops | bytes accessed | tf_op | source)
XLA Modules:
  0.0 522.3 jit_solution(12473315449121171732)
XLA Ops:
  4.9 3.6 collective-permute-start.2
  23.0 11.3 %collective-permute-done.4.refs_1_ = bf16[1,192,1920]{2,1,0:T(8,128)(2,1)S(1)} collective-permute-done((bf16[1,192,1920]{2,1,0:T(8,128)(2,1)S(1)}, bf16[1,192,1920]{2,1,0:T(8,128)(2,1)S(1)}, u32[]{:S(2)}, u32[]{:S(2)}) %collective-permute-start.4) | collective-permute-done | bytes 737312 | tf_op jit(solution)/shard_map/ppermute | solution.py:846
  42.4 2.2 broadcast_select_fusion.1
  44.8 29.6 %collective-permute-done.8.refs_2_ = bf16[2,192,1920]{2,1,0:T(8,128)(2,1)S(1)} collective-permute-done((bf16[2,192,1920]{2,1,0:T(8,128)(2,1)S(1)}, bf16[2,192,1920]{2,1,0:T(8,128)(2,1)S(1)}, u32[]{:S(2)}, u32[]{:S(2)}) %collective-permute-start.8) | collective-permute-done | bytes 1474592 | tf_op jit(solution)/shard_map/ppermute | solution.py:846
  79.6 11.4 %section_forward.4 = (f32[512,768]{1,0:T(8,128)S(1)}, f32[2,4,1,128]{3,2,1,0:T(1,128)S(1)}, f32[128,768]{1,0:T(8,128)S(1)}, f32[8,1024]{1,0:T(8,128)S(1)}) custom-call(s32[1]{0:T(128)} %bitcast.1.part_ref.index_ref, bf16[512,1536]{1,0:T(8,128)(2,1)S(1)} %bitcast.405, bf16[1536,1152]{1,0:T(8,128)(2,1)S(1)} %bitcast.446, bf16[1536,768]{1,0:T(8,128)(2,1)S(1)} %bitcast.454, ...), custom_call_target="tpu_custom_call" | custom-call | flops 15728640000 | bytes 12582912 | tf_op jit(solution)/shard_map/section_forward/pallas_call | solution.py:380
  95.9 12.1 %section_forward.5 = (f32[512,768]{1,0:T(8,128)S(1)}, f32[2,4,1,128]{3,2,1,0:T(1,128)S(1)}, f32[128,768]{1,0:T(8,128)}, f32[8,1024]{1,0:T(8,128)}) custom-call(s32[1]{0:T(128)} %bitcast.1.part_ref.index_ref, bf16[512,1536]{1,0:T(8,128)(2,1)S(1)} %bitcast.402, bf16[1536,1152]{1,0:T(8,128)(2,1)S(1)} %bitcast.447, bf16[1536,768]{1,0:T(8,128)(2,1)S(1)} %bitcast.455, ...), custom_call_target="tpu_custom_call" | custom-call | flops 15728640000 | bytes 12582912 | tf_op jit(solution)/shard_map/section_forward/pallas_call | solution.py:380
  111.3 3.4 out_forward.2
  124.1 3.5 out_forward.3
  128.9 9.0 %collective-permute-done.24 = bf16[128,1536]{1,0:T(8,128)(2,1)S(1)} collective-permute-done((bf16[128,1536]{1,0:T(8,128)(2,1)S(1)}, bf16[128,1536]{1,0:T(8,128)(2,1)S(1)}, u32[]{:S(2)}, u32[]{:S(2)}) %collective-permute-start.24) | collective-permute-done | bytes 393248 | tf_op jit(solution)/shard_map/ppermute | solution.py:846
  142.1 4.6 collective-permute-start.27
  148.8 2.2 broadcast_select_fusion
  151.2 2.6 copy-done.18
  156.6 7.4 %collective-permute-done.21 = f16[2,64,1536]{2,1,0:T(8,128)(2,1)S(1)} collective-permute-done((f16[2,64,1536]{2,1,0:T(8,128)(2,1)S(1)}, f16[2,64,1536]{2,1,0:T(8,128)(2,1)S(1)}, u32[]{:S(2)}, u32[]{:S(2)}) %collective-permute-start.21) | collective-permute-done | bytes 393248 | tf_op jit(solution)/shard_map/ppermute | solution.py:852
  165.4 2.5 collective-permute-start.28
  167.9 3.0 collective-permute-start.29
  171.0 6.5 %collective-permute-done.28.refs_1_ = bf16[2,64,1536]{2,1,0:T(8,128)(2,1)S(1)} collective-permute-done((bf16[2,64,1536]{2,1,0:T(8,128)(2,1)S(1)}, bf16[2,64,1536]{2,1,0:T(8,128)(2,1)S(1)}, u32[]{:S(2)}, u32[]{:S(2)}) %collective-permute-start.28) | collective-permute-done | bytes 393248 | tf_op jit(solution)/shard_map/ppermute | solution.py:852
  177.5 7.1 %collective-permute-done.29 = bf16[2,64,1536]{2,1,0:T(8,128)(2,1)S(1)} collective-permute-done((bf16[2,64,1536]{2,1,0:T(8,128)(2,1)S(1)}, bf16[2,64,1536]{2,1,0:T(8,128)(2,1)S(1)}, u32[]{:S(2)}, u32[]{:S(2)}) %collective-permute-start.29) | collective-permute-done | bytes 393248 | tf_op jit(solution)/shard_map/ppermute | solution.py:856
  184.9 2.3 collective-permute-done.30.refs_1_
  187.4 3.7 collective-permute-start.31
  191.1 13.4 %section_forward.6 = (f32[2,128,1536]{2,1,0:T(8,128)S(1)}, bf16[1,2,128,1536]{3,2,1,0:T(8,128)(2,1)S(1)}, f32[2,4,1,128]{3,2,1,0:T(1,128)S(1)}, f32[128,768]{1,0...) custom-call(s32[1]{0:T(128)} %bitcast.1.part_ref.index_ref, ...), custom_call_target="tpu_custom_call" | custom-call | flops 15728640000 | bytes 12582912 | tf_op jit(solution)/shard_map/section_forward/pallas_call | solution.py:380
  207.3 14.1 %section_forward.7 = (f32[2,128,1536]{2,1,0:T(8,128)S(1)}, bf16[1,2,128,1536]{3,2,1,0:T(8,128)(2,1)S(1)}, f32[2,4,1,128]{3,2,1,0:T(1,128)S(1)}, f32[128,768]{1,0...) custom-call(s32[1]{0:T(128)} %bitcast.1.part_ref.index_ref, ...), custom_call_target="tpu_custom_call" | custom-call | flops 15728640000 | bytes 12582912 | tf_op jit(solution)/shard_map/section_forward/pallas_call | solution.py:380
  231.9 17.0 %section_backward.4 = (f32[2,128,1536]{2,1,0:T(8,128)S(1)}, bf16[1,2,128,1536]{3,2,1,0:T(8,128)(2,1)S(1)}, bf16[512,1152]{1,0:T(8,128)(2,1)}, f32[128,768]{1,0:T...) custom-call(s32[1]{0:T(128)} %bitcast.1.part_ref.index_ref, f32[512,768]{1,0:T(8,128)S(1)} %get-tuple-element.309.dy_ref, ...), custom_call_target="tpu_custom_call" | custom-call | flops 23592960000 | bytes 12582912 | tf_op jit(solution)/shard_map/section_backward/pallas_call | solution.py:723
  251.6 2.3 collective-permute-done.39.refs_0_
  257.2 8.4 %collective-permute-done.40.refs_0_ = bf16[2,64,1536]{2,1,0:T(8,128)(2,1)S(1)} collective-permute-done((bf16[2,64,1536]{2,1,0:T(8,128)(2,1)S(1)}, bf16[2,64,1536]{2,1,0:T(8,128)(2,1)S(1)}, u32[]{:S(2)}, u32[]{:S(2)}) %collective-permute-start.40) | collective-permute-done | bytes 393248 | tf_op jit(solution)/shard_map/ppermute | solution.py:852
  265.6 2.2 finish_gradient.4
  269.1 17.2 %section_backward.5 = (f32[2,128,1536]{2,1,0:T(8,128)S(1)}, bf16[1,2,128,1536]{3,2,1,0:T(8,128)(2,1)}, bf16[512,1152]{1,0:T(8,128)(2,1)}, f32[128,768]{1,0:T(8,1...) custom-call(s32[1]{0:T(128)} %bitcast.1.part_ref.index_ref, f32[512,768]{1,0:T(8,128)S(1)} %get-tuple-element.327.dy_ref, ...), custom_call_target="tpu_custom_call" | custom-call | flops 23592960000 | bytes 12582912 | tf_op jit(solution)/shard_map/section_backward/pallas_call | solution.py:723
  287.4 2.3 collective-permute-done.41
  298.8 5.8 %collective-permute-done.44.refs_1_ = bf16[2,64,1536]{2,1,0:T(8,128)(2,1)} collective-permute-done((bf16[2,64,1536]{2,1,0:T(8,128)(2,1)}, bf16[2,64,1536]{2,1,0:T(8,128)(2,1)}, u32[]{:S(2)}, u32[]{:S(2)}) %collective-permute-start.44) | collective-permute-done | bytes 393248 | tf_op jit(solution)/shard_map/ppermute | solution.py:852
  304.6 8.0 %collective-permute-done.43.refs_0_ = bf16[2,64,1536]{2,1,0:T(8,128)(2,1)} collective-permute-done((bf16[2,64,1536]{2,1,0:T(8,128)(2,1)}, bf16[2,64,1536]{2,1,0:T(8,128)(2,1)}, u32[]{:S(2)}, u32[]{:S(2)}) %collective-permute-start.43) | collective-permute-done | bytes 393248 | tf_op jit(solution)/shard_map/ppermute | solution.py:852
  316.6 2.2 norm_backward.2
  320.2 3.1 finish_gradient.5
  325.0 3.6 fusion.64
  336.0 18.1 %section_backward.6 = (f32[2,128,1536]{2,1,0:T(8,128)S(1)}, bf16[1,2,128,1536]{3,2,1,0:T(8,128)(2,1)S(1)}, bf16[512,1152]{1,0:T(8,128)(2,1)S(1)}, f32[128,768]{1...) custom-call(s32[1]{0:T(128)} %bitcast.1.part_ref.index_ref, f32[512,768]{1,0:T(8,128)S(1)} %get-tuple-element.357.dy_ref, ...), custom_call_target="tpu_custom_call" | custom-call | flops 23592960000 | bytes 12582912 | tf_op jit(solution)/shard_map/section_backward/pallas_call | solution.py:723
  359.1 7.5 %collective-permute-done.52.refs_1_ = bf16[2,64,1536]{2,1,0:T(8,128)(2,1)S(1)} collective-permute-done((bf16[2,64,1536]{2,1,0:T(8,128)(2,1)S(1)}, bf16[2,64,1536]{2,1,0:T(8,128)(2,1)S(1)}, u32[]{:S(2)}, u32[]{:S(2)}) %collective-permute-start.52) | collective-permute-done | bytes 393248 | tf_op jit(solution)/shard_map/ppermute | solution.py:852
  366.9 2.3 collective-permute-done.54.refs_1_
  369.4 2.2 norm_backward.3
  376.5 3.0 fusion.65
  379.6 3.1 add.530
  396.3 19.0 %section_backward.7 = (f32[2,128,1536]{2,1,0:T(8,128)S(1)}, bf16[1,2,128,1536]{3,2,1,0:T(8,128)(2,1)}, bf16[512,1152]{1,0:T(8,128)(2,1)S(1)}, f32[128,768]{1,0:T...) custom-call(s32[1]{0:T(128)} %bitcast.1.part_ref.index_ref, f32[512,768]{1,0:T(8,128)S(1)} %get-tuple-element.388.dy_ref, ...), custom_call_target="tpu_custom_call" | custom-call | flops 23592960000 | bytes 12582912 | tf_op jit(solution)/shard_map/section_backward/pallas_call | solution.py:723
  431.7 2.3 fusion.67
  434.0 2.4 fusion
  460.0 9.5 %collective-permute-done.65.refs_1_ = bf16[64,1536]{1,0:T(8,128)(2,1)} collective-permute-done((bf16[64,1536]{1,0:T(8,128)(2,1)}, bf16[64,1536]{1,0:T(8,128)(2,1)}, u32[]{:S(2)}, u32[]{:S(2)}) %collective-permute-start.65) | collective-permute-done | bytes 196640 | tf_op jit(solution)/shard_map/ppermute | solution.py:846
  469.5 4.3 collective-permute-done.67.refs_3_
  481.4 7.5 %collective-permute-done.72.refs_2_ = bf16[192,1152]{1,0:T(8,128)(2,1)S(1)} collective-permute-done((bf16[192,1152]{1,0:T(8,128)(2,1)S(1)}, bf16[192,1152]{1,0:T(8,128)(2,1)S(1)}, u32[]{:S(2)}, u32[]{:S(2)}) %collective-permute-start.72) | collective-permute-done | bytes 442400 | tf_op jit(solution)/shard_map/ppermute | solution.py:846
  492.2 2.5 order_blocks.22
  497.2 2.6 collective-permute-done.75
  511.5 2.1 convert.24
  518.5 2.9 collective-permute-done.79
  (570 shorter events, 200.4 us)
Async XLA Ops:
  9.1 25.2 %collective-permute-start.4 = (bf16[1,192,1920]{2,1,0:T(8,128)(2,1)S(1)}, bf16[1,192,1920]{2,1,0:T(8,128)(2,1)S(1)}, u32[]{:S(2)}, u32[]{:S(2)}) collective-permute-start(bf16[1,192,1920]{2,1,0:T(8,128)(2,1)S(1)} %get-tuple-element.523.refs_0_), channel_id=1, source_target_pairs={{0,4},{2,6},{4,0},{6,2},{8,12},{10,14},{12,8},{14,10},{1,5},{3,7},... | collective-permute-start | bytes 2211848 | tf_op jit(solution)/shard_map/ppermute | solution.py:846
  14.3 61.7 %collective-permute-start.10 = (bf16[1,192,768]{2,1,0:T(8,128)(2,1)}, bf16[1,192,768]{2,1,0:T(8,128)(2,1)}, u32[]{:S(2)}, u32[]{:S(2)}) collective-permute-start(bf16[1,192,768]{2,1,0:T(8,128)(2,1)} %get-tuple-element.513), channel_id=1, source_target_pairs={{0,2},{2,0},{4,6},{6,4},{8,10},{10,8},{12,14},{14,12},{1,3},{3,1},... | collective-permute-start | bytes 884744 | tf_op jit(solution)/shard_map/ppermute | solution.py:846
  14.3 21.1 %collective-permute-start.6 = (bf16[1,192,1920]{2,1,0:T(8,128)(2,1)S(1)}, bf16[1,192,1920]{2,1,0:T(8,128)(2,1)S(1)}, u32[]{:S(2)}, u32[]{:S(2)}) collective-permute-start(bf16[1,192,1920]{2,1,0:T(8,128)(2,1)S(1)} %collective-permute-done.5.refs_3_), channel_id=1, source_target_pairs={{0,8},{2,10},{4,12},{6,14},{8,0},{10,2},{12,4},{14,6},{1,9},{3,11}... | collective-permute-start | bytes 2211848 | tf_op jit(solution)/shard_map/ppermute | solution.py:846
  19.8 15.5 %collective-permute-start.3 = (bf16[3,64,1536]{2,1,0:T(8,128)(2,1)}, bf16[3,64,1536]{2,1,0:T(8,128)(2,1)}, u32[]{:S(2)}, u32[]{:S(2)}) collective-permute-start(bf16[3,64,1536]{2,1,0:T(8,128)(2,1)} %pad_maximum_fusion.6), channel_id=1, source_target_pairs={{0,1},{1,0},{2,3},{3,2},{4,5},{5,4},{6,7},{7,6},{8,9},{9,8},{10,11... | collective-permute-start | bytes 1769480 | tf_op jit(solution)/shard_map/ppermute | solution.py:852
  39.6 34.8 %collective-permute-start.8 = (bf16[2,192,1920]{2,1,0:T(8,128)(2,1)S(1)}, bf16[2,192,1920]{2,1,0:T(8,128)(2,1)S(1)}, u32[]{:S(2)}, u32[]{:S(2)}) collective-permute-start(bf16[2,192,1920]{2,1,0:T(8,128)(2,1)S(1)} %pad_maximum_fusion), channel_id=1, source_target_pairs={{0,8},{2,10},{4,12},{6,14},{8,0},{10,2},{12,4},{14,6},{1,9},{3,11}... | collective-permute-start | bytes 4423688 | tf_op jit(solution)/shard_map/ppermute | solution.py:846
  41.5 34.5 %collective-permute-start.9 = (bf16[2,192,1920]{2,1,0:T(8,128)(2,1)S(1)}, bf16[2,192,1920]{2,1,0:T(8,128)(2,1)S(1)}, u32[]{:S(2)}, u32[]{:S(2)}) collective-permute-start(bf16[2,192,1920]{2,1,0:T(8,128)(2,1)S(1)} %pad_maximum_fusion.1), channel_id=1, source_target_pairs={{0,4},{2,6},{4,0},{6,2},{8,12},{10,14},{12,8},{14,10},{1,5},{3,7},... | collective-permute-start | bytes 4423688 | tf_op jit(solution)/shard_map/ppermute | solution.py:846
  76.0 15.0 %collective-permute-start.11 = (bf16[1,192,768]{2,1,0:T(8,128)(2,1)S(1)}, bf16[1,192,768]{2,1,0:T(8,128)(2,1)S(1)}, u32[]{:S(2)}, u32[]{:S(2)}) collective-permute-start(bf16[1,192,768]{2,1,0:T(8,128)(2,1)S(1)} %get-tuple-element.243.refs_0_), channel_id=1, source_target_pairs={{0,4},{2,6},{4,0},{6,2},{8,12},{10,14},{12,8},{14,10},{1,5},{3,7},... | collective-permute-start | bytes 884744 | tf_op jit(solution)/shard_map/ppermute | solution.py:846
  76.3 14.7 %collective-permute-start.12 = (bf16[1,192,768]{2,1,0:T(8,128)(2,1)}, bf16[1,192,768]{2,1,0:T(8,128)(2,1)S(1)}, u32[]{:S(2)}, u32[]{:S(2)}) collective-permute-start(bf16[1,192,768]{2,1,0:T(8,128)(2,1)} %collective-permute-done.10.refs_3_), channel_id=1, source_target_pairs={{0,8},{2,10},{4,12},{6,14},{8,0},{10,2},{12,4},{14,6},{1,9},{3,11}... | collective-permute-start | bytes 884744 | tf_op jit(solution)/shard_map/ppermute | solution.py:846
  92.3 15.8 %collective-permute-start.14 = (f32[4,128]{1,0:T(4,128)S(1)}, f32[4,128]{1,0:T(4,128)S(1)}, u32[]{:S(2)}, u32[]{:S(2)}) collective-permute-start(f32[4,128]{1,0:T(4,128)S(1)} %fusion.52), channel_id=1, source_target_pairs={{0,1},{1,0},{2,3},{3,2},{4,5},{5,4},{6,7},{7,6},{8,9},{9,8},{10,11... | collective-permute-start | bytes 6152 | tf_op jit(solution)/shard_map/ppermute | solution.py:852
  93.9 15.4 %collective-permute-start.15 = (bf16[2,192,768]{2,1,0:T(8,128)(2,1)S(1)}, bf16[2,192,768]{2,1,0:T(8,128)(2,1)S(1)}, u32[]{:S(2)}, u32[]{:S(2)}) collective-permute-start(bf16[2,192,768]{2,1,0:T(8,128)(2,1)S(1)} %pad_maximum_fusion.7), channel_id=1, source_target_pairs={{0,8},{2,10},{4,12},{6,14},{8,0},{10,2},{12,4},{14,6},{1,9},{3,11}... | collective-permute-start | bytes 1769480 | tf_op jit(solution)/shard_map/ppermute | solution.py:846
  94.2 15.2 %collective-permute-start.16 = (bf16[2,192,768]{2,1,0:T(8,128)(2,1)S(1)}, bf16[2,192,768]{2,1,0:T(8,128)(2,1)S(1)}, u32[]{:S(2)}, u32[]{:S(2)}) collective-permute-start(bf16[2,192,768]{2,1,0:T(8,128)(2,1)S(1)} %pad_maximum_fusion.8), channel_id=1, source_target_pairs={{0,4},{2,6},{4,0},{6,2},{8,12},{10,14},{12,8},{14,10},{1,5},{3,7},... | collective-permute-start | bytes 1769480 | tf_op jit(solution)/shard_map/ppermute | solution.py:846
  116.9 12.0 %collective-permute-start.23 = (bf16[128,1536]{1,0:T(8,128)(2,1)S(1)}, bf16[128,1536]{1,0:T(8,128)(2,1)S(1)}, u32[]{:S(2)}, u32[]{:S(2)}) collective-permute-start(bf16[128,1536]{1,0:T(8,128)(2,1)S(1)} %get-tuple-element.492), channel_id=1, source_target_pairs={{0,4},{2,6},{4,0},{6,2},{8,12},{10,14},{12,8},{14,10},{1,5},{3,7},... | collective-permute-start | bytes 1179656 | tf_op jit(solution)/shard_map/ppermute | solution.py:846
  118.7 19.3 %collective-permute-start.24 = (bf16[128,1536]{1,0:T(8,128)(2,1)S(1)}, bf16[128,1536]{1,0:T(8,128)(2,1)S(1)}, u32[]{:S(2)}, u32[]{:S(2)}) collective-permute-start(bf16[128,1536]{1,0:T(8,128)(2,1)S(1)} %get-tuple-element.491), channel_id=1, source_target_pairs={{0,8},{2,10},{4,12},{6,14},{8,0},{10,2},{12,4},{14,6},{1,9},{3,11}... | collective-permute-start | bytes 1179656 | tf_op jit(solution)/shard_map/ppermute | solution.py:846
  119.2 18.8 %collective-permute-start.25 = (bf16[128,1536]{1,0:T(8,128)(2,1)S(1)}, bf16[128,1536]{1,0:T(8,128)(2,1)S(1)}, u32[]{:S(2)}, u32[]{:S(2)}) collective-permute-start(bf16[128,1536]{1,0:T(8,128)(2,1)S(1)} %get-tuple-element.490), channel_id=1, source_target_pairs={{0,12},{2,14},{4,8},{6,10},{8,4},{10,6},{12,0},{14,2},{1,13},{3,15... | collective-permute-start | bytes 1179656 | tf_op jit(solution)/shard_map/ppermute | solution.py:846
  122.2 15.8 %collective-permute-start.22 = (f16[2,64,1536]{2,1,0:T(8,128)(2,1)S(1)}, f16[2,64,1536]{2,1,0:T(8,128)(2,1)S(1)}, u32[]{:S(2)}, u32[]{:S(2)}) collective-permute-start(f16[2,64,1536]{2,1,0:T(8,128)(2,1)S(1)} %fusion.26), channel_id=1, source_target_pairs={{0,1},{1,0},{2,3},{3,2},{4,5},{5,4},{6,7},{7,6},{8,9},{9,8},{10,11... | collective-permute-start | bytes 1179656 | tf_op jit(solution)/shard_map/ppermute | solution.py:852
  128.8 18.0 %collective-permute-start.20 = (f32[2,128,1536]{2,1,0:T(8,128)}, f32[2,128,1536]{2,1,0:T(8,128)}, u32[]{:S(2)}, u32[]{:S(2)}) collective-permute-start(f32[2,128,1536]{2,1,0:T(8,128)} %bitcast.68), channel_id=1, source_target_pairs={{0,2},{2,0},{4,6},{6,4},{8,10},{10,8},{12,14},{14,12},{1,3},{3,1},... | collective-permute-start | bytes 4718600 | tf_op jit(solution)/shard_map/ppermute | solution.py:846
  142.1 23.2 %collective-permute-start.27 = (bf16[2,64,1536]{2,1,0:T(8,128)(2,1)S(1)}, bf16[2,64,1536]{2,1,0:T(8,128)(2,1)S(1)}, u32[]{:S(2)}, u32[]{:S(2)}) collective-permute-start(bf16[2,64,1536]{2,1,0:T(8,128)(2,1)S(1)} %fusion.11), channel_id=1, source_target_pairs={{0,17},{1,16},{2,19},{3,18},{4,21},{5,20},{6,23},{7,22},{8,25},{9,... | collective-permute-start | bytes 1179656 | tf_op jit(solution)/shard_map/ppermute | solution.py:856
  148.1 15.9 %collective-permute-start.21 = (f16[2,64,1536]{2,1,0:T(8,128)(2,1)S(1)}, f16[2,64,1536]{2,1,0:T(8,128)(2,1)S(1)}, u32[]{:S(2)}, u32[]{:S(2)}) collective-permute-start(f16[2,64,1536]{2,1,0:T(8,128)(2,1)S(1)} %fusion.27), channel_id=1, source_target_pairs={{0,1},{1,0},{2,3},{3,2},{4,5},{5,4},{6,7},{7,6},{8,9},{9,8},{10,11... | collective-permute-start | bytes 1179656 | tf_op jit(solution)/shard_map/ppermute | solution.py:852
  165.4 12.1 %collective-permute-start.28 = (bf16[2,64,1536]{2,1,0:T(8,128)(2,1)S(1)}, bf16[2,64,1536]{2,1,0:T(8,128)(2,1)S(1)}, u32[]{:S(2)}, u32[]{:S(2)}) collective-permute-start(bf16[2,64,1536]{2,1,0:T(8,128)(2,1)S(1)} %bitcast_select_fusion.1.refs_0_), channel_id=1, source_target_pairs={{0,1},{1,0},{2,3},{3,2},{4,5},{5,4},{6,7},{7,6},{8,9},{9,8},{10,11... | collective-permute-start | bytes 1179656 | tf_op jit(solution)/shard_map/ppermute | solution.py:852
  167.9 16.7 %collective-permute-start.29 = (bf16[2,64,1536]{2,1,0:T(8,128)(2,1)S(1)}, bf16[2,64,1536]{2,1,0:T(8,128)(2,1)S(1)}, u32[]{:S(2)}, u32[]{:S(2)}) collective-permute-start(bf16[2,64,1536]{2,1,0:T(8,128)(2,1)S(1)} %fusion.16), channel_id=1, source_target_pairs={{0,17},{1,16},{2,19},{3,18},{4,21},{5,20},{6,23},{7,22},{8,25},{9,... | collective-permute-start | bytes 1179656 | tf_op jit(solution)/shard_map/ppermute | solution.py:856
  187.4 17.1 %collective-permute-start.31 = (bf16[2,64,1536]{2,1,0:T(8,128)(2,1)S(1)}, bf16[2,64,1536]{2,1,0:T(8,128)(2,1)S(1)}, u32[]{:S(2)}, u32[]{:S(2)}) collective-permute-start(bf16[2,64,1536]{2,1,0:T(8,128)(2,1)S(1)} %bitcast_select_fusion.refs_0_), channel_id=1, source_target_pairs={{0,1},{1,0},{2,3},{3,2},{4,5},{5,4},{6,7},{7,6},{8,9},{9,8},{10,11... | collective-permute-start | bytes 1179656 | tf_op jit(solution)/shard_map/ppermute | solution.py:852
  204.9 18.9 %collective-permute-start.34 = (bf16[2,128,1536]{2,1,0:T(8,128)(2,1)S(1)}, bf16[2,128,1536]{2,1,0:T(8,128)(2,1)S(1)}, u32[]{:S(2)}, u32[]{:S(2)}) collective-permute-start(bf16[2,128,1536]{2,1,0:T(8,128)(2,1)S(1)} %bitcast.462), channel_id=1, source_target_pairs={{0,2},{2,0},{4,6},{6,4},{8,10},{10,8},{12,14},{14,12},{1,3},{3,1},... | collective-permute-start | bytes 2359304 | tf_op jit(solution)/shard_map/ppermute | solution.py:846
  224.9 26.5 %collective-permute-start.36 = (bf16[2,64,1536]{2,1,0:T(8,128)(2,1)S(1)}, bf16[2,64,1536]{2,1,0:T(8,128)(2,1)S(1)}, u32[]{:S(2)}, u32[]{:S(2)}) collective-permute-start(bf16[2,64,1536]{2,1,0:T(8,128)(2,1)S(1)} %bitcast.468), channel_id=1, source_target_pairs={{0,1},{1,0},{2,3},{3,2},{4,5},{5,4},{6,7},{7,6},{8,9},{9,8},{10,11... | collective-permute-start | bytes 1179656 | tf_op jit(solution)/shard_map/ppermute | solution.py:852
  228.6 22.9 %collective-permute-start.35 = (bf16[2,64,1536]{2,1,0:T(8,128)(2,1)S(1)}, bf16[2,64,1536]{2,1,0:T(8,128)(2,1)S(1)}, u32[]{:S(2)}, u32[]{:S(2)}) collective-permute-start(bf16[2,64,1536]{2,1,0:T(8,128)(2,1)S(1)} %bitcast.470), channel_id=1, source_target_pairs={{0,1},{1,0},{2,3},{3,2},{4,5},{5,4},{6,7},{7,6},{8,9},{9,8},{10,11... | collective-permute-start | bytes 1179656 | tf_op jit(solution)/shard_map/ppermute | solution.py:852
  254.1 11.5 %collective-permute-start.40 = (bf16[2,64,1536]{2,1,0:T(8,128)(2,1)S(1)}, bf16[2,64,1536]{2,1,0:T(8,128)(2,1)S(1)}, u32[]{:S(2)}, u32[]{:S(2)}) collective-permute-start(bf16[2,64,1536]{2,1,0:T(8,128)(2,1)S(1)} %bitcast.471), channel_id=1, source_target_pairs={{0,1},{1,0},{2,3},{3,2},{4,5},{5,4},{6,7},{7,6},{8,9},{9,8},{10,11... | collective-permute-start | bytes 1179656 | tf_op jit(solution)/shard_map/ppermute | solution.py:852
  267.8 21.9 %collective-permute-start.41 = (bf16[2,64,1536]{2,1,0:T(8,128)(2,1)S(1)}, bf16[2,64,1536]{2,1,0:T(8,128)(2,1)S(1)}, u32[]{:S(2)}, u32[]{:S(2)}) collective-permute-start(bf16[2,64,1536]{2,1,0:T(8,128)(2,1)S(1)} %get-tuple-element.335), channel_id=1, source_target_pairs={{16,0},{17,1},{18,2},{19,3},{20,4},{21,5},{22,6},{23,7},{24,8},{25... | collective-permute-start | bytes 1179656 | tf_op jit(solution)/shard_map/ppermute | solution.py:856
  292.4 12.2 %collective-permute-start.44 = (bf16[2,64,1536]{2,1,0:T(8,128)(2,1)}, bf16[2,64,1536]{2,1,0:T(8,128)(2,1)}, u32[]{:S(2)}, u32[]{:S(2)}) collective-permute-start(bf16[2,64,1536]{2,1,0:T(8,128)(2,1)} %bitcast_select_fusion.2.refs_0_), channel_id=1, source_target_pairs={{0,1},{1,0},{2,3},{3,2},{4,5},{5,4},{6,7},{7,6},{8,9},{9,8},{10,11... | collective-permute-start | bytes 1179656 | tf_op jit(solution)/shard_map/ppermute | solution.py:852
  297.3 15.4 %collective-permute-start.43 = (bf16[2,64,1536]{2,1,0:T(8,128)(2,1)}, bf16[2,64,1536]{2,1,0:T(8,128)(2,1)}, u32[]{:S(2)}, u32[]{:S(2)}) collective-permute-start(bf16[2,64,1536]{2,1,0:T(8,128)(2,1)} %bitcast.111), channel_id=1, source_target_pairs={{0,1},{1,0},{2,3},{3,2},{4,5},{5,4},{6,7},{7,6},{8,9},{9,8},{10,11... | collective-permute-start | bytes 1179656 | tf_op jit(solution)/shard_map/ppermute | solution.py:852
  323.3 31.6 %collective-permute-start.45 = (bf16[2,64,1536]{2,1,0:T(8,128)(2,1)S(1)}, bf16[2,64,1536]{2,1,0:T(8,128)(2,1)S(1)}, u32[]{:S(2)}, u32[]{:S(2)}) collective-permute-start(bf16[2,64,1536]{2,1,0:T(8,128)(2,1)S(1)} %get-tuple-element.343), channel_id=1, source_target_pairs={{16,0},{17,1},{18,2},{19,3},{20,4},{21,5},{22,6},{23,7},{24,8},{25... | collective-permute-start | bytes 1179656 | tf_op jit(solution)/shard_map/ppermute | solution.py:856
  328.6 26.2 %collective-permute-start.49 = (bf16[64,1536]{1,0:T(8,128)(2,1)S(1)}, bf16[64,1536]{1,0:T(8,128)(2,1)S(1)}, u32[]{:S(2)}, u32[]{:S(2)}) collective-permute-start(bf16[64,1536]{1,0:T(8,128)(2,1)S(1)} %get-tuple-element.352), channel_id=1, source_target_pairs={{0,4},{2,6},{4,0},{6,2},{8,12},{10,14},{12,8},{14,10},{1,5},{3,7},... | collective-permute-start | bytes 589832 | tf_op jit(solution)/shard_map/ppermute | solution.py:846
  329.0 25.9 %collective-permute-start.50 = (bf16[64,1536]{1,0:T(8,128)(2,1)S(1)}, bf16[64,1536]{1,0:T(8,128)(2,1)S(1)}, u32[]{:S(2)}, u32[]{:S(2)}) collective-permute-start(bf16[64,1536]{1,0:T(8,128)(2,1)S(1)} %get-tuple-element.353), channel_id=1, source_target_pairs={{0,8},{2,10},{4,12},{6,14},{8,0},{10,2},{12,4},{14,6},{1,9},{3,11}... | collective-permute-start | bytes 589832 | tf_op jit(solution)/shard_map/ppermute | solution.py:846
  330.6 24.2 %collective-permute-start.51 = (bf16[64,1536]{1,0:T(8,128)(2,1)S(1)}, bf16[64,1536]{1,0:T(8,128)(2,1)S(1)}, u32[]{:S(2)}, u32[]{:S(2)}) collective-permute-start(bf16[64,1536]{1,0:T(8,128)(2,1)S(1)} %get-tuple-element.354), channel_id=1, source_target_pairs={{0,12},{2,14},{4,8},{6,10},{8,4},{10,6},{12,0},{14,2},{1,13},{3,15... | collective-permute-start | bytes 589832 | tf_op jit(solution)/shard_map/ppermute | solution.py:846
  355.0 11.6 %collective-permute-start.52 = (bf16[2,64,1536]{2,1,0:T(8,128)(2,1)S(1)}, bf16[2,64,1536]{2,1,0:T(8,128)(2,1)S(1)}, u32[]{:S(2)}, u32[]{:S(2)}) collective-permute-start(bf16[2,64,1536]{2,1,0:T(8,128)(2,1)S(1)} %bitcast_select_fusion.3.refs_0_), channel_id=1, source_target_pairs={{0,1},{1,0},{2,3},{3,2},{4,5},{5,4},{6,7},{7,6},{8,9},{9,8},{10,11... | collective-permute-start | bytes 1179656 | tf_op jit(solution)/shard_map/ppermute | solution.py:852
  382.8 34.7 %collective-permute-start.57 = (bf16[2,64,1536]{2,1,0:T(8,128)(2,1)S(1)}, bf16[2,64,1536]{2,1,0:T(8,128)(2,1)S(1)}, u32[]{:S(2)}, u32[]{:S(2)}) collective-permute-start(bf16[2,64,1536]{2,1,0:T(8,128)(2,1)S(1)} %bitcast.467), channel_id=1, source_target_pairs={{0,1},{1,0},{2,3},{3,2},{4,5},{5,4},{6,7},{7,6},{8,9},{9,8},{10,11... | collective-permute-start | bytes 1179656 | tf_op jit(solution)/shard_map/ppermute | solution.py:852
  392.9 30.7 %collective-permute-start.58 = (bf16[2,192,1536]{2,1,0:T(8,128)(2,1)}, bf16[2,192,1536]{2,1,0:T(8,128)(2,1)}, u32[]{:S(2)}, u32[]{:S(2)}) collective-permute-start(bf16[2,192,1536]{2,1,0:T(8,128)(2,1)} %pad_maximum_fusion.2), channel_id=1, source_target_pairs={{0,4},{2,6},{4,0},{6,2},{8,12},{10,14},{12,8},{14,10},{1,5},{3,7},... | collective-permute-start | bytes 3538952 | tf_op jit(solution)/shard_map/ppermute | solution.py:846
  393.2 30.4 %collective-permute-start.59 = (bf16[2,192,1536]{2,1,0:T(8,128)(2,1)}, bf16[2,192,1536]{2,1,0:T(8,128)(2,1)}, u32[]{:S(2)}, u32[]{:S(2)}) collective-permute-start(bf16[2,192,1536]{2,1,0:T(8,128)(2,1)} %pad_maximum_fusion.3), channel_id=1, source_target_pairs={{0,8},{2,10},{4,12},{6,14},{8,0},{10,2},{12,4},{14,6},{1,9},{3,11}... | collective-permute-start | bytes 3538952 | tf_op jit(solution)/shard_map/ppermute | solution.py:846
  394.9 28.7 %collective-permute-start.60 = (bf16[4,64,1536]{2,1,0:T(8,128)(2,1)}, bf16[4,64,1536]{2,1,0:T(8,128)(2,1)}, u32[]{:S(2)}, u32[]{:S(2)}) collective-permute-start(bf16[4,64,1536]{2,1,0:T(8,128)(2,1)} %order_blocks.19.refs_0_), channel_id=1, source_target_pairs={{0,1},{1,0},{2,3},{3,2},{4,5},{5,4},{6,7},{7,6},{8,9},{9,8},{10,11... | collective-permute-start | bytes 2359304 | tf_op jit(solution)/shard_map/ppermute | solution.py:852
  425.1 18.2 %collective-permute-start.62 = (bf16[2,64,1536]{2,1,0:T(8,128)(2,1)S(1)}, bf16[2,64,1536]{2,1,0:T(8,128)(2,1)S(1)}, u32[]{:S(2)}, u32[]{:S(2)}) collective-permute-start(bf16[2,64,1536]{2,1,0:T(8,128)(2,1)S(1)} %bitcast.469), channel_id=1, source_target_pairs={{0,1},{1,0},{2,3},{3,2},{4,5},{5,4},{6,7},{7,6},{8,9},{9,8},{10,11... | collective-permute-start | bytes 1179656 | tf_op jit(solution)/shard_map/ppermute | solution.py:852
  428.3 16.2 %collective-permute-start.63 = (bf16[192,1536]{1,0:T(8,128)(2,1)S(1)}, bf16[192,1536]{1,0:T(8,128)(2,1)S(1)}, u32[]{:S(2)}, u32[]{:S(2)}) collective-permute-start(bf16[192,1536]{1,0:T(8,128)(2,1)S(1)} %fusion.3), channel_id=1, source_target_pairs={{0,8},{2,10},{4,12},{6,14},{8,0},{10,2},{12,4},{14,6},{1,9},{3,11}... | collective-permute-start | bytes 1769480 | tf_op jit(solution)/shard_map/ppermute | solution.py:846
  430.0 16.3 %collective-permute-start.64 = (bf16[192,1536]{1,0:T(8,128)(2,1)S(1)}, bf16[192,1536]{1,0:T(8,128)(2,1)S(1)}, u32[]{:S(2)}, u32[]{:S(2)}) collective-permute-start(bf16[192,1536]{1,0:T(8,128)(2,1)S(1)} %fusion.2), channel_id=1, source_target_pairs={{0,4},{2,6},{4,0},{6,2},{8,12},{10,14},{12,8},{14,10},{1,5},{3,7},... | collective-permute-start | bytes 1769480 | tf_op jit(solution)/shard_map/ppermute | solution.py:846
  437.8 36.0 %collective-permute-start.68 = (bf16[2,192,1152]{2,1,0:T(8,128)(2,1)}, bf16[2,192,1152]{2,1,0:T(8,128)(2,1)}, u32[]{:S(2)}, u32[]{:S(2)}) collective-permute-start(bf16[2,192,1152]{2,1,0:T(8,128)(2,1)} %dynamic-slice_bitcast_fusion.1), channel_id=1, source_target_pairs={{0,4},{2,6},{4,0},{6,2},{8,12},{10,14},{12,8},{14,10},{1,5},{3,7},... | collective-permute-start | bytes 2654216 | tf_op jit(solution)/shard_map/ppermute | solution.py:846
  439.1 34.7 %collective-permute-start.69 = (bf16[2,192,1152]{2,1,0:T(8,128)(2,1)}, bf16[2,192,1152]{2,1,0:T(8,128)(2,1)}, u32[]{:S(2)}, u32[]{:S(2)}) collective-permute-start(bf16[2,192,1152]{2,1,0:T(8,128)(2,1)} %dynamic-slice_bitcast_fusion), channel_id=1, source_target_pairs={{0,8},{2,10},{4,12},{6,14},{8,0},{10,2},{12,4},{14,6},{1,9},{3,11}... | collective-permute-start | bytes 2654216 | tf_op jit(solution)/shard_map/ppermute | solution.py:846
  449.7 19.8 %collective-permute-start.65 = (bf16[64,1536]{1,0:T(8,128)(2,1)}, bf16[64,1536]{1,0:T(8,128)(2,1)}, u32[]{:S(2)}, u32[]{:S(2)}) collective-permute-start(bf16[64,1536]{1,0:T(8,128)(2,1)} %get-tuple-element.508), channel_id=1, source_target_pairs={{0,4},{2,6},{4,0},{6,2},{8,12},{10,14},{12,8},{14,10},{1,5},{3,7},... | collective-permute-start | bytes 589832 | tf_op jit(solution)/shard_map/ppermute | solution.py:846
  451.4 18.1 %collective-permute-start.66 = (bf16[64,1536]{1,0:T(8,128)(2,1)}, bf16[64,1536]{1,0:T(8,128)(2,1)}, u32[]{:S(2)}, u32[]{:S(2)}) collective-permute-start(bf16[64,1536]{1,0:T(8,128)(2,1)} %get-tuple-element.507), channel_id=1, source_target_pairs={{0,8},{2,10},{4,12},{6,14},{8,0},{10,2},{12,4},{14,6},{1,9},{3,11}... | collective-permute-start | bytes 589832 | tf_op jit(solution)/shard_map/ppermute | solution.py:846
  455.6 18.2 %collective-permute-start.67 = (bf16[64,1536]{1,0:T(8,128)(2,1)}, bf16[64,1536]{1,0:T(8,128)(2,1)}, u32[]{:S(2)}, u32[]{:S(2)}) collective-permute-start(bf16[64,1536]{1,0:T(8,128)(2,1)} %get-tuple-element.506), channel_id=1, source_target_pairs={{0,12},{2,14},{4,8},{6,10},{8,4},{10,6},{12,0},{14,2},{1,13},{3,15... | collective-permute-start | bytes 589832 | tf_op jit(solution)/shard_map/ppermute | solution.py:846
  477.7 11.2 %collective-permute-start.72 = (bf16[192,1152]{1,0:T(8,128)(2,1)S(1)}, bf16[192,1152]{1,0:T(8,128)(2,1)S(1)}, u32[]{:S(2)}, u32[]{:S(2)}) collective-permute-start(bf16[192,1152]{1,0:T(8,128)(2,1)S(1)} %fusion.7), channel_id=1, source_target_pairs={{0,8},{2,10},{4,12},{6,14},{8,0},{10,2},{12,4},{14,6},{1,9},{3,11}... | collective-permute-start | bytes 1327112 | tf_op jit(solution)/shard_map/ppermute | solution.py:846
  478.1 11.5 %collective-permute-start.73 = (bf16[192,1152]{1,0:T(8,128)(2,1)S(1)}, bf16[192,1152]{1,0:T(8,128)(2,1)S(1)}, u32[]{:S(2)}, u32[]{:S(2)}) collective-permute-start(bf16[192,1152]{1,0:T(8,128)(2,1)S(1)} %fusion.6), channel_id=1, source_target_pairs={{0,4},{2,6},{4,0},{6,2},{8,12},{10,14},{12,8},{14,10},{1,5},{3,7},... | collective-permute-start | bytes 1327112 | tf_op jit(solution)/shard_map/ppermute | solution.py:846
  479.9 30.3 %collective-permute-start.71 = (bf16[4,64,1536]{2,1,0:T(8,128)(2,1)S(1)}, bf16[4,64,1536]{2,1,0:T(8,128)(2,1)}, u32[]{:S(2)}, u32[]{:S(2)}) collective-permute-start(bf16[4,64,1536]{2,1,0:T(8,128)(2,1)S(1)} %order_blocks.24.refs_0_), channel_id=1, source_target_pairs={{0,1},{1,0},{2,3},{3,2},{4,5},{5,4},{6,7},{7,6},{8,9},{9,8},{10,11... | collective-permute-start | bytes 2359304 | tf_op jit(solution)/shard_map/ppermute | solution.py:852
  (168 other events, 1449.7 us)

commit v4 on v3

--- a/solution.py
+++ b/solution.py
@@ -851,6 +851,10 @@
     def swap_tensor(self, block, mask):
         return lax.ppermute(block, "tensor", [(i, i ^ mask) for i in range(self.tensors)])
 
+    def swap_both(self, block):
+        count = self.context * self.tensors
+        return lax.ppermute(block, ("context", "tensor"), [(i, i ^ self.tensors ^ 1) for i in range(count)])
+
     def next_section(self, block, step, flip):
         count, tensors = lax.axis_size("section"), self.tensors
         return lax.ppermute(
@@ -933,13 +937,18 @@
 
 
 def sum_all(place, block, micro=True, part=True, tensor=True):
-    if part:
-        for mask in bits_of(place.parts):
-            block = block + place.swap_part(block, mask)
-    if tensor:
-        for mask in bits_of(place.tensors):
-            block = block + place.swap_tensor(block, mask)
-    if micro:
+    if part and tensor and place.parts == place.tensors == 2:
+        block = (block + place.swap_part(block, 1)) + (place.swap_tensor(block, 1) + place.swap_both(block))
+    else:
+        if part:
+            for mask in bits_of(place.parts):
+                block = block + place.swap_part(block, mask)
+        if tensor:
+            for mask in bits_of(place.tensors):
+                block = block + place.swap_tensor(block, mask)
+    if micro and place.micros == 4:
+        block = (block + place.swap_micro(block, 1)) + (place.swap_micro(block, 2) + place.swap_micro(block, 3))
+    elif micro:
         for mask in bits_of(place.micros):
             block = block + place.swap_micro(block, mask)
     return block
@@ -1739,7 +1748,9 @@
     scatter = scatter.trade()
     gate_grad = columns_beside(place, scatter, width, width)
     out_grad = order([block[:, :width].astype(f32).T for block in scatter], part, 0).reshape(-1, w_out.shape[2])
-    homing.came, mixes.next, gate_grad, out_grad = tie(homing.came, mixes.next, gate_grad, out_grad)
+    homing.came, mixes.next, gate_grad, out_grad, outputs = tie(
+        homing.came, mixes.next, gate_grad, out_grad, outputs
+    )
     mixes.land()
     mixes.prepare()
     homing.collect()
@@ -1755,16 +1766,16 @@
         [jnp.pad(packed, ((0, 0), (0, lanes - mixed))), jnp.pad(norm_grad[None], ((0, 7), (0, lanes - norm_grad.size)))],
         axis=0,
     )
-    packed, mixes.next = tie(packed, mixes.next)
     mixes.land()
     while mixes.left[0]:
         mixes.prepare()
         mixes.launch()
         mixes.land()
+    mixes = mixes.trade()
+    packed, mixes = tie(packed, mixes)
     packed = sum_all(place, packed, part=False, tensor=False)
     by_part = [packed] + [place.swap_part(packed, d) for d in range(1, parts)]
     input_grads = homing.result().reshape(block_input.shape).astype(f32)
-    mixes = mixes.trade()
     value_grad = columns_beside(place, mixes, 0, width)
     step_grad = beside([block[:, mixed : mixed + heads_here].astype(f32) for block in mixes], part)
     maps_grad = sum(block[:, width:mixed].astype(f32) for block in mixes).astype(bf16)
@@ -1772,10 +1783,7 @@
     for mask in bits_of(place.tensors):
         maps_sum = maps_sum + place.swap_tensor(maps_sum, mask)
 
-    both = by_part[0]
-    for distance in range(1, parts):
-        both = both + by_part[distance]
-    both = sum_all(place, both, micro=False, part=False)
+    both = sum_all(place, packed, micro=False)
     wide, bias_grad, gain_grad, maps_small, maps_bias, norm_sum, by_head = unpack(
         place, both, by_part, width, heads_here, norm_grad.size
     )

time: 532 us -> 522 us (0.981)
    ppermute x54 -> x55, waiting for transfers between devices: 98.7 us -> 88.6 us  [swap_part(): lax.ppermute(block, 'context', [(i, i ^ mask) for i in range(self.context)])]
    unnamed x274 -> x268, local copies, waits for them, and re-layouts: 34.5 us -> 31.9 us
    ppermute x54 -> x55, starting transfers between devices: 39.1 us -> 41.1 us  [swap_part(): lax.ppermute(block, 'context', [(i, i ^ mask) for i in range(self.context)])]
  transfers between devices with their start and end apart: 80 -> 85, of which waited for: 39 -> 37; matrix products, arithmetic and copies ran while one was open for 14% -> 14% of each run, Pallas kernels for 29% -> 30%
where the time goes in v4:
time: 522 us; the launch traced here: 516 us
  Pallas kernels  171 us (33%)
  waiting for transfers between devices  151 us (29%)
  starting transfers between devices  80.7 us (15%)
  local copies, waits for them, and re-layouts  61.4 us (12%)
  other arithmetic  33.4 us (6%)
  matrix products  15.4 us (3%)
    ppermute x55, waiting for transfers between devices, swap_part(): lax.ppermute(block, 'context', [(i, i ^ mask) for i in range(self.context)])  88.6 us
    pallas_call x4, Pallas kernels, backward_call(): pl.pallas_call(functools.partial(backward_kernel, exact, width, place.par...  70.8 us
    ppermute x22, waiting for transfers between devices, swap_tensor(): lax.ppermute(block, 'tensor', [(i, i ^ mask) for i in range(self.tensors)])  52.6 us
    pallas_call x4, Pallas kernels, forward_call(): pl.pallas_call(functools.partial(forward_kernel, keep, width, place.parts...  51 us
    ppermute x55, starting transfers between devices, swap_part(): lax.ppermute(block, 'context', [(i, i ^ mask) for i in range(self.context)])  41.1 us
    unnamed x268, local copies, waits for them, and re-layouts  31.9 us
    ppermute x22, starting transfers between devices, swap_tensor(): lax.ppermute(block, 'tensor', [(i, i ^ mask) for i in range(self.tensors)])  24.5 us
    squeeze x19, local copies, waits for them, and re-layouts, pick(): return lax.dynamic_index_in_dim(array, index, axis, False)  14.8 us
  transfers between devices with their start and end apart: 85, of which 37 were waited for; matrix products, arithmetic and copies ran while one was open for 14% of the time, Pallas kernels for 30%

profile of v4, /device:TPU:0, one launch (start us, length us, event | category | flops | bytes accessed | tf_op | source)
XLA Modules:
  0.0 516.2 jit_solution(17326006544302858493)
XLA Ops:
  4.9 3.6 collective-permute-start.2
  16.2 2.1 collective-permute-done.1
  23.0 11.3 %collective-permute-done.4.refs_1_ = bf16[1,192,1920]{2,1,0:T(8,128)(2,1)S(1)} collective-permute-done((bf16[1,192,1920]{2,1,0:T(8,128)(2,1)S(1)}, bf16[1,192,1920]{2,1,0:T(8,128)(2,1)S(1)}, u32[]{:S(2)}, u32[]{:S(2)}) %collective-permute-start.4) | collective-permute-done | bytes 737312 | tf_op jit(solution)/shard_map/ppermute | solution.py:846
  42.4 2.2 broadcast_select_fusion.1
  44.8 29.6 %collective-permute-done.8.refs_2_ = bf16[2,192,1920]{2,1,0:T(8,128)(2,1)S(1)} collective-permute-done((bf16[2,192,1920]{2,1,0:T(8,128)(2,1)S(1)}, bf16[2,192,1920]{2,1,0:T(8,128)(2,1)S(1)}, u32[]{:S(2)}, u32[]{:S(2)}) %collective-permute-start.8) | collective-permute-done | bytes 1474592 | tf_op jit(solution)/shard_map/ppermute | solution.py:846
  79.6 11.4 %section_forward.4 = (f32[512,768]{1,0:T(8,128)S(1)}, f32[2,4,1,128]{3,2,1,0:T(1,128)S(1)}, f32[128,768]{1,0:T(8,128)S(1)}, f32[8,1024]{1,0:T(8,128)S(1)}) custom-call(s32[1]{0:T(128)} %bitcast.part_ref.index_ref, bf16[512,1536]{1,0:T(8,128)(2,1)S(1)} %bitcast.404, bf16[1536,1152]{1,0:T(8,128)(2,1)S(1)} %bitcast.447, bf16[1536,768]{1,0:T(8,128)(2,1)S(1)} %bitcast.455, ...), custom_call_target="tpu_custom_call" | custom-call | flops 15728640000 | bytes 12582912 | tf_op jit(solution)/shard_map/section_forward/pallas_call | solution.py:380
  96.0 12.1 %section_forward.5 = (f32[512,768]{1,0:T(8,128)S(1)}, f32[2,4,1,128]{3,2,1,0:T(1,128)S(1)}, f32[128,768]{1,0:T(8,128)}, f32[8,1024]{1,0:T(8,128)}) custom-call(s32[1]{0:T(128)} %bitcast.part_ref.index_ref, bf16[512,1536]{1,0:T(8,128)(2,1)S(1)} %bitcast.401, bf16[1536,1152]{1,0:T(8,128)(2,1)S(1)} %bitcast.448, bf16[1536,768]{1,0:T(8,128)(2,1)S(1)} %bitcast.456, ...), custom_call_target="tpu_custom_call" | custom-call | flops 15728640000 | bytes 12582912 | tf_op jit(solution)/shard_map/section_forward/pallas_call | solution.py:380
  111.3 3.4 out_forward.2
  124.2 3.4 out_forward.3
  129.0 9.0 %collective-permute-done.24 = bf16[128,1536]{1,0:T(8,128)(2,1)S(1)} collective-permute-done((bf16[128,1536]{1,0:T(8,128)(2,1)S(1)}, bf16[128,1536]{1,0:T(8,128)(2,1)S(1)}, u32[]{:S(2)}, u32[]{:S(2)}) %collective-permute-start.24) | collective-permute-done | bytes 393248 | tf_op jit(solution)/shard_map/ppermute | solution.py:846
  142.2 4.9 collective-permute-start.27
  149.1 2.2 broadcast_select_fusion
  151.5 2.6 copy-done.18
  156.8 7.2 %collective-permute-done.21 = f16[2,64,1536]{2,1,0:T(8,128)(2,1)S(1)} collective-permute-done((f16[2,64,1536]{2,1,0:T(8,128)(2,1)S(1)}, f16[2,64,1536]{2,1,0:T(8,128)(2,1)S(1)}, u32[]{:S(2)}, u32[]{:S(2)}) %collective-permute-start.21) | collective-permute-done | bytes 393248 | tf_op jit(solution)/shard_map/ppermute | solution.py:852
  165.4 2.5 collective-permute-start.28
  167.9 3.2 collective-permute-start.29
  171.1 6.3 %collective-permute-done.28.refs_1_ = bf16[2,64,1536]{2,1,0:T(8,128)(2,1)S(1)} collective-permute-done((bf16[2,64,1536]{2,1,0:T(8,128)(2,1)S(1)}, bf16[2,64,1536]{2,1,0:T(8,128)(2,1)S(1)}, u32[]{:S(2)}, u32[]{:S(2)}) %collective-permute-start.28) | collective-permute-done | bytes 393248 | tf_op jit(solution)/shard_map/ppermute | solution.py:852
  177.5 7.1 %collective-permute-done.29 = bf16[2,64,1536]{2,1,0:T(8,128)(2,1)S(1)} collective-permute-done((bf16[2,64,1536]{2,1,0:T(8,128)(2,1)S(1)}, bf16[2,64,1536]{2,1,0:T(8,128)(2,1)S(1)}, u32[]{:S(2)}, u32[]{:S(2)}) %collective-permute-start.29) | collective-permute-done | bytes 393248 | tf_op jit(solution)/shard_map/ppermute | solution.py:860
  184.9 2.3 collective-permute-done.30.refs_1_
  187.4 3.9 collective-permute-start.31
  191.3 13.4 %section_forward.6 = (f32[2,128,1536]{2,1,0:T(8,128)S(1)}, bf16[1,2,128,1536]{3,2,1,0:T(8,128)(2,1)S(1)}, f32[2,4,1,128]{3,2,1,0:T(1,128)S(1)}, f32[128,768]{1,0...) custom-call(s32[1]{0:T(128)} %bitcast.part_ref.index_ref, ...), custom_call_target="tpu_custom_call" | custom-call | flops 15728640000 | bytes 12582912 | tf_op jit(solution)/shard_map/section_forward/pallas_call | solution.py:380
  207.5 14.1 %section_forward.7 = (f32[2,128,1536]{2,1,0:T(8,128)S(1)}, bf16[1,2,128,1536]{3,2,1,0:T(8,128)(2,1)S(1)}, f32[2,4,1,128]{3,2,1,0:T(1,128)S(1)}, f32[128,768]{1,0...) custom-call(s32[1]{0:T(128)} %bitcast.part_ref.index_ref, ...), custom_call_target="tpu_custom_call" | custom-call | flops 15728640000 | bytes 12582912 | tf_op jit(solution)/shard_map/section_forward/pallas_call | solution.py:380
  231.7 16.7 %section_backward.4 = (f32[2,128,1536]{2,1,0:T(8,128)S(1)}, bf16[1,2,128,1536]{3,2,1,0:T(8,128)(2,1)S(1)}, bf16[512,1152]{1,0:T(8,128)(2,1)}, f32[128,768]{1,0:T...) custom-call(s32[1]{0:T(128)} %bitcast.part_ref.index_ref, f32[512,768]{1,0:T(8,128)S(1)} %get-tuple-element.310.dy_ref, ...), custom_call_target="tpu_custom_call" | custom-call | flops 23592960000 | bytes 12582912 | tf_op jit(solution)/shard_map/section_backward/pallas_call | solution.py:723
  251.2 2.3 collective-permute-done.40.refs_0_
  255.2 9.7 %collective-permute-done.41.refs_0_ = bf16[2,64,1536]{2,1,0:T(8,128)(2,1)S(1)} collective-permute-done((bf16[2,64,1536]{2,1,0:T(8,128)(2,1)S(1)}, bf16[2,64,1536]{2,1,0:T(8,128)(2,1)S(1)}, u32[]{:S(2)}, u32[]{:S(2)}) %collective-permute-start.41) | collective-permute-done | bytes 393248 | tf_op jit(solution)/shard_map/ppermute | solution.py:852
  264.9 2.2 finish_gradient.4
  268.5 16.9 %section_backward.5 = (f32[2,128,1536]{2,1,0:T(8,128)S(1)}, bf16[1,2,128,1536]{3,2,1,0:T(8,128)(2,1)}, bf16[512,1152]{1,0:T(8,128)(2,1)}, f32[128,768]{1,0:T(8,1...) custom-call(s32[1]{0:T(128)} %bitcast.part_ref.index_ref, f32[512,768]{1,0:T(8,128)S(1)} %get-tuple-element.328.dy_ref, ...), custom_call_target="tpu_custom_call" | custom-call | flops 23592960000 | bytes 12582912 | tf_op jit(solution)/shard_map/section_backward/pallas_call | solution.py:723
  286.5 2.1 collective-permute-done.42
  297.8 5.8 %collective-permute-done.45.refs_1_ = bf16[2,64,1536]{2,1,0:T(8,128)(2,1)} collective-permute-done((bf16[2,64,1536]{2,1,0:T(8,128)(2,1)}, bf16[2,64,1536]{2,1,0:T(8,128)(2,1)}, u32[]{:S(2)}, u32[]{:S(2)}) %collective-permute-start.45) | collective-permute-done | bytes 393248 | tf_op jit(solution)/shard_map/ppermute | solution.py:852
  303.6 8.0 %collective-permute-done.44.refs_0_ = bf16[2,64,1536]{2,1,0:T(8,128)(2,1)} collective-permute-done((bf16[2,64,1536]{2,1,0:T(8,128)(2,1)}, bf16[2,64,1536]{2,1,0:T(8,128)(2,1)}, u32[]{:S(2)}, u32[]{:S(2)}) %collective-permute-start.44) | collective-permute-done | bytes 393248 | tf_op jit(solution)/shard_map/ppermute | solution.py:852
  314.7 3.4 finish_gradient.5
  319.9 2.2 norm_backward.2
  324.3 3.6 fusion.62
  335.4 18.1 %section_backward.6 = (f32[2,128,1536]{2,1,0:T(8,128)S(1)}, bf16[1,2,128,1536]{3,2,1,0:T(8,128)(2,1)S(1)}, bf16[512,1152]{1,0:T(8,128)(2,1)S(1)}, f32[128,768]{1...) custom-call(s32[1]{0:T(128)} %bitcast.part_ref.index_ref, f32[512,768]{1,0:T(8,128)S(1)} %get-tuple-element.358.dy_ref, ...), custom_call_target="tpu_custom_call" | custom-call | flops 23592960000 | bytes 12582912 | tf_op jit(solution)/shard_map/section_backward/pallas_call | solution.py:723
  356.9 8.9 %collective-permute-done.54.refs_1_ = bf16[2,64,1536]{2,1,0:T(8,128)(2,1)S(1)} collective-permute-done((bf16[2,64,1536]{2,1,0:T(8,128)(2,1)S(1)}, bf16[2,64,1536]{2,1,0:T(8,128)(2,1)S(1)}, u32[]{:S(2)}, u32[]{:S(2)}) %collective-permute-start.54) | collective-permute-done | bytes 393248 | tf_op jit(solution)/shard_map/ppermute | solution.py:852
  367.1 2.5 collective-permute-done.56.refs_1_
  374.5 2.6 norm_backward.3
  380.8 3.1 add.548
  397.0 19.0 %section_backward.7 = (f32[2,128,1536]{2,1,0:T(8,128)S(1)}, bf16[1,2,128,1536]{3,2,1,0:T(8,128)(2,1)}, bf16[512,1152]{1,0:T(8,128)(2,1)S(1)}, f32[128,768]{1,0:T...) custom-call(s32[1]{0:T(128)} %bitcast.part_ref.index_ref, f32[512,768]{1,0:T(8,128)S(1)} %get-tuple-element.388.dy_ref, ...), custom_call_target="tpu_custom_call" | custom-call | flops 23592960000 | bytes 12582912 | tf_op jit(solution)/shard_map/section_backward/pallas_call | solution.py:723
  432.8 2.3 fusion.65
  435.1 2.4 fusion
  441.9 2.5 order_blocks.23
  454.9 2.1 slice_bitcast_fusion.refs_0_
  462.4 8.6 %collective-permute-done.68.refs_1_ = bf16[64,1536]{1,0:T(8,128)(2,1)} collective-permute-done((bf16[64,1536]{1,0:T(8,128)(2,1)}, bf16[64,1536]{1,0:T(8,128)(2,1)}, u32[]{:S(2)}, u32[]{:S(2)}) %collective-permute-start.68) | collective-permute-done | bytes 196640 | tf_op jit(solution)/shard_map/ppermute | solution.py:846
  471.0 3.9 collective-permute-done.70.refs_3_
  484.8 6.7 %collective-permute-done.75.refs_2_ = bf16[192,1152]{1,0:T(8,128)(2,1)S(1)} collective-permute-done((bf16[192,1152]{1,0:T(8,128)(2,1)S(1)}, bf16[192,1152]{1,0:T(8,128)(2,1)S(1)}, u32[]{:S(2)}, u32[]{:S(2)}) %collective-permute-start.75) | collective-permute-done | bytes 442400 | tf_op jit(solution)/shard_map/ppermute | solution.py:846
  494.9 2.7 collective-permute-done.74.refs_1_
  498.8 2.1 convert.24
  (569 shorter events, 194.7 us)
Async XLA Ops:
  3.2 11.1 %collective-permute-start.5 = (bf16[1,192,1920]{2,1,0:T(8,128)(2,1)S(1)}, bf16[1,192,1920]{2,1,0:T(8,128)(2,1)S(1)}, u32[]{:S(2)}, u32[]{:S(2)}) collective-permute-start(bf16[1,192,1920]{2,1,0:T(8,128)(2,1)S(1)} %get-tuple-element.524), channel_id=1, source_target_pairs={{0,2},{2,0},{4,6},{6,4},{8,10},{10,8},{12,14},{14,12},{1,3},{3,1},... | collective-permute-start | bytes 2211848 | tf_op jit(solution)/shard_map/ppermute | solution.py:846
  9.1 25.2 %collective-permute-start.4 = (bf16[1,192,1920]{2,1,0:T(8,128)(2,1)S(1)}, bf16[1,192,1920]{2,1,0:T(8,128)(2,1)S(1)}, u32[]{:S(2)}, u32[]{:S(2)}) collective-permute-start(bf16[1,192,1920]{2,1,0:T(8,128)(2,1)S(1)} %get-tuple-element.525.refs_0_), channel_id=1, source_target_pairs={{0,4},{2,6},{4,0},{6,2},{8,12},{10,14},{12,8},{14,10},{1,5},{3,7},... | collective-permute-start | bytes 2211848 | tf_op jit(solution)/shard_map/ppermute | solution.py:846
  14.3 61.7 %collective-permute-start.10 = (bf16[1,192,768]{2,1,0:T(8,128)(2,1)}, bf16[1,192,768]{2,1,0:T(8,128)(2,1)}, u32[]{:S(2)}, u32[]{:S(2)}) collective-permute-start(bf16[1,192,768]{2,1,0:T(8,128)(2,1)} %get-tuple-element.515), channel_id=1, source_target_pairs={{0,2},{2,0},{4,6},{6,4},{8,10},{10,8},{12,14},{14,12},{1,3},{3,1},... | collective-permute-start | bytes 884744 | tf_op jit(solution)/shard_map/ppermute | solution.py:846
  14.3 21.1 %collective-permute-start.6 = (bf16[1,192,1920]{2,1,0:T(8,128)(2,1)S(1)}, bf16[1,192,1920]{2,1,0:T(8,128)(2,1)S(1)}, u32[]{:S(2)}, u32[]{:S(2)}) collective-permute-start(bf16[1,192,1920]{2,1,0:T(8,128)(2,1)S(1)} %collective-permute-done.5.refs_3_), channel_id=1, source_target_pairs={{0,8},{2,10},{4,12},{6,14},{8,0},{10,2},{12,4},{14,6},{1,9},{3,11}... | collective-permute-start | bytes 2211848 | tf_op jit(solution)/shard_map/ppermute | solution.py:846
  19.8 15.5 %collective-permute-start.3 = (bf16[3,64,1536]{2,1,0:T(8,128)(2,1)}, bf16[3,64,1536]{2,1,0:T(8,128)(2,1)}, u32[]{:S(2)}, u32[]{:S(2)}) collective-permute-start(bf16[3,64,1536]{2,1,0:T(8,128)(2,1)} %pad_maximum_fusion.6), channel_id=1, source_target_pairs={{0,1},{1,0},{2,3},{3,2},{4,5},{5,4},{6,7},{7,6},{8,9},{9,8},{10,11... | collective-permute-start | bytes 1769480 | tf_op jit(solution)/shard_map/ppermute | solution.py:852
  39.6 34.8 %collective-permute-start.8 = (bf16[2,192,1920]{2,1,0:T(8,128)(2,1)S(1)}, bf16[2,192,1920]{2,1,0:T(8,128)(2,1)S(1)}, u32[]{:S(2)}, u32[]{:S(2)}) collective-permute-start(bf16[2,192,1920]{2,1,0:T(8,128)(2,1)S(1)} %pad_maximum_fusion), channel_id=1, source_target_pairs={{0,8},{2,10},{4,12},{6,14},{8,0},{10,2},{12,4},{14,6},{1,9},{3,11}... | collective-permute-start | bytes 4423688 | tf_op jit(solution)/shard_map/ppermute | solution.py:846
  41.5 34.5 %collective-permute-start.9 = (bf16[2,192,1920]{2,1,0:T(8,128)(2,1)S(1)}, bf16[2,192,1920]{2,1,0:T(8,128)(2,1)S(1)}, u32[]{:S(2)}, u32[]{:S(2)}) collective-permute-start(bf16[2,192,1920]{2,1,0:T(8,128)(2,1)S(1)} %pad_maximum_fusion.1), channel_id=1, source_target_pairs={{0,4},{2,6},{4,0},{6,2},{8,12},{10,14},{12,8},{14,10},{1,5},{3,7},... | collective-permute-start | bytes 4423688 | tf_op jit(solution)/shard_map/ppermute | solution.py:846
  76.0 15.0 %collective-permute-start.11 = (bf16[1,192,768]{2,1,0:T(8,128)(2,1)S(1)}, bf16[1,192,768]{2,1,0:T(8,128)(2,1)S(1)}, u32[]{:S(2)}, u32[]{:S(2)}) collective-permute-start(bf16[1,192,768]{2,1,0:T(8,128)(2,1)S(1)} %get-tuple-element.244.refs_0_), channel_id=1, source_target_pairs={{0,4},{2,6},{4,0},{6,2},{8,12},{10,14},{12,8},{14,10},{1,5},{3,7},... | collective-permute-start | bytes 884744 | tf_op jit(solution)/shard_map/ppermute | solution.py:846
  76.3 14.8 %collective-permute-start.12 = (bf16[1,192,768]{2,1,0:T(8,128)(2,1)}, bf16[1,192,768]{2,1,0:T(8,128)(2,1)S(1)}, u32[]{:S(2)}, u32[]{:S(2)}) collective-permute-start(bf16[1,192,768]{2,1,0:T(8,128)(2,1)} %collective-permute-done.10.refs_3_), channel_id=1, source_target_pairs={{0,8},{2,10},{4,12},{6,14},{8,0},{10,2},{12,4},{14,6},{1,9},{3,11}... | collective-permute-start | bytes 884744 | tf_op jit(solution)/shard_map/ppermute | solution.py:846
  92.3 15.7 %collective-permute-start.14 = (f32[4,128]{1,0:T(4,128)S(1)}, f32[4,128]{1,0:T(4,128)S(1)}, u32[]{:S(2)}, u32[]{:S(2)}) collective-permute-start(f32[4,128]{1,0:T(4,128)S(1)} %fusion.51), channel_id=1, source_target_pairs={{0,1},{1,0},{2,3},{3,2},{4,5},{5,4},{6,7},{7,6},{8,9},{9,8},{10,11... | collective-permute-start | bytes 6152 | tf_op jit(solution)/shard_map/ppermute | solution.py:852
  93.9 15.4 %collective-permute-start.15 = (bf16[2,192,768]{2,1,0:T(8,128)(2,1)S(1)}, bf16[2,192,768]{2,1,0:T(8,128)(2,1)S(1)}, u32[]{:S(2)}, u32[]{:S(2)}) collective-permute-start(bf16[2,192,768]{2,1,0:T(8,128)(2,1)S(1)} %pad_maximum_fusion.7), channel_id=1, source_target_pairs={{0,8},{2,10},{4,12},{6,14},{8,0},{10,2},{12,4},{14,6},{1,9},{3,11}... | collective-permute-start | bytes 1769480 | tf_op jit(solution)/shard_map/ppermute | solution.py:846
  94.3 15.2 %collective-permute-start.16 = (bf16[2,192,768]{2,1,0:T(8,128)(2,1)S(1)}, bf16[2,192,768]{2,1,0:T(8,128)(2,1)S(1)}, u32[]{:S(2)}, u32[]{:S(2)}) collective-permute-start(bf16[2,192,768]{2,1,0:T(8,128)(2,1)S(1)} %pad_maximum_fusion.8), channel_id=1, source_target_pairs={{0,4},{2,6},{4,0},{6,2},{8,12},{10,14},{12,8},{14,10},{1,5},{3,7},... | collective-permute-start | bytes 1769480 | tf_op jit(solution)/shard_map/ppermute | solution.py:846
  116.9 12.0 %collective-permute-start.23 = (bf16[128,1536]{1,0:T(8,128)(2,1)S(1)}, bf16[128,1536]{1,0:T(8,128)(2,1)S(1)}, u32[]{:S(2)}, u32[]{:S(2)}) collective-permute-start(bf16[128,1536]{1,0:T(8,128)(2,1)S(1)} %get-tuple-element.494), channel_id=1, source_target_pairs={{0,4},{2,6},{4,0},{6,2},{8,12},{10,14},{12,8},{14,10},{1,5},{3,7},... | collective-permute-start | bytes 1179656 | tf_op jit(solution)/shard_map/ppermute | solution.py:846
  118.7 19.3 %collective-permute-start.24 = (bf16[128,1536]{1,0:T(8,128)(2,1)S(1)}, bf16[128,1536]{1,0:T(8,128)(2,1)S(1)}, u32[]{:S(2)}, u32[]{:S(2)}) collective-permute-start(bf16[128,1536]{1,0:T(8,128)(2,1)S(1)} %get-tuple-element.493), channel_id=1, source_target_pairs={{0,8},{2,10},{4,12},{6,14},{8,0},{10,2},{12,4},{14,6},{1,9},{3,11}... | collective-permute-start | bytes 1179656 | tf_op jit(solution)/shard_map/ppermute | solution.py:846
  119.2 18.8 %collective-permute-start.25 = (bf16[128,1536]{1,0:T(8,128)(2,1)S(1)}, bf16[128,1536]{1,0:T(8,128)(2,1)S(1)}, u32[]{:S(2)}, u32[]{:S(2)}) collective-permute-start(bf16[128,1536]{1,0:T(8,128)(2,1)S(1)} %get-tuple-element.492), channel_id=1, source_target_pairs={{0,12},{2,14},{4,8},{6,10},{8,4},{10,6},{12,0},{14,2},{1,13},{3,15... | collective-permute-start | bytes 1179656 | tf_op jit(solution)/shard_map/ppermute | solution.py:846
  122.2 15.8 %collective-permute-start.22 = (f16[2,64,1536]{2,1,0:T(8,128)(2,1)S(1)}, f16[2,64,1536]{2,1,0:T(8,128)(2,1)S(1)}, u32[]{:S(2)}, u32[]{:S(2)}) collective-permute-start(f16[2,64,1536]{2,1,0:T(8,128)(2,1)S(1)} %fusion.26), channel_id=1, source_target_pairs={{0,1},{1,0},{2,3},{3,2},{4,5},{5,4},{6,7},{7,6},{8,9},{9,8},{10,11... | collective-permute-start | bytes 1179656 | tf_op jit(solution)/shard_map/ppermute | solution.py:852
  128.7 18.3 %collective-permute-start.20 = (f32[2,128,1536]{2,1,0:T(8,128)}, f32[2,128,1536]{2,1,0:T(8,128)}, u32[]{:S(2)}, u32[]{:S(2)}) collective-permute-start(f32[2,128,1536]{2,1,0:T(8,128)} %bitcast.68), channel_id=1, source_target_pairs={{0,2},{2,0},{4,6},{6,4},{8,10},{10,8},{12,14},{14,12},{1,3},{3,1},... | collective-permute-start | bytes 4718600 | tf_op jit(solution)/shard_map/ppermute | solution.py:846
  142.2 23.1 %collective-permute-start.27 = (bf16[2,64,1536]{2,1,0:T(8,128)(2,1)S(1)}, bf16[2,64,1536]{2,1,0:T(8,128)(2,1)S(1)}, u32[]{:S(2)}, u32[]{:S(2)}) collective-permute-start(bf16[2,64,1536]{2,1,0:T(8,128)(2,1)S(1)} %fusion.11), channel_id=1, source_target_pairs={{0,17},{1,16},{2,19},{3,18},{4,21},{5,20},{6,23},{7,22},{8,25},{9,... | collective-permute-start | bytes 1179656 | tf_op jit(solution)/shard_map/ppermute | solution.py:860
  148.3 15.7 %collective-permute-start.21 = (f16[2,64,1536]{2,1,0:T(8,128)(2,1)S(1)}, f16[2,64,1536]{2,1,0:T(8,128)(2,1)S(1)}, u32[]{:S(2)}, u32[]{:S(2)}) collective-permute-start(f16[2,64,1536]{2,1,0:T(8,128)(2,1)S(1)} %fusion.27), channel_id=1, source_target_pairs={{0,1},{1,0},{2,3},{3,2},{4,5},{5,4},{6,7},{7,6},{8,9},{9,8},{10,11... | collective-permute-start | bytes 1179656 | tf_op jit(solution)/shard_map/ppermute | solution.py:852
  165.4 12.1 %collective-permute-start.28 = (bf16[2,64,1536]{2,1,0:T(8,128)(2,1)S(1)}, bf16[2,64,1536]{2,1,0:T(8,128)(2,1)S(1)}, u32[]{:S(2)}, u32[]{:S(2)}) collective-permute-start(bf16[2,64,1536]{2,1,0:T(8,128)(2,1)S(1)} %bitcast_select_fusion.1.refs_0_), channel_id=1, source_target_pairs={{0,1},{1,0},{2,3},{3,2},{4,5},{5,4},{6,7},{7,6},{8,9},{9,8},{10,11... | collective-permute-start | bytes 1179656 | tf_op jit(solution)/shard_map/ppermute | solution.py:852
  167.9 16.7 %collective-permute-start.29 = (bf16[2,64,1536]{2,1,0:T(8,128)(2,1)S(1)}, bf16[2,64,1536]{2,1,0:T(8,128)(2,1)S(1)}, u32[]{:S(2)}, u32[]{:S(2)}) collective-permute-start(bf16[2,64,1536]{2,1,0:T(8,128)(2,1)S(1)} %fusion.16), channel_id=1, source_target_pairs={{0,17},{1,16},{2,19},{3,18},{4,21},{5,20},{6,23},{7,22},{8,25},{9,... | collective-permute-start | bytes 1179656 | tf_op jit(solution)/shard_map/ppermute | solution.py:860
  187.4 17.3 %collective-permute-start.31 = (bf16[2,64,1536]{2,1,0:T(8,128)(2,1)S(1)}, bf16[2,64,1536]{2,1,0:T(8,128)(2,1)S(1)}, u32[]{:S(2)}, u32[]{:S(2)}) collective-permute-start(bf16[2,64,1536]{2,1,0:T(8,128)(2,1)S(1)} %bitcast_select_fusion.refs_0_), channel_id=1, source_target_pairs={{0,1},{1,0},{2,3},{3,2},{4,5},{5,4},{6,7},{7,6},{8,9},{9,8},{10,11... | collective-permute-start | bytes 1179656 | tf_op jit(solution)/shard_map/ppermute | solution.py:852
  205.1 18.9 %collective-permute-start.34 = (bf16[2,128,1536]{2,1,0:T(8,128)(2,1)S(1)}, bf16[2,128,1536]{2,1,0:T(8,128)(2,1)S(1)}, u32[]{:S(2)}, u32[]{:S(2)}) collective-permute-start(bf16[2,128,1536]{2,1,0:T(8,128)(2,1)S(1)} %bitcast.464), channel_id=1, source_target_pairs={{0,2},{2,0},{4,6},{6,4},{8,10},{10,8},{12,14},{14,12},{1,3},{3,1},... | collective-permute-start | bytes 2359304 | tf_op jit(solution)/shard_map/ppermute | solution.py:846
  225.1 26.0 %collective-permute-start.36 = (bf16[2,64,1536]{2,1,0:T(8,128)(2,1)S(1)}, bf16[2,64,1536]{2,1,0:T(8,128)(2,1)S(1)}, u32[]{:S(2)}, u32[]{:S(2)}) collective-permute-start(bf16[2,64,1536]{2,1,0:T(8,128)(2,1)S(1)} %bitcast.470), channel_id=1, source_target_pairs={{0,1},{1,0},{2,3},{3,2},{4,5},{5,4},{6,7},{7,6},{8,9},{9,8},{10,11... | collective-permute-start | bytes 1179656 | tf_op jit(solution)/shard_map/ppermute | solution.py:852
  226.7 24.4 %collective-permute-start.35 = (bf16[2,64,1536]{2,1,0:T(8,128)(2,1)S(1)}, bf16[2,64,1536]{2,1,0:T(8,128)(2,1)S(1)}, u32[]{:S(2)}, u32[]{:S(2)}) collective-permute-start(bf16[2,64,1536]{2,1,0:T(8,128)(2,1)S(1)} %bitcast.472), channel_id=1, source_target_pairs={{0,1},{1,0},{2,3},{3,2},{4,5},{5,4},{6,7},{7,6},{8,9},{9,8},{10,11... | collective-permute-start | bytes 1179656 | tf_op jit(solution)/shard_map/ppermute | solution.py:852
  253.7 11.2 %collective-permute-start.41 = (bf16[2,64,1536]{2,1,0:T(8,128)(2,1)S(1)}, bf16[2,64,1536]{2,1,0:T(8,128)(2,1)S(1)}, u32[]{:S(2)}, u32[]{:S(2)}) collective-permute-start(bf16[2,64,1536]{2,1,0:T(8,128)(2,1)S(1)} %bitcast.473), channel_id=1, source_target_pairs={{0,1},{1,0},{2,3},{3,2},{4,5},{5,4},{6,7},{7,6},{8,9},{9,8},{10,11... | collective-permute-start | bytes 1179656 | tf_op jit(solution)/shard_map/ppermute | solution.py:852
  267.1 21.5 %collective-permute-start.42 = (bf16[2,64,1536]{2,1,0:T(8,128)(2,1)S(1)}, bf16[2,64,1536]{2,1,0:T(8,128)(2,1)S(1)}, u32[]{:S(2)}, u32[]{:S(2)}) collective-permute-start(bf16[2,64,1536]{2,1,0:T(8,128)(2,1)S(1)} %get-tuple-element.336), channel_id=1, source_target_pairs={{16,0},{17,1},{18,2},{19,3},{20,4},{21,5},{22,6},{23,7},{24,8},{25... | collective-permute-start | bytes 1179656 | tf_op jit(solution)/shard_map/ppermute | solution.py:860
  291.3 12.2 %collective-permute-start.45 = (bf16[2,64,1536]{2,1,0:T(8,128)(2,1)}, bf16[2,64,1536]{2,1,0:T(8,128)(2,1)}, u32[]{:S(2)}, u32[]{:S(2)}) collective-permute-start(bf16[2,64,1536]{2,1,0:T(8,128)(2,1)} %bitcast_select_fusion.2.refs_0_), channel_id=1, source_target_pairs={{0,1},{1,0},{2,3},{3,2},{4,5},{5,4},{6,7},{7,6},{8,9},{9,8},{10,11... | collective-permute-start | bytes 1179656 | tf_op jit(solution)/shard_map/ppermute | solution.py:852
  296.2 15.4 %collective-permute-start.44 = (bf16[2,64,1536]{2,1,0:T(8,128)(2,1)}, bf16[2,64,1536]{2,1,0:T(8,128)(2,1)}, u32[]{:S(2)}, u32[]{:S(2)}) collective-permute-start(bf16[2,64,1536]{2,1,0:T(8,128)(2,1)} %bitcast.111), channel_id=1, source_target_pairs={{0,1},{1,0},{2,3},{3,2},{4,5},{5,4},{6,7},{7,6},{8,9},{9,8},{10,11... | collective-permute-start | bytes 1179656 | tf_op jit(solution)/shard_map/ppermute | solution.py:852
  318.1 36.1 %collective-permute-start.46 = (bf16[2,64,1536]{2,1,0:T(8,128)(2,1)S(1)}, bf16[2,64,1536]{2,1,0:T(8,128)(2,1)S(1)}, u32[]{:S(2)}, u32[]{:S(2)}) collective-permute-start(bf16[2,64,1536]{2,1,0:T(8,128)(2,1)S(1)} %get-tuple-element.344), channel_id=1, source_target_pairs={{16,0},{17,1},{18,2},{19,3},{20,4},{21,5},{22,6},{23,7},{24,8},{25... | collective-permute-start | bytes 1179656 | tf_op jit(solution)/shard_map/ppermute | solution.py:860
  328.0 26.2 %collective-permute-start.51 = (bf16[64,1536]{1,0:T(8,128)(2,1)S(1)}, bf16[64,1536]{1,0:T(8,128)(2,1)S(1)}, u32[]{:S(2)}, u32[]{:S(2)}) collective-permute-start(bf16[64,1536]{1,0:T(8,128)(2,1)S(1)} %get-tuple-element.353), channel_id=1, source_target_pairs={{0,4},{2,6},{4,0},{6,2},{8,12},{10,14},{12,8},{14,10},{1,5},{3,7},... | collective-permute-start | bytes 589832 | tf_op jit(solution)/shard_map/ppermute | solution.py:846
  328.4 25.7 %collective-permute-start.52 = (bf16[64,1536]{1,0:T(8,128)(2,1)S(1)}, bf16[64,1536]{1,0:T(8,128)(2,1)S(1)}, u32[]{:S(2)}, u32[]{:S(2)}) collective-permute-start(bf16[64,1536]{1,0:T(8,128)(2,1)S(1)} %get-tuple-element.354), channel_id=1, source_target_pairs={{0,8},{2,10},{4,12},{6,14},{8,0},{10,2},{12,4},{14,6},{1,9},{3,11}... | collective-permute-start | bytes 589832 | tf_op jit(solution)/shard_map/ppermute | solution.py:846
  330.0 24.1 %collective-permute-start.53 = (bf16[64,1536]{1,0:T(8,128)(2,1)S(1)}, bf16[64,1536]{1,0:T(8,128)(2,1)S(1)}, u32[]{:S(2)}, u32[]{:S(2)}) collective-permute-start(bf16[64,1536]{1,0:T(8,128)(2,1)S(1)} %get-tuple-element.355), channel_id=1, source_target_pairs={{0,12},{2,14},{4,8},{6,10},{8,4},{10,6},{12,0},{14,2},{1,13},{3,15... | collective-permute-start | bytes 589832 | tf_op jit(solution)/shard_map/ppermute | solution.py:846
  354.3 11.6 %collective-permute-start.54 = (bf16[2,64,1536]{2,1,0:T(8,128)(2,1)S(1)}, bf16[2,64,1536]{2,1,0:T(8,128)(2,1)S(1)}, u32[]{:S(2)}, u32[]{:S(2)}) collective-permute-start(bf16[2,64,1536]{2,1,0:T(8,128)(2,1)S(1)} %bitcast_select_fusion.3.refs_0_), channel_id=1, source_target_pairs={{0,1},{1,0},{2,3},{3,2},{4,5},{5,4},{6,7},{7,6},{8,9},{9,8},{10,11... | collective-permute-start | bytes 1179656 | tf_op jit(solution)/shard_map/ppermute | solution.py:852
  384.0 34.2 %collective-permute-start.60 = (bf16[2,64,1536]{2,1,0:T(8,128)(2,1)S(1)}, bf16[2,64,1536]{2,1,0:T(8,128)(2,1)S(1)}, u32[]{:S(2)}, u32[]{:S(2)}) collective-permute-start(bf16[2,64,1536]{2,1,0:T(8,128)(2,1)S(1)} %bitcast.469), channel_id=1, source_target_pairs={{0,1},{1,0},{2,3},{3,2},{4,5},{5,4},{6,7},{7,6},{8,9},{9,8},{10,11... | collective-permute-start | bytes 1179656 | tf_op jit(solution)/shard_map/ppermute | solution.py:852
  393.2 31.1 %collective-permute-start.61 = (bf16[2,192,1536]{2,1,0:T(8,128)(2,1)}, bf16[2,192,1536]{2,1,0:T(8,128)(2,1)}, u32[]{:S(2)}, u32[]{:S(2)}) collective-permute-start(bf16[2,192,1536]{2,1,0:T(8,128)(2,1)} %pad_maximum_fusion.2), channel_id=1, source_target_pairs={{0,4},{2,6},{4,0},{6,2},{8,12},{10,14},{12,8},{14,10},{1,5},{3,7},... | collective-permute-start | bytes 3538952 | tf_op jit(solution)/shard_map/ppermute | solution.py:846
  393.6 30.7 %collective-permute-start.62 = (bf16[2,192,1536]{2,1,0:T(8,128)(2,1)}, bf16[2,192,1536]{2,1,0:T(8,128)(2,1)}, u32[]{:S(2)}, u32[]{:S(2)}) collective-permute-start(bf16[2,192,1536]{2,1,0:T(8,128)(2,1)} %pad_maximum_fusion.3), channel_id=1, source_target_pairs={{0,8},{2,10},{4,12},{6,14},{8,0},{10,2},{12,4},{14,6},{1,9},{3,11}... | collective-permute-start | bytes 3538952 | tf_op jit(solution)/shard_map/ppermute | solution.py:846
  395.2 29.1 %collective-permute-start.63 = (bf16[4,64,1536]{2,1,0:T(8,128)(2,1)}, bf16[4,64,1536]{2,1,0:T(8,128)(2,1)}, u32[]{:S(2)}, u32[]{:S(2)}) collective-permute-start(bf16[4,64,1536]{2,1,0:T(8,128)(2,1)} %order_blocks.19.refs_0_), channel_id=1, source_target_pairs={{0,1},{1,0},{2,3},{3,2},{4,5},{5,4},{6,7},{7,6},{8,9},{9,8},{10,11... | collective-permute-start | bytes 2359304 | tf_op jit(solution)/shard_map/ppermute | solution.py:852
  425.6 20.4 %collective-permute-start.65 = (bf16[2,64,1536]{2,1,0:T(8,128)(2,1)S(1)}, bf16[2,64,1536]{2,1,0:T(8,128)(2,1)S(1)}, u32[]{:S(2)}, u32[]{:S(2)}) collective-permute-start(bf16[2,64,1536]{2,1,0:T(8,128)(2,1)S(1)} %bitcast.471), channel_id=1, source_target_pairs={{0,1},{1,0},{2,3},{3,2},{4,5},{5,4},{6,7},{7,6},{8,9},{9,8},{10,11... | collective-permute-start | bytes 1179656 | tf_op jit(solution)/shard_map/ppermute | solution.py:852
  428.3 17.6 %collective-permute-start.66 = (bf16[192,1536]{1,0:T(8,128)(2,1)S(1)}, bf16[192,1536]{1,0:T(8,128)(2,1)S(1)}, u32[]{:S(2)}, u32[]{:S(2)}) collective-permute-start(bf16[192,1536]{1,0:T(8,128)(2,1)S(1)} %fusion.3), channel_id=1, source_target_pairs={{0,8},{2,10},{4,12},{6,14},{8,0},{10,2},{12,4},{14,6},{1,9},{3,11}... | collective-permute-start | bytes 1769480 | tf_op jit(solution)/shard_map/ppermute | solution.py:846
  431.5 16.3 %collective-permute-start.67 = (bf16[192,1536]{1,0:T(8,128)(2,1)S(1)}, bf16[192,1536]{1,0:T(8,128)(2,1)S(1)}, u32[]{:S(2)}, u32[]{:S(2)}) collective-permute-start(bf16[192,1536]{1,0:T(8,128)(2,1)S(1)} %fusion.2), channel_id=1, source_target_pairs={{0,4},{2,6},{4,0},{6,2},{8,12},{10,14},{12,8},{14,10},{1,5},{3,7},... | collective-permute-start | bytes 1769480 | tf_op jit(solution)/shard_map/ppermute | solution.py:846
  438.9 36.0 %collective-permute-start.71 = (bf16[2,192,1152]{2,1,0:T(8,128)(2,1)}, bf16[2,192,1152]{2,1,0:T(8,128)(2,1)}, u32[]{:S(2)}, u32[]{:S(2)}) collective-permute-start(bf16[2,192,1152]{2,1,0:T(8,128)(2,1)} %dynamic-slice_bitcast_fusion.1), channel_id=1, source_target_pairs={{0,4},{2,6},{4,0},{6,2},{8,12},{10,14},{12,8},{14,10},{1,5},{3,7},... | collective-permute-start | bytes 2654216 | tf_op jit(solution)/shard_map/ppermute | solution.py:846
  440.6 34.3 %collective-permute-start.72 = (bf16[2,192,1152]{2,1,0:T(8,128)(2,1)}, bf16[2,192,1152]{2,1,0:T(8,128)(2,1)}, u32[]{:S(2)}, u32[]{:S(2)}) collective-permute-start(bf16[2,192,1152]{2,1,0:T(8,128)(2,1)} %dynamic-slice_bitcast_fusion), channel_id=1, source_target_pairs={{0,8},{2,10},{4,12},{6,14},{8,0},{10,2},{12,4},{14,6},{1,9},{3,11}... | collective-permute-start | bytes 2654216 | tf_op jit(solution)/shard_map/ppermute | solution.py:846
  451.2 19.8 %collective-permute-start.68 = (bf16[64,1536]{1,0:T(8,128)(2,1)}, bf16[64,1536]{1,0:T(8,128)(2,1)}, u32[]{:S(2)}, u32[]{:S(2)}) collective-permute-start(bf16[64,1536]{1,0:T(8,128)(2,1)} %get-tuple-element.510), channel_id=1, source_target_pairs={{0,4},{2,6},{4,0},{6,2},{8,12},{10,14},{12,8},{14,10},{1,5},{3,7},... | collective-permute-start | bytes 589832 | tf_op jit(solution)/shard_map/ppermute | solution.py:846
  452.5 18.6 %collective-permute-start.69 = (bf16[64,1536]{1,0:T(8,128)(2,1)}, bf16[64,1536]{1,0:T(8,128)(2,1)}, u32[]{:S(2)}, u32[]{:S(2)}) collective-permute-start(bf16[64,1536]{1,0:T(8,128)(2,1)} %get-tuple-element.509), channel_id=1, source_target_pairs={{0,8},{2,10},{4,12},{6,14},{8,0},{10,2},{12,4},{14,6},{1,9},{3,11}... | collective-permute-start | bytes 589832 | tf_op jit(solution)/shard_map/ppermute | solution.py:846
  456.9 18.0 %collective-permute-start.70 = (bf16[64,1536]{1,0:T(8,128)(2,1)}, bf16[64,1536]{1,0:T(8,128)(2,1)}, u32[]{:S(2)}, u32[]{:S(2)}) collective-permute-start(bf16[64,1536]{1,0:T(8,128)(2,1)} %get-tuple-element.508), channel_id=1, source_target_pairs={{0,12},{2,14},{4,8},{6,10},{8,4},{10,6},{12,0},{14,2},{1,13},{3,15... | collective-permute-start | bytes 589832 | tf_op jit(solution)/shard_map/ppermute | solution.py:846
  478.9 18.7 %collective-permute-start.74 = (bf16[4,64,1536]{2,1,0:T(8,128)(2,1)S(1)}, bf16[4,64,1536]{2,1,0:T(8,128)(2,1)}, u32[]{:S(2)}, u32[]{:S(2)}) collective-permute-start(bf16[4,64,1536]{2,1,0:T(8,128)(2,1)S(1)} %order_blocks.24.refs_0_), channel_id=1, source_target_pairs={{0,1},{1,0},{2,3},{3,2},{4,5},{5,4},{6,7},{7,6},{8,9},{9,8},{10,11... | collective-permute-start | bytes 2359304 | tf_op jit(solution)/shard_map/ppermute | solution.py:852
  480.7 10.9 %collective-permute-start.75 = (bf16[192,1152]{1,0:T(8,128)(2,1)S(1)}, bf16[192,1152]{1,0:T(8,128)(2,1)S(1)}, u32[]{:S(2)}, u32[]{:S(2)}) collective-permute-start(bf16[192,1152]{1,0:T(8,128)(2,1)S(1)} %fusion.7), channel_id=1, source_target_pairs={{0,8},{2,10},{4,12},{6,14},{8,0},{10,2},{12,4},{14,6},{1,9},{3,11}... | collective-permute-start | bytes 1327112 | tf_op jit(solution)/shard_map/ppermute | solution.py:846
  (170 other events, 1722.9 us)

commit v5 on v4

--- a/solution.py
+++ b/solution.py
@@ -240,7 +240,7 @@
             sums_ref[1, c] = as_row(pulls)
         return 0
 
-    lax.fori_loop(0, per_step, chunk, 0)
+    lax.fori_loop(0, per_step, chunk, 0, unroll=2 if per_step % 2 == 0 else 1)
     if keep:
         total[...] = lax.dot_general(
             gg[...], wo_ref[...], (((1,), (1,)), ((), ())), preferred_element_type=f32
@@ -257,7 +257,7 @@
             n[here, span] = (g_ref[here, span] * q[:, :lanes] * inner_ref[1:2, span]).astype(bf16)
         return 0
 
-    lax.fori_loop(0, per_step, chunk, 0)
+    lax.fori_loop(0, per_step, chunk, 0, unroll=2 if per_step % 2 == 0 else 1)
     total[...] = lax.dot_general(n[...], wo_ref[...], (((1,), (1,)), ((), ())), preferred_element_type=f32)
     deal(part_ref[0], parts, pl.program_id(0) * per_step, per_step, total, own_ref, send_ref, sems)
 
@@ -383,7 +383,7 @@
             num_scalar_prefetch=1, grid=(steps,), in_specs=in_specs, out_specs=out_specs, scratch_shapes=scratch
         ),
         out_shape=out_shape,
-        compiler_params=kernel_params(steps, 10 if keep else 11),
+        compiler_params=kernel_params(steps, 12 if keep else 13),
         cost_estimate=pl.CostEstimate(
             flops=tokens * width * 40000, bytes_accessed=tokens * depth * 16, transcendentals=0
         ),
@@ -413,7 +413,7 @@
         pull_ref[c] = as_row(pulls)
         return 0
 
-    lax.fori_loop(0, per_step, chunk, 0)
+    lax.fori_loop(0, per_step, chunk, 0, unroll=2 if per_step % 2 == 0 else 1)
     gain_ref[...] = jnp.broadcast_to(jnp.sum(gains[...], axis=0, keepdims=True), gains.shape)
 
 
@@ -432,7 +432,7 @@
             dz_ref[here, span] = (dg * y * (sig + silu * (1.0 - sig))).astype(bf16)
         return 0
 
-    lax.fori_loop(0, per_step, chunk, 0)
+    lax.fori_loop(0, per_step, chunk, 0, unroll=2 if per_step % 2 == 0 else 1)
 
 
 def normal_call(e, weights, z, y, q, inner):
@@ -681,7 +681,7 @@
         dvbd_ref[here, mixed:] = ddt_cols.astype(bf16)
         return 0
 
-    lax.fori_loop(0, per_step, chunk, 0)
+    lax.fori_loop(0, per_step, chunk, 0, unroll=2 if per_step % 2 == 0 else 1)
     nt = (((1,), (1,)), ((), ()))
     total[...] = lax.dot_general(dvbd_ref[...], w1_ref[...], nt, preferred_element_type=f32)
     total[...] += lax.dot_general(dz_ref[...], wg_ref[...], nt, preferred_element_type=f32)
@@ -767,7 +767,7 @@
             jax.ShapeDtypeStruct(vbd.shape, bf16),
         ]
         + [jax.ShapeDtypeStruct(*item) for item in shapes],
-        compiler_params=kernel_params(steps, 12),
+        compiler_params=kernel_params(steps, 14),
         cost_estimate=pl.CostEstimate(
             flops=tokens * width * 60000, bytes_accessed=tokens * depth * 16, transcendentals=0
         ),

time: 522 us -> 522 us (level)
  transfers between devices with their start and end apart: 85 -> 85, of which waited for: 37 -> 36; matrix products, arithmetic and copies ran while one was open for 14% -> 14% of each run, Pallas kernels for 30% -> 29%
where the time goes in v5:
time: 522 us; the launch traced here: 516 us
  Pallas kernels  169 us (32%)
  waiting for transfers between devices  153 us (29%)
  starting transfers between devices  79.3 us (15%)
  local copies, waits for them, and re-layouts  62.6 us (12%)
  other arithmetic  33.4 us (6%)
  matrix products  15.4 us (3%)
    ppermute x55, waiting for transfers between devices, swap_part(): lax.ppermute(block, 'context', [(i, i ^ mask) for i in range(self.context)])  89.2 us
    pallas_call x4, Pallas kernels, backward_call(): pl.pallas_call(functools.partial(backward_kernel, exact, width, place.par...  71 us
    ppermute x22, waiting for transfers between devices, swap_tensor(): lax.ppermute(block, 'tensor', [(i, i ^ mask) for i in range(self.tensors)])  53.6 us
    pallas_call x4, Pallas kernels, forward_call(): pl.pallas_call(functools.partial(forward_kernel, keep, width, place.parts...  49.5 us
    ppermute x55, starting transfers between devices, swap_part(): lax.ppermute(block, 'context', [(i, i ^ mask) for i in range(self.context)])  41.1 us
    unnamed x268, local copies, waits for them, and re-layouts  33.1 us
    ppermute x22, starting transfers between devices, swap_tensor(): lax.ppermute(block, 'tensor', [(i, i ^ mask) for i in range(self.tensors)])  24 us
    squeeze x19, local copies, waits for them, and re-layouts, pick(): return lax.dynamic_index_in_dim(array, index, axis, False)  14.8 us
  transfers between devices with their start and end apart: 85, of which 36 were waited for; matrix products, arithmetic and copies ran while one was open for 14% of the time, Pallas kernels for 29%

profile of v5, /device:TPU:0, one launch (start us, length us, event | category | flops | bytes accessed | tf_op | source)
XLA Modules:
  0.0 515.7 jit_solution(3151130996409773478)
XLA Ops:
  4.9 3.6 collective-permute-start.2
  16.2 2.1 collective-permute-done.1
  23.0 11.3 %collective-permute-done.4.refs_1_ = bf16[1,192,1920]{2,1,0:T(8,128)(2,1)S(1)} collective-permute-done((bf16[1,192,1920]{2,1,0:T(8,128)(2,1)S(1)}, bf16[1,192,1920]{2,1,0:T(8,128)(2,1)S(1)}, u32[]{:S(2)}, u32[]{:S(2)}) %collective-permute-start.4) | collective-permute-done | bytes 737312 | tf_op jit(solution)/shard_map/ppermute | solution.py:846
  42.4 2.2 broadcast_select_fusion.1
  44.8 29.6 %collective-permute-done.8.refs_2_ = bf16[2,192,1920]{2,1,0:T(8,128)(2,1)S(1)} collective-permute-done((bf16[2,192,1920]{2,1,0:T(8,128)(2,1)S(1)}, bf16[2,192,1920]{2,1,0:T(8,128)(2,1)S(1)}, u32[]{:S(2)}, u32[]{:S(2)}) %collective-permute-start.8) | collective-permute-done | bytes 1474592 | tf_op jit(solution)/shard_map/ppermute | solution.py:846
  79.6 11.0 %section_forward.4 = (f32[512,768]{1,0:T(8,128)S(1)}, f32[2,4,1,128]{3,2,1,0:T(1,128)S(1)}, f32[128,768]{1,0:T(8,128)S(1)}, f32[8,1024]{1,0:T(8,128)S(1)}) custom-call(s32[1]{0:T(128)} %bitcast.part_ref.index_ref, bf16[512,1536]{1,0:T(8,128)(2,1)S(1)} %bitcast.404, bf16[1536,1152]{1,0:T(8,128)(2,1)S(1)} %bitcast.447, bf16[1536,768]{1,0:T(8,128)(2,1)S(1)} %bitcast.455, ...), custom_call_target="tpu_custom_call" | custom-call | flops 15728640000 | bytes 12582912 | tf_op jit(solution)/shard_map/section_forward/pallas_call | solution.py:380
  95.5 11.6 %section_forward.5 = (f32[512,768]{1,0:T(8,128)S(1)}, f32[2,4,1,128]{3,2,1,0:T(1,128)S(1)}, f32[128,768]{1,0:T(8,128)}, f32[8,1024]{1,0:T(8,128)}) custom-call(s32[1]{0:T(128)} %bitcast.part_ref.index_ref, bf16[512,1536]{1,0:T(8,128)(2,1)S(1)} %bitcast.401, bf16[1536,1152]{1,0:T(8,128)(2,1)S(1)} %bitcast.448, bf16[1536,768]{1,0:T(8,128)(2,1)S(1)} %bitcast.456, ...), custom_call_target="tpu_custom_call" | custom-call | flops 15728640000 | bytes 12582912 | tf_op jit(solution)/shard_map/section_forward/pallas_call | solution.py:380
  110.8 3.3 out_forward.2
  123.5 3.3 out_forward.3
  128.3 9.0 %collective-permute-done.24 = bf16[128,1536]{1,0:T(8,128)(2,1)S(1)} collective-permute-done((bf16[128,1536]{1,0:T(8,128)(2,1)S(1)}, bf16[128,1536]{1,0:T(8,128)(2,1)S(1)}, u32[]{:S(2)}, u32[]{:S(2)}) %collective-permute-start.24) | collective-permute-done | bytes 393248 | tf_op jit(solution)/shard_map/ppermute | solution.py:846
  141.6 4.4 collective-permute-start.27
  148.0 2.2 broadcast_select_fusion
  150.4 2.6 copy-done.18
  155.7 7.6 %collective-permute-done.21 = f16[2,64,1536]{2,1,0:T(8,128)(2,1)S(1)} collective-permute-done((f16[2,64,1536]{2,1,0:T(8,128)(2,1)S(1)}, f16[2,64,1536]{2,1,0:T(8,128)(2,1)S(1)}, u32[]{:S(2)}, u32[]{:S(2)}) %collective-permute-start.21) | collective-permute-done | bytes 393248 | tf_op jit(solution)/shard_map/ppermute | solution.py:852
  164.8 2.5 collective-permute-start.28
  167.3 2.7 collective-permute-start.29
  170.1 6.8 %collective-permute-done.28.refs_1_ = bf16[2,64,1536]{2,1,0:T(8,128)(2,1)S(1)} collective-permute-done((bf16[2,64,1536]{2,1,0:T(8,128)(2,1)S(1)}, bf16[2,64,1536]{2,1,0:T(8,128)(2,1)S(1)}, u32[]{:S(2)}, u32[]{:S(2)}) %collective-permute-start.28) | collective-permute-done | bytes 393248 | tf_op jit(solution)/shard_map/ppermute | solution.py:852
  176.9 7.1 %collective-permute-done.29 = bf16[2,64,1536]{2,1,0:T(8,128)(2,1)S(1)} collective-permute-done((bf16[2,64,1536]{2,1,0:T(8,128)(2,1)S(1)}, bf16[2,64,1536]{2,1,0:T(8,128)(2,1)S(1)}, u32[]{:S(2)}, u32[]{:S(2)}) %collective-permute-start.29) | collective-permute-done | bytes 393248 | tf_op jit(solution)/shard_map/ppermute | solution.py:860
  184.3 2.3 collective-permute-done.30.refs_1_
  186.8 3.4 collective-permute-start.31
  190.2 13.0 %section_forward.6 = (f32[2,128,1536]{2,1,0:T(8,128)S(1)}, bf16[1,2,128,1536]{3,2,1,0:T(8,128)(2,1)S(1)}, f32[2,4,1,128]{3,2,1,0:T(1,128)S(1)}, f32[128,768]{1,0...) custom-call(s32[1]{0:T(128)} %bitcast.part_ref.index_ref, ...), custom_call_target="tpu_custom_call" | custom-call | flops 15728640000 | bytes 12582912 | tf_op jit(solution)/shard_map/section_forward/pallas_call | solution.py:380
  206.0 13.9 %section_forward.7 = (f32[2,128,1536]{2,1,0:T(8,128)S(1)}, bf16[1,2,128,1536]{3,2,1,0:T(8,128)(2,1)S(1)}, f32[2,4,1,128]{3,2,1,0:T(1,128)S(1)}, f32[128,768]{1,0...) custom-call(s32[1]{0:T(128)} %bitcast.part_ref.index_ref, ...), custom_call_target="tpu_custom_call" | custom-call | flops 15728640000 | bytes 12582912 | tf_op jit(solution)/shard_map/section_forward/pallas_call | solution.py:380
  229.9 16.5 %section_backward.4 = (f32[2,128,1536]{2,1,0:T(8,128)S(1)}, bf16[1,2,128,1536]{3,2,1,0:T(8,128)(2,1)S(1)}, bf16[512,1152]{1,0:T(8,128)(2,1)}, f32[128,768]{1,0:T...) custom-call(s32[1]{0:T(128)} %bitcast.part_ref.index_ref, f32[512,768]{1,0:T(8,128)S(1)} %get-tuple-element.310.dy_ref, ...), custom_call_target="tpu_custom_call" | custom-call | flops 23592960000 | bytes 12582912 | tf_op jit(solution)/shard_map/section_backward/pallas_call | solution.py:723
  249.1 2.3 collective-permute-done.40.refs_0_
  253.1 9.8 %collective-permute-done.41.refs_0_ = bf16[2,64,1536]{2,1,0:T(8,128)(2,1)S(1)} collective-permute-done((bf16[2,64,1536]{2,1,0:T(8,128)(2,1)S(1)}, bf16[2,64,1536]{2,1,0:T(8,128)(2,1)S(1)}, u32[]{:S(2)}, u32[]{:S(2)}) %collective-permute-start.41) | collective-permute-done | bytes 393248 | tf_op jit(solution)/shard_map/ppermute | solution.py:852
  262.9 2.2 finish_gradient.4
  266.4 17.0 %section_backward.5 = (f32[2,128,1536]{2,1,0:T(8,128)S(1)}, bf16[1,2,128,1536]{3,2,1,0:T(8,128)(2,1)}, bf16[512,1152]{1,0:T(8,128)(2,1)}, f32[128,768]{1,0:T(8,1...) custom-call(s32[1]{0:T(128)} %bitcast.part_ref.index_ref, f32[512,768]{1,0:T(8,128)S(1)} %get-tuple-element.328.dy_ref, ...), custom_call_target="tpu_custom_call" | custom-call | flops 23592960000 | bytes 12582912 | tf_op jit(solution)/shard_map/section_backward/pallas_call | solution.py:723
  284.6 2.0 collective-permute-done.42
  295.7 5.8 %collective-permute-done.45.refs_1_ = bf16[2,64,1536]{2,1,0:T(8,128)(2,1)} collective-permute-done((bf16[2,64,1536]{2,1,0:T(8,128)(2,1)}, bf16[2,64,1536]{2,1,0:T(8,128)(2,1)}, u32[]{:S(2)}, u32[]{:S(2)}) %collective-permute-start.45) | collective-permute-done | bytes 393248 | tf_op jit(solution)/shard_map/ppermute | solution.py:852
  301.5 8.0 %collective-permute-done.44.refs_0_ = bf16[2,64,1536]{2,1,0:T(8,128)(2,1)} collective-permute-done((bf16[2,64,1536]{2,1,0:T(8,128)(2,1)}, bf16[2,64,1536]{2,1,0:T(8,128)(2,1)}, u32[]{:S(2)}, u32[]{:S(2)}) %collective-permute-start.44) | collective-permute-done | bytes 393248 | tf_op jit(solution)/shard_map/ppermute | solution.py:852
  312.6 3.4 finish_gradient.5
  318.0 2.1 norm_backward.2
  322.4 3.6 fusion.62
  333.5 18.3 %section_backward.6 = (f32[2,128,1536]{2,1,0:T(8,128)S(1)}, bf16[1,2,128,1536]{3,2,1,0:T(8,128)(2,1)S(1)}, bf16[512,1152]{1,0:T(8,128)(2,1)S(1)}, f32[128,768]{1...) custom-call(s32[1]{0:T(128)} %bitcast.part_ref.index_ref, f32[512,768]{1,0:T(8,128)S(1)} %get-tuple-element.358.dy_ref, ...), custom_call_target="tpu_custom_call" | custom-call | flops 23592960000 | bytes 12582912 | tf_op jit(solution)/shard_map/section_backward/pallas_call | solution.py:723
  355.6 8.9 %collective-permute-done.54.refs_1_ = bf16[2,64,1536]{2,1,0:T(8,128)(2,1)S(1)} collective-permute-done((bf16[2,64,1536]{2,1,0:T(8,128)(2,1)S(1)}, bf16[2,64,1536]{2,1,0:T(8,128)(2,1)S(1)}, u32[]{:S(2)}, u32[]{:S(2)}) %collective-permute-start.54) | collective-permute-done | bytes 393248 | tf_op jit(solution)/shard_map/ppermute | solution.py:852
  365.9 2.5 collective-permute-done.56.refs_1_
  373.2 2.2 norm_backward.3
  379.1 3.1 add.548
  395.9 19.3 %section_backward.7 = (f32[2,128,1536]{2,1,0:T(8,128)S(1)}, bf16[1,2,128,1536]{3,2,1,0:T(8,128)(2,1)}, bf16[512,1152]{1,0:T(8,128)(2,1)S(1)}, f32[128,768]{1,0:T...) custom-call(s32[1]{0:T(128)} %bitcast.part_ref.index_ref, f32[512,768]{1,0:T(8,128)S(1)} %get-tuple-element.388.dy_ref, ...), custom_call_target="tpu_custom_call" | custom-call | flops 23592960000 | bytes 12582912 | tf_op jit(solution)/shard_map/section_backward/pallas_call | solution.py:723
  432.2 2.2 fusion.65
  434.5 2.4 fusion
  441.3 2.5 order_blocks.23
  454.2 2.1 slice_bitcast_fusion.refs_0_
  461.6 8.6 %collective-permute-done.68.refs_1_ = bf16[64,1536]{1,0:T(8,128)(2,1)} collective-permute-done((bf16[64,1536]{1,0:T(8,128)(2,1)}, bf16[64,1536]{1,0:T(8,128)(2,1)}, u32[]{:S(2)}, u32[]{:S(2)}) %collective-permute-start.68) | collective-permute-done | bytes 196640 | tf_op jit(solution)/shard_map/ppermute | solution.py:846
  470.2 4.0 collective-permute-done.70.refs_3_
  484.2 6.7 %collective-permute-done.75.refs_2_ = bf16[192,1152]{1,0:T(8,128)(2,1)S(1)} collective-permute-done((bf16[192,1152]{1,0:T(8,128)(2,1)S(1)}, bf16[192,1152]{1,0:T(8,128)(2,1)S(1)}, u32[]{:S(2)}, u32[]{:S(2)}) %collective-permute-start.75) | collective-permute-done | bytes 442400 | tf_op jit(solution)/shard_map/ppermute | solution.py:846
  494.3 2.7 collective-permute-done.74.refs_1_
  498.2 2.1 convert.24
  (569 shorter events, 196.6 us)
Async XLA Ops:
  3.2 11.1 %collective-permute-start.5 = (bf16[1,192,1920]{2,1,0:T(8,128)(2,1)S(1)}, bf16[1,192,1920]{2,1,0:T(8,128)(2,1)S(1)}, u32[]{:S(2)}, u32[]{:S(2)}) collective-permute-start(bf16[1,192,1920]{2,1,0:T(8,128)(2,1)S(1)} %get-tuple-element.524), channel_id=1, source_target_pairs={{0,2},{2,0},{4,6},{6,4},{8,10},{10,8},{12,14},{14,12},{1,3},{3,1},... | collective-permute-start | bytes 2211848 | tf_op jit(solution)/shard_map/ppermute | solution.py:846
  9.1 25.2 %collective-permute-start.4 = (bf16[1,192,1920]{2,1,0:T(8,128)(2,1)S(1)}, bf16[1,192,1920]{2,1,0:T(8,128)(2,1)S(1)}, u32[]{:S(2)}, u32[]{:S(2)}) collective-permute-start(bf16[1,192,1920]{2,1,0:T(8,128)(2,1)S(1)} %get-tuple-element.525.refs_0_), channel_id=1, source_target_pairs={{0,4},{2,6},{4,0},{6,2},{8,12},{10,14},{12,8},{14,10},{1,5},{3,7},... | collective-permute-start | bytes 2211848 | tf_op jit(solution)/shard_map/ppermute | solution.py:846
  14.3 61.7 %collective-permute-start.10 = (bf16[1,192,768]{2,1,0:T(8,128)(2,1)}, bf16[1,192,768]{2,1,0:T(8,128)(2,1)}, u32[]{:S(2)}, u32[]{:S(2)}) collective-permute-start(bf16[1,192,768]{2,1,0:T(8,128)(2,1)} %get-tuple-element.515), channel_id=1, source_target_pairs={{0,2},{2,0},{4,6},{6,4},{8,10},{10,8},{12,14},{14,12},{1,3},{3,1},... | collective-permute-start | bytes 884744 | tf_op jit(solution)/shard_map/ppermute | solution.py:846
  14.3 21.1 %collective-permute-start.6 = (bf16[1,192,1920]{2,1,0:T(8,128)(2,1)S(1)}, bf16[1,192,1920]{2,1,0:T(8,128)(2,1)S(1)}, u32[]{:S(2)}, u32[]{:S(2)}) collective-permute-start(bf16[1,192,1920]{2,1,0:T(8,128)(2,1)S(1)} %collective-permute-done.5.refs_3_), channel_id=1, source_target_pairs={{0,8},{2,10},{4,12},{6,14},{8,0},{10,2},{12,4},{14,6},{1,9},{3,11}... | collective-permute-start | bytes 2211848 | tf_op jit(solution)/shard_map/ppermute | solution.py:846
  19.8 15.5 %collective-permute-start.3 = (bf16[3,64,1536]{2,1,0:T(8,128)(2,1)}, bf16[3,64,1536]{2,1,0:T(8,128)(2,1)}, u32[]{:S(2)}, u32[]{:S(2)}) collective-permute-start(bf16[3,64,1536]{2,1,0:T(8,128)(2,1)} %pad_maximum_fusion.6), channel_id=1, source_target_pairs={{0,1},{1,0},{2,3},{3,2},{4,5},{5,4},{6,7},{7,6},{8,9},{9,8},{10,11... | collective-permute-start | bytes 1769480 | tf_op jit(solution)/shard_map/ppermute | solution.py:852
  39.6 34.8 %collective-permute-start.8 = (bf16[2,192,1920]{2,1,0:T(8,128)(2,1)S(1)}, bf16[2,192,1920]{2,1,0:T(8,128)(2,1)S(1)}, u32[]{:S(2)}, u32[]{:S(2)}) collective-permute-start(bf16[2,192,1920]{2,1,0:T(8,128)(2,1)S(1)} %pad_maximum_fusion), channel_id=1, source_target_pairs={{0,8},{2,10},{4,12},{6,14},{8,0},{10,2},{12,4},{14,6},{1,9},{3,11}... | collective-permute-start | bytes 4423688 | tf_op jit(solution)/shard_map/ppermute | solution.py:846
  41.5 34.5 %collective-permute-start.9 = (bf16[2,192,1920]{2,1,0:T(8,128)(2,1)S(1)}, bf16[2,192,1920]{2,1,0:T(8,128)(2,1)S(1)}, u32[]{:S(2)}, u32[]{:S(2)}) collective-permute-start(bf16[2,192,1920]{2,1,0:T(8,128)(2,1)S(1)} %pad_maximum_fusion.1), channel_id=1, source_target_pairs={{0,4},{2,6},{4,0},{6,2},{8,12},{10,14},{12,8},{14,10},{1,5},{3,7},... | collective-permute-start | bytes 4423688 | tf_op jit(solution)/shard_map/ppermute | solution.py:846
  76.0 14.6 %collective-permute-start.11 = (bf16[1,192,768]{2,1,0:T(8,128)(2,1)S(1)}, bf16[1,192,768]{2,1,0:T(8,128)(2,1)S(1)}, u32[]{:S(2)}, u32[]{:S(2)}) collective-permute-start(bf16[1,192,768]{2,1,0:T(8,128)(2,1)S(1)} %get-tuple-element.244.refs_0_), channel_id=1, source_target_pairs={{0,4},{2,6},{4,0},{6,2},{8,12},{10,14},{12,8},{14,10},{1,5},{3,7},... | collective-permute-start | bytes 884744 | tf_op jit(solution)/shard_map/ppermute | solution.py:846
  76.3 14.3 %collective-permute-start.12 = (bf16[1,192,768]{2,1,0:T(8,128)(2,1)}, bf16[1,192,768]{2,1,0:T(8,128)(2,1)S(1)}, u32[]{:S(2)}, u32[]{:S(2)}) collective-permute-start(bf16[1,192,768]{2,1,0:T(8,128)(2,1)} %collective-permute-done.10.refs_3_), channel_id=1, source_target_pairs={{0,8},{2,10},{4,12},{6,14},{8,0},{10,2},{12,4},{14,6},{1,9},{3,11}... | collective-permute-start | bytes 884744 | tf_op jit(solution)/shard_map/ppermute | solution.py:846
  91.8 15.3 %collective-permute-start.14 = (f32[4,128]{1,0:T(4,128)S(1)}, f32[4,128]{1,0:T(4,128)S(1)}, u32[]{:S(2)}, u32[]{:S(2)}) collective-permute-start(f32[4,128]{1,0:T(4,128)S(1)} %fusion.51), channel_id=1, source_target_pairs={{0,1},{1,0},{2,3},{3,2},{4,5},{5,4},{6,7},{7,6},{8,9},{9,8},{10,11... | collective-permute-start | bytes 6152 | tf_op jit(solution)/shard_map/ppermute | solution.py:852
  93.4 15.4 %collective-permute-start.15 = (bf16[2,192,768]{2,1,0:T(8,128)(2,1)S(1)}, bf16[2,192,768]{2,1,0:T(8,128)(2,1)S(1)}, u32[]{:S(2)}, u32[]{:S(2)}) collective-permute-start(bf16[2,192,768]{2,1,0:T(8,128)(2,1)S(1)} %pad_maximum_fusion.7), channel_id=1, source_target_pairs={{0,8},{2,10},{4,12},{6,14},{8,0},{10,2},{12,4},{14,6},{1,9},{3,11}... | collective-permute-start | bytes 1769480 | tf_op jit(solution)/shard_map/ppermute | solution.py:846
  93.8 15.2 %collective-permute-start.16 = (bf16[2,192,768]{2,1,0:T(8,128)(2,1)S(1)}, bf16[2,192,768]{2,1,0:T(8,128)(2,1)S(1)}, u32[]{:S(2)}, u32[]{:S(2)}) collective-permute-start(bf16[2,192,768]{2,1,0:T(8,128)(2,1)S(1)} %pad_maximum_fusion.8), channel_id=1, source_target_pairs={{0,4},{2,6},{4,0},{6,2},{8,12},{10,14},{12,8},{14,10},{1,5},{3,7},... | collective-permute-start | bytes 1769480 | tf_op jit(solution)/shard_map/ppermute | solution.py:846
  116.3 12.0 %collective-permute-start.23 = (bf16[128,1536]{1,0:T(8,128)(2,1)S(1)}, bf16[128,1536]{1,0:T(8,128)(2,1)S(1)}, u32[]{:S(2)}, u32[]{:S(2)}) collective-permute-start(bf16[128,1536]{1,0:T(8,128)(2,1)S(1)} %get-tuple-element.494), channel_id=1, source_target_pairs={{0,4},{2,6},{4,0},{6,2},{8,12},{10,14},{12,8},{14,10},{1,5},{3,7},... | collective-permute-start | bytes 1179656 | tf_op jit(solution)/shard_map/ppermute | solution.py:846
  118.1 19.3 %collective-permute-start.24 = (bf16[128,1536]{1,0:T(8,128)(2,1)S(1)}, bf16[128,1536]{1,0:T(8,128)(2,1)S(1)}, u32[]{:S(2)}, u32[]{:S(2)}) collective-permute-start(bf16[128,1536]{1,0:T(8,128)(2,1)S(1)} %get-tuple-element.493), channel_id=1, source_target_pairs={{0,8},{2,10},{4,12},{6,14},{8,0},{10,2},{12,4},{14,6},{1,9},{3,11}... | collective-permute-start | bytes 1179656 | tf_op jit(solution)/shard_map/ppermute | solution.py:846
  118.6 18.8 %collective-permute-start.25 = (bf16[128,1536]{1,0:T(8,128)(2,1)S(1)}, bf16[128,1536]{1,0:T(8,128)(2,1)S(1)}, u32[]{:S(2)}, u32[]{:S(2)}) collective-permute-start(bf16[128,1536]{1,0:T(8,128)(2,1)S(1)} %get-tuple-element.492), channel_id=1, source_target_pairs={{0,12},{2,14},{4,8},{6,10},{8,4},{10,6},{12,0},{14,2},{1,13},{3,15... | collective-permute-start | bytes 1179656 | tf_op jit(solution)/shard_map/ppermute | solution.py:846
  121.6 15.8 %collective-permute-start.22 = (f16[2,64,1536]{2,1,0:T(8,128)(2,1)S(1)}, f16[2,64,1536]{2,1,0:T(8,128)(2,1)S(1)}, u32[]{:S(2)}, u32[]{:S(2)}) collective-permute-start(f16[2,64,1536]{2,1,0:T(8,128)(2,1)S(1)} %fusion.26), channel_id=1, source_target_pairs={{0,1},{1,0},{2,3},{3,2},{4,5},{5,4},{6,7},{7,6},{8,9},{9,8},{10,11... | collective-permute-start | bytes 1179656 | tf_op jit(solution)/shard_map/ppermute | solution.py:852
  128.0 18.0 %collective-permute-start.20 = (f32[2,128,1536]{2,1,0:T(8,128)}, f32[2,128,1536]{2,1,0:T(8,128)}, u32[]{:S(2)}, u32[]{:S(2)}) collective-permute-start(f32[2,128,1536]{2,1,0:T(8,128)} %bitcast.68), channel_id=1, source_target_pairs={{0,2},{2,0},{4,6},{6,4},{8,10},{10,8},{12,14},{14,12},{1,3},{3,1},... | collective-permute-start | bytes 4718600 | tf_op jit(solution)/shard_map/ppermute | solution.py:846
  141.6 23.1 %collective-permute-start.27 = (bf16[2,64,1536]{2,1,0:T(8,128)(2,1)S(1)}, bf16[2,64,1536]{2,1,0:T(8,128)(2,1)S(1)}, u32[]{:S(2)}, u32[]{:S(2)}) collective-permute-start(bf16[2,64,1536]{2,1,0:T(8,128)(2,1)S(1)} %fusion.11), channel_id=1, source_target_pairs={{0,17},{1,16},{2,19},{3,18},{4,21},{5,20},{6,23},{7,22},{8,25},{9,... | collective-permute-start | bytes 1179656 | tf_op jit(solution)/shard_map/ppermute | solution.py:860
  147.2 16.2 %collective-permute-start.21 = (f16[2,64,1536]{2,1,0:T(8,128)(2,1)S(1)}, f16[2,64,1536]{2,1,0:T(8,128)(2,1)S(1)}, u32[]{:S(2)}, u32[]{:S(2)}) collective-permute-start(f16[2,64,1536]{2,1,0:T(8,128)(2,1)S(1)} %fusion.27), channel_id=1, source_target_pairs={{0,1},{1,0},{2,3},{3,2},{4,5},{5,4},{6,7},{7,6},{8,9},{9,8},{10,11... | collective-permute-start | bytes 1179656 | tf_op jit(solution)/shard_map/ppermute | solution.py:852
  164.8 12.1 %collective-permute-start.28 = (bf16[2,64,1536]{2,1,0:T(8,128)(2,1)S(1)}, bf16[2,64,1536]{2,1,0:T(8,128)(2,1)S(1)}, u32[]{:S(2)}, u32[]{:S(2)}) collective-permute-start(bf16[2,64,1536]{2,1,0:T(8,128)(2,1)S(1)} %bitcast_select_fusion.1.refs_0_), channel_id=1, source_target_pairs={{0,1},{1,0},{2,3},{3,2},{4,5},{5,4},{6,7},{7,6},{8,9},{9,8},{10,11... | collective-permute-start | bytes 1179656 | tf_op jit(solution)/shard_map/ppermute | solution.py:852
  167.3 16.7 %collective-permute-start.29 = (bf16[2,64,1536]{2,1,0:T(8,128)(2,1)S(1)}, bf16[2,64,1536]{2,1,0:T(8,128)(2,1)S(1)}, u32[]{:S(2)}, u32[]{:S(2)}) collective-permute-start(bf16[2,64,1536]{2,1,0:T(8,128)(2,1)S(1)} %fusion.16), channel_id=1, source_target_pairs={{0,17},{1,16},{2,19},{3,18},{4,21},{5,20},{6,23},{7,22},{8,25},{9,... | collective-permute-start | bytes 1179656 | tf_op jit(solution)/shard_map/ppermute | solution.py:860
  186.8 16.5 %collective-permute-start.31 = (bf16[2,64,1536]{2,1,0:T(8,128)(2,1)S(1)}, bf16[2,64,1536]{2,1,0:T(8,128)(2,1)S(1)}, u32[]{:S(2)}, u32[]{:S(2)}) collective-permute-start(bf16[2,64,1536]{2,1,0:T(8,128)(2,1)S(1)} %bitcast_select_fusion.refs_0_), channel_id=1, source_target_pairs={{0,1},{1,0},{2,3},{3,2},{4,5},{5,4},{6,7},{7,6},{8,9},{9,8},{10,11... | collective-permute-start | bytes 1179656 | tf_op jit(solution)/shard_map/ppermute | solution.py:852
  203.6 18.7 %collective-permute-start.34 = (bf16[2,128,1536]{2,1,0:T(8,128)(2,1)S(1)}, bf16[2,128,1536]{2,1,0:T(8,128)(2,1)S(1)}, u32[]{:S(2)}, u32[]{:S(2)}) collective-permute-start(bf16[2,128,1536]{2,1,0:T(8,128)(2,1)S(1)} %bitcast.464), channel_id=1, source_target_pairs={{0,2},{2,0},{4,6},{6,4},{8,10},{10,8},{12,14},{14,12},{1,3},{3,1},... | collective-permute-start | bytes 2359304 | tf_op jit(solution)/shard_map/ppermute | solution.py:846
  223.4 25.7 %collective-permute-start.36 = (bf16[2,64,1536]{2,1,0:T(8,128)(2,1)S(1)}, bf16[2,64,1536]{2,1,0:T(8,128)(2,1)S(1)}, u32[]{:S(2)}, u32[]{:S(2)}) collective-permute-start(bf16[2,64,1536]{2,1,0:T(8,128)(2,1)S(1)} %bitcast.470), channel_id=1, source_target_pairs={{0,1},{1,0},{2,3},{3,2},{4,5},{5,4},{6,7},{7,6},{8,9},{9,8},{10,11... | collective-permute-start | bytes 1179656 | tf_op jit(solution)/shard_map/ppermute | solution.py:852
  225.0 24.1 %collective-permute-start.35 = (bf16[2,64,1536]{2,1,0:T(8,128)(2,1)S(1)}, bf16[2,64,1536]{2,1,0:T(8,128)(2,1)S(1)}, u32[]{:S(2)}, u32[]{:S(2)}) collective-permute-start(bf16[2,64,1536]{2,1,0:T(8,128)(2,1)S(1)} %bitcast.472), channel_id=1, source_target_pairs={{0,1},{1,0},{2,3},{3,2},{4,5},{5,4},{6,7},{7,6},{8,9},{9,8},{10,11... | collective-permute-start | bytes 1179656 | tf_op jit(solution)/shard_map/ppermute | solution.py:852
  251.6 11.2 %collective-permute-start.41 = (bf16[2,64,1536]{2,1,0:T(8,128)(2,1)S(1)}, bf16[2,64,1536]{2,1,0:T(8,128)(2,1)S(1)}, u32[]{:S(2)}, u32[]{:S(2)}) collective-permute-start(bf16[2,64,1536]{2,1,0:T(8,128)(2,1)S(1)} %bitcast.473), channel_id=1, source_target_pairs={{0,1},{1,0},{2,3},{3,2},{4,5},{5,4},{6,7},{7,6},{8,9},{9,8},{10,11... | collective-permute-start | bytes 1179656 | tf_op jit(solution)/shard_map/ppermute | solution.py:852
  265.1 21.5 %collective-permute-start.42 = (bf16[2,64,1536]{2,1,0:T(8,128)(2,1)S(1)}, bf16[2,64,1536]{2,1,0:T(8,128)(2,1)S(1)}, u32[]{:S(2)}, u32[]{:S(2)}) collective-permute-start(bf16[2,64,1536]{2,1,0:T(8,128)(2,1)S(1)} %get-tuple-element.336), channel_id=1, source_target_pairs={{16,0},{17,1},{18,2},{19,3},{20,4},{21,5},{22,6},{23,7},{24,8},{25... | collective-permute-start | bytes 1179656 | tf_op jit(solution)/shard_map/ppermute | solution.py:860
  289.3 12.2 %collective-permute-start.45 = (bf16[2,64,1536]{2,1,0:T(8,128)(2,1)}, bf16[2,64,1536]{2,1,0:T(8,128)(2,1)}, u32[]{:S(2)}, u32[]{:S(2)}) collective-permute-start(bf16[2,64,1536]{2,1,0:T(8,128)(2,1)} %bitcast_select_fusion.2.refs_0_), channel_id=1, source_target_pairs={{0,1},{1,0},{2,3},{3,2},{4,5},{5,4},{6,7},{7,6},{8,9},{9,8},{10,11... | collective-permute-start | bytes 1179656 | tf_op jit(solution)/shard_map/ppermute | solution.py:852
  294.2 15.4 %collective-permute-start.44 = (bf16[2,64,1536]{2,1,0:T(8,128)(2,1)}, bf16[2,64,1536]{2,1,0:T(8,128)(2,1)}, u32[]{:S(2)}, u32[]{:S(2)}) collective-permute-start(bf16[2,64,1536]{2,1,0:T(8,128)(2,1)} %bitcast.111), channel_id=1, source_target_pairs={{0,1},{1,0},{2,3},{3,2},{4,5},{5,4},{6,7},{7,6},{8,9},{9,8},{10,11... | collective-permute-start | bytes 1179656 | tf_op jit(solution)/shard_map/ppermute | solution.py:852
  316.0 36.8 %collective-permute-start.46 = (bf16[2,64,1536]{2,1,0:T(8,128)(2,1)S(1)}, bf16[2,64,1536]{2,1,0:T(8,128)(2,1)S(1)}, u32[]{:S(2)}, u32[]{:S(2)}) collective-permute-start(bf16[2,64,1536]{2,1,0:T(8,128)(2,1)S(1)} %get-tuple-element.344), channel_id=1, source_target_pairs={{16,0},{17,1},{18,2},{19,3},{20,4},{21,5},{22,6},{23,7},{24,8},{25... | collective-permute-start | bytes 1179656 | tf_op jit(solution)/shard_map/ppermute | solution.py:860
  326.1 26.8 %collective-permute-start.51 = (bf16[64,1536]{1,0:T(8,128)(2,1)S(1)}, bf16[64,1536]{1,0:T(8,128)(2,1)S(1)}, u32[]{:S(2)}, u32[]{:S(2)}) collective-permute-start(bf16[64,1536]{1,0:T(8,128)(2,1)S(1)} %get-tuple-element.353), channel_id=1, source_target_pairs={{0,4},{2,6},{4,0},{6,2},{8,12},{10,14},{12,8},{14,10},{1,5},{3,7},... | collective-permute-start | bytes 589832 | tf_op jit(solution)/shard_map/ppermute | solution.py:846
  326.5 26.4 %collective-permute-start.52 = (bf16[64,1536]{1,0:T(8,128)(2,1)S(1)}, bf16[64,1536]{1,0:T(8,128)(2,1)S(1)}, u32[]{:S(2)}, u32[]{:S(2)}) collective-permute-start(bf16[64,1536]{1,0:T(8,128)(2,1)S(1)} %get-tuple-element.354), channel_id=1, source_target_pairs={{0,8},{2,10},{4,12},{6,14},{8,0},{10,2},{12,4},{14,6},{1,9},{3,11}... | collective-permute-start | bytes 589832 | tf_op jit(solution)/shard_map/ppermute | solution.py:846
  328.1 24.7 %collective-permute-start.53 = (bf16[64,1536]{1,0:T(8,128)(2,1)S(1)}, bf16[64,1536]{1,0:T(8,128)(2,1)S(1)}, u32[]{:S(2)}, u32[]{:S(2)}) collective-permute-start(bf16[64,1536]{1,0:T(8,128)(2,1)S(1)} %get-tuple-element.355), channel_id=1, source_target_pairs={{0,12},{2,14},{4,8},{6,10},{8,4},{10,6},{12,0},{14,2},{1,13},{3,15... | collective-permute-start | bytes 589832 | tf_op jit(solution)/shard_map/ppermute | solution.py:846
  353.0 11.6 %collective-permute-start.54 = (bf16[2,64,1536]{2,1,0:T(8,128)(2,1)S(1)}, bf16[2,64,1536]{2,1,0:T(8,128)(2,1)S(1)}, u32[]{:S(2)}, u32[]{:S(2)}) collective-permute-start(bf16[2,64,1536]{2,1,0:T(8,128)(2,1)S(1)} %bitcast_select_fusion.3.refs_0_), channel_id=1, source_target_pairs={{0,1},{1,0},{2,3},{3,2},{4,5},{5,4},{6,7},{7,6},{8,9},{9,8},{10,11... | collective-permute-start | bytes 1179656 | tf_op jit(solution)/shard_map/ppermute | solution.py:852
  382.2 35.0 %collective-permute-start.60 = (bf16[2,64,1536]{2,1,0:T(8,128)(2,1)S(1)}, bf16[2,64,1536]{2,1,0:T(8,128)(2,1)S(1)}, u32[]{:S(2)}, u32[]{:S(2)}) collective-permute-start(bf16[2,64,1536]{2,1,0:T(8,128)(2,1)S(1)} %bitcast.469), channel_id=1, source_target_pairs={{0,1},{1,0},{2,3},{3,2},{4,5},{5,4},{6,7},{7,6},{8,9},{9,8},{10,11... | collective-permute-start | bytes 1179656 | tf_op jit(solution)/shard_map/ppermute | solution.py:852
  392.1 31.3 %collective-permute-start.61 = (bf16[2,192,1536]{2,1,0:T(8,128)(2,1)}, bf16[2,192,1536]{2,1,0:T(8,128)(2,1)}, u32[]{:S(2)}, u32[]{:S(2)}) collective-permute-start(bf16[2,192,1536]{2,1,0:T(8,128)(2,1)} %pad_maximum_fusion.2), channel_id=1, source_target_pairs={{0,4},{2,6},{4,0},{6,2},{8,12},{10,14},{12,8},{14,10},{1,5},{3,7},... | collective-permute-start | bytes 3538952 | tf_op jit(solution)/shard_map/ppermute | solution.py:846
  392.4 31.0 %collective-permute-start.62 = (bf16[2,192,1536]{2,1,0:T(8,128)(2,1)}, bf16[2,192,1536]{2,1,0:T(8,128)(2,1)}, u32[]{:S(2)}, u32[]{:S(2)}) collective-permute-start(bf16[2,192,1536]{2,1,0:T(8,128)(2,1)} %pad_maximum_fusion.3), channel_id=1, source_target_pairs={{0,8},{2,10},{4,12},{6,14},{8,0},{10,2},{12,4},{14,6},{1,9},{3,11}... | collective-permute-start | bytes 3538952 | tf_op jit(solution)/shard_map/ppermute | solution.py:846
  394.1 29.3 %collective-permute-start.63 = (bf16[4,64,1536]{2,1,0:T(8,128)(2,1)}, bf16[4,64,1536]{2,1,0:T(8,128)(2,1)}, u32[]{:S(2)}, u32[]{:S(2)}) collective-permute-start(bf16[4,64,1536]{2,1,0:T(8,128)(2,1)} %order_blocks.19.refs_0_), channel_id=1, source_target_pairs={{0,1},{1,0},{2,3},{3,2},{4,5},{5,4},{6,7},{7,6},{8,9},{9,8},{10,11... | collective-permute-start | bytes 2359304 | tf_op jit(solution)/shard_map/ppermute | solution.py:852
  424.9 20.3 %collective-permute-start.65 = (bf16[2,64,1536]{2,1,0:T(8,128)(2,1)S(1)}, bf16[2,64,1536]{2,1,0:T(8,128)(2,1)S(1)}, u32[]{:S(2)}, u32[]{:S(2)}) collective-permute-start(bf16[2,64,1536]{2,1,0:T(8,128)(2,1)S(1)} %bitcast.471), channel_id=1, source_target_pairs={{0,1},{1,0},{2,3},{3,2},{4,5},{5,4},{6,7},{7,6},{8,9},{9,8},{10,11... | collective-permute-start | bytes 1179656 | tf_op jit(solution)/shard_map/ppermute | solution.py:852
  427.6 17.6 %collective-permute-start.66 = (bf16[192,1536]{1,0:T(8,128)(2,1)S(1)}, bf16[192,1536]{1,0:T(8,128)(2,1)S(1)}, u32[]{:S(2)}, u32[]{:S(2)}) collective-permute-start(bf16[192,1536]{1,0:T(8,128)(2,1)S(1)} %fusion.3), channel_id=1, source_target_pairs={{0,8},{2,10},{4,12},{6,14},{8,0},{10,2},{12,4},{14,6},{1,9},{3,11}... | collective-permute-start | bytes 1769480 | tf_op jit(solution)/shard_map/ppermute | solution.py:846
  430.7 16.3 %collective-permute-start.67 = (bf16[192,1536]{1,0:T(8,128)(2,1)S(1)}, bf16[192,1536]{1,0:T(8,128)(2,1)S(1)}, u32[]{:S(2)}, u32[]{:S(2)}) collective-permute-start(bf16[192,1536]{1,0:T(8,128)(2,1)S(1)} %fusion.2), channel_id=1, source_target_pairs={{0,4},{2,6},{4,0},{6,2},{8,12},{10,14},{12,8},{14,10},{1,5},{3,7},... | collective-permute-start | bytes 1769480 | tf_op jit(solution)/shard_map/ppermute | solution.py:846
  438.3 36.0 %collective-permute-start.71 = (bf16[2,192,1152]{2,1,0:T(8,128)(2,1)}, bf16[2,192,1152]{2,1,0:T(8,128)(2,1)}, u32[]{:S(2)}, u32[]{:S(2)}) collective-permute-start(bf16[2,192,1152]{2,1,0:T(8,128)(2,1)} %dynamic-slice_bitcast_fusion.1), channel_id=1, source_target_pairs={{0,4},{2,6},{4,0},{6,2},{8,12},{10,14},{12,8},{14,10},{1,5},{3,7},... | collective-permute-start | bytes 2654216 | tf_op jit(solution)/shard_map/ppermute | solution.py:846
  439.8 34.4 %collective-permute-start.72 = (bf16[2,192,1152]{2,1,0:T(8,128)(2,1)}, bf16[2,192,1152]{2,1,0:T(8,128)(2,1)}, u32[]{:S(2)}, u32[]{:S(2)}) collective-permute-start(bf16[2,192,1152]{2,1,0:T(8,128)(2,1)} %dynamic-slice_bitcast_fusion), channel_id=1, source_target_pairs={{0,8},{2,10},{4,12},{6,14},{8,0},{10,2},{12,4},{14,6},{1,9},{3,11}... | collective-permute-start | bytes 2654216 | tf_op jit(solution)/shard_map/ppermute | solution.py:846
  450.4 19.8 %collective-permute-start.68 = (bf16[64,1536]{1,0:T(8,128)(2,1)}, bf16[64,1536]{1,0:T(8,128)(2,1)}, u32[]{:S(2)}, u32[]{:S(2)}) collective-permute-start(bf16[64,1536]{1,0:T(8,128)(2,1)} %get-tuple-element.510), channel_id=1, source_target_pairs={{0,4},{2,6},{4,0},{6,2},{8,12},{10,14},{12,8},{14,10},{1,5},{3,7},... | collective-permute-start | bytes 589832 | tf_op jit(solution)/shard_map/ppermute | solution.py:846
  451.8 18.4 %collective-permute-start.69 = (bf16[64,1536]{1,0:T(8,128)(2,1)}, bf16[64,1536]{1,0:T(8,128)(2,1)}, u32[]{:S(2)}, u32[]{:S(2)}) collective-permute-start(bf16[64,1536]{1,0:T(8,128)(2,1)} %get-tuple-element.509), channel_id=1, source_target_pairs={{0,8},{2,10},{4,12},{6,14},{8,0},{10,2},{12,4},{14,6},{1,9},{3,11}... | collective-permute-start | bytes 589832 | tf_op jit(solution)/shard_map/ppermute | solution.py:846
  456.3 18.0 %collective-permute-start.70 = (bf16[64,1536]{1,0:T(8,128)(2,1)}, bf16[64,1536]{1,0:T(8,128)(2,1)}, u32[]{:S(2)}, u32[]{:S(2)}) collective-permute-start(bf16[64,1536]{1,0:T(8,128)(2,1)} %get-tuple-element.508), channel_id=1, source_target_pairs={{0,12},{2,14},{4,8},{6,10},{8,4},{10,6},{12,0},{14,2},{1,13},{3,15... | collective-permute-start | bytes 589832 | tf_op jit(solution)/shard_map/ppermute | solution.py:846
  478.2 18.7 %collective-permute-start.74 = (bf16[4,64,1536]{2,1,0:T(8,128)(2,1)S(1)}, bf16[4,64,1536]{2,1,0:T(8,128)(2,1)}, u32[]{:S(2)}, u32[]{:S(2)}) collective-permute-start(bf16[4,64,1536]{2,1,0:T(8,128)(2,1)S(1)} %order_blocks.24.refs_0_), channel_id=1, source_target_pairs={{0,1},{1,0},{2,3},{3,2},{4,5},{5,4},{6,7},{7,6},{8,9},{9,8},{10,11... | collective-permute-start | bytes 2359304 | tf_op jit(solution)/shard_map/ppermute | solution.py:852
  480.0 10.9 %collective-permute-start.75 = (bf16[192,1152]{1,0:T(8,128)(2,1)S(1)}, bf16[192,1152]{1,0:T(8,128)(2,1)S(1)}, u32[]{:S(2)}, u32[]{:S(2)}) collective-permute-start(bf16[192,1152]{1,0:T(8,128)(2,1)S(1)} %fusion.7), channel_id=1, source_target_pairs={{0,8},{2,10},{4,12},{6,14},{8,0},{10,2},{12,4},{14,6},{1,9},{3,11}... | collective-permute-start | bytes 1327112 | tf_op jit(solution)/shard_map/ppermute | solution.py:846
  (170 other events, 1713.3 us)
